TPU v7x, 32 devices: a whole 2x2x4 slice. The times are simulated.
32 devices in a mesh: ctx: 8 (over z, x), fsdp: 4 (over y, core).
Axes of the slice: x: 2, y: 2, z: 4, core: 2. Of those that a mesh axis runs over, the one named last changes fastest.
Arguments:
- layer_input: bfloat16 [4, 3072, 1536], P('fsdp', 'ctx'), may hold values from -6 to 6
- lengths: int32 [4, 3], P('fsdp'), may hold values from 64 to 2944, as said below
- expert_ids: int32 [4, 3072, 4], P('fsdp', 'ctx'), may hold values from 0 to 15, all different within a row; in each aligned block of 384 rows (0 to 383, 384 to 767, ..., all dimensions but the last counted through in order) at most 144 rows name the same one
- gate_weights: float32 [4, 3072, 4], P('fsdp', 'ctx'), may hold values from 0.15 to 0.35
- attn_gain: bfloat16 [1536], P(('ctx', 'fsdp')), may hold values from 0.5 to 1.5
- wq: bfloat16 [1536, 1536], P(('ctx', 'fsdp')), may hold values from -0.15625 to 0.15625
- wk: bfloat16 [1536, 256], P(('ctx', 'fsdp')), may hold values from -0.15625 to 0.15625
- wv: bfloat16 [1536, 256], P(('ctx', 'fsdp')), may hold values from -0.15625 to 0.15625
- wo: bfloat16 [1536, 1536], P(None, ('ctx', 'fsdp')), may hold values from -2.5 to 2.5
- moe_gain: bfloat16 [1536], P(('ctx', 'fsdp')), may hold values from 0.5 to 1.5
- w_gate: bfloat16 [16, 1536, 768], P('ctx', 'fsdp'), may hold values from -0.15625 to 0.15625
- w_up: bfloat16 [16, 1536, 768], P('ctx', 'fsdp'), may hold values from -0.15625 to 0.15625
- w_down: bfloat16 [16, 768, 1536], P('ctx', None, 'fsdp'), may hold values from -0.625 to 0.625
- cotangent: bfloat16 [4, 3072, 1536], P('fsdp', 'ctx'), may hold values from -6 to 6
Outputs:
- output: bfloat16 [4, 3072, 1536], P('fsdp', 'ctx')
- input_grad: bfloat16 [4, 3072, 1536], P('fsdp', 'ctx')
- attn_gain_grad: float32 [1536], P(('ctx', 'fsdp'))
- wq_grad: float32 [1536, 1536], P(('ctx', 'fsdp'))
- wk_grad: float32 [1536, 256], P(('ctx', 'fsdp'))
- wv_grad: float32 [1536, 256], P(('ctx', 'fsdp'))
- wo_grad: float32 [1536, 1536], P(None, ('ctx', 'fsdp'))
- moe_gain_grad: float32 [1536], P(('ctx', 'fsdp'))
- w_gate_grad: float32 [16, 1536, 768], P('ctx', 'fsdp')
- w_up_grad: float32 [16, 1536, 768], P('ctx', 'fsdp')
- w_down_grad: float32 [16, 768, 1536], P('ctx', None, 'fsdp')
Inputs may be any that keep to these rules, and one draw needn't show every extreme that they name: Each row holds the lengths of the 3 sequences that fill a group's 3072 tokens in order. In each row one sequence is long and the other 2 each have at most 192 tokens; the long one spans from the group's first device to its last. In some row the short ones all equal the least. `expert_ids`: A token names 4 different experts. Among the 384 tokens of one device (aligned blocks of rows) no expert is named more than 144 times, a bound that some block reaches.
All inputs are finite; a program needn't handle non-finite values.
Results may differ from a plain program's by a relative error of at most 0.018.
Values may be sent and summed in bfloat16 or wider, within the bound.
No kernel may reach another device: no remote copies, remote signals or barrier semaphores. Data moves between devices by JAX's collectives and lax.ppermute only.
A program may use at most 256 MiB of HBM per device.

v0:
```python
import math

import jax
import jax.numpy as jnp
from jax import lax
from jax.sharding import PartitionSpec as P

HEADS = 12
KV_HEADS = 2
HEAD = 128
TOPK = 4


EPS = 1e-06
ROPE_BASE = 10000.0
NEG = -1e30


def rope_tables(positions, head_size):
    half = head_size // 2
    freq = jnp.exp(jnp.arange(half, dtype=jnp.float32) * (-2.0 * math.log(ROPE_BASE) / head_size))
    angle = positions.astype(jnp.float32)[:, None] * freq[None, :]
    return (jnp.cos(angle), jnp.sin(angle))


def rotate(values, cosine, sine):
    half = values.shape[-1] // 2
    first = values[..., :half]
    second = values[..., half:]
    cosine = cosine[:, None, :]
    sine = sine[:, None, :]
    return jnp.concatenate([first * cosine - second * sine, second * cosine + first * sine], -1)


def seq_info(index, seq_lengths):
    ends = jnp.cumsum(seq_lengths)
    after = (index[:, None] >= ends[None, :]).astype(jnp.int32)
    return (jnp.sum(after, 1), index - jnp.sum(after * seq_lengths[None, :], 1))


def rms_scale(values):
    return lax.rsqrt(jnp.mean(values * values, -1, keepdims=True) + EPS)


def norm_back(grad, normed, scale_rows):
    return scale_rows * (grad - normed * jnp.mean(grad * normed, -1, keepdims=True))


def cross_rows(left, right):
    return lax.dot_general(
        left, right, (((0,), (0,)), ((), ())), preferred_element_type=jnp.float32
    )


def cross_cols(left, right):
    return lax.dot_general(
        left, right, (((1,), (1,)), ((), ())), preferred_element_type=jnp.float32
    )


def row_index(device, tokens):
    offsets = jnp.arange(tokens, dtype=jnp.int32)
    return device[:, None] * tokens + offsets[None, :]


def to_experts(buffer):
    return lax.all_to_all(buffer, "ctx", split_axis=0, concat_axis=2, tiled=True)


def from_experts(buffer):
    return lax.all_to_all(buffer, "ctx", split_axis=2, concat_axis=0, tiled=True)


def keep_same(state):
    return state


def local(
    layer_input,
    lengths,
    expert_ids,
    gate_weights,
    attn_gain,
    wq,
    wk,
    wv,
    wo,
    moe_gain,
    w_gate,
    w_up,
    w_down,
    cotangent,
):
    count = lax.axis_size("ctx")
    position = lax.axis_index("ctx")
    tokens = layer_input.shape[1]
    width = layer_input.shape[2]
    repeat = HEADS // KV_HEADS
    kv_width = KV_HEADS * HEAD
    scale = HEAD ** (-0.5)
    exp_dev = w_gate.shape[0]
    experts = exp_dev * count
    capacity = 3 * tokens * TOPK // (2 * experts)
    seq_lengths = lengths[0]
    input_rows = layer_input[0]
    input_wide = input_rows.astype(jnp.float32)
    gain_attn, q_weight, k_weight, v_weight, o_weight, gain_moe = (
        lax.all_gather(attn_gain, ("ctx", "fsdp"), axis=0, tiled=True),
        lax.all_gather(wq, ("ctx", "fsdp"), axis=0, tiled=True),
        lax.all_gather(wk, ("ctx", "fsdp"), axis=0, tiled=True),
        lax.all_gather(wv, ("ctx", "fsdp"), axis=0, tiled=True),
        lax.all_gather(wo, ("ctx", "fsdp"), axis=1, tiled=True),
        lax.all_gather(moe_gain, ("ctx", "fsdp"), axis=0, tiled=True),
    )
    gain_attn = gain_attn.astype(jnp.float32)
    gain_moe = gain_moe.astype(jnp.float32)
    parts = 1
    all_index = row_index(jnp.arange(count, dtype=jnp.int32), tokens)
    all_seq = seq_info(all_index.reshape(-1), seq_lengths)[0]
    query_index = lax.dynamic_index_in_dim(all_index, position, 0, keepdims=False)
    query_seq, query_pos = seq_info(query_index, seq_lengths)
    cosine, sine = rope_tables(query_pos, HEAD)
    attn_in = input_rows.astype(jnp.float32)
    scale_one = rms_scale(attn_in)
    normed_one = attn_in * scale_one
    normed_low = (normed_one * gain_attn).astype(jnp.bfloat16)
    q_raw = jnp.dot(normed_low, q_weight, preferred_element_type=jnp.float32)
    k_raw = jnp.dot(normed_low, k_weight, preferred_element_type=jnp.float32)
    v_raw = jnp.dot(normed_low, v_weight, preferred_element_type=jnp.float32)
    q_rot = rotate(q_raw.reshape(tokens, HEADS, HEAD), cosine, sine).astype(jnp.bfloat16)
    k_rot = (
        rotate(k_raw.reshape(tokens, KV_HEADS, HEAD), cosine, sine)
        .astype(jnp.bfloat16)
        .reshape(tokens, kv_width)
    )
    v_low = v_raw.astype(jnp.bfloat16)
    k_all, v_all = (
        lax.all_gather(k_rot, "ctx", axis=0, tiled=True),
        lax.all_gather(v_low, "ctx", axis=0, tiled=True),
    )
    tile = tokens // parts
    q_tiles = q_rot.reshape(parts, tile, KV_HEADS, repeat, HEAD)
    q_tile_index = query_index.reshape(parts, tile)
    q_tile_seq = query_seq.reshape(parts, tile)
    key_pieces = (
        k_all.reshape(count, parts, tile, KV_HEADS, HEAD),
        v_all.reshape(count, parts, tile, KV_HEADS, HEAD),
        all_index.reshape(count, parts, tile),
        all_seq.reshape(count, parts, tile),
    )

    def tile_mask(query_part, key_rows, key_seq):
        return (q_tile_seq[query_part][:, None] == key_seq[None, :]) & (
            key_rows[None, :] <= q_tile_index[query_part][:, None]
        )

    def tile_scores(query_part, key_tile, mask):
        raw = (
            jnp.einsum(
                "qgrd,kgd->grqk", q_tiles[query_part], key_tile, preferred_element_type=jnp.float32
            )
            * scale
        )
        return jnp.where(mask, raw, NEG)

    def total_step(carry, piece):
        states = list(carry)
        query_part = 0
        mask = tile_mask(query_part, piece[2][0], piece[3][0])

        def total_update(state, query_part=query_part, key_tile=piece[0][0], mask=mask):
            scores = tile_scores(query_part, key_tile, mask)
            peak = jnp.maximum(state[0], jnp.max(scores, -1))
            summed = state[1] * jnp.exp(state[0] - peak) + jnp.sum(
                jnp.exp(scores - peak[..., None]), -1
            )
            return (peak, summed)

        states[query_part] = lax.cond(jnp.any(mask), total_update, keep_same, states[query_part])
        return (tuple(states), None)

    start_state = tuple(
        (
            (
                jnp.full((KV_HEADS, repeat, tile), NEG, jnp.float32),
                jnp.zeros((KV_HEADS, repeat, tile), jnp.float32),
            )
            for query_part in range(parts)
        )
    )
    final_state = lax.scan(total_step, start_state, key_pieces)[0]
    log_total = [state[0] + jnp.log(state[1]) for state in final_state]

    def output_step(carry, piece):
        outs = list(carry)
        query_part = 0
        mask = tile_mask(query_part, piece[2][0], piece[3][0])

        def output_update(
            accum, query_part=query_part, key_tile=piece[0][0], value_tile=piece[1][0], mask=mask
        ):
            scores = tile_scores(query_part, key_tile, mask)
            probs = jnp.exp(scores - log_total[query_part][..., None]).astype(jnp.bfloat16)
            return accum + jnp.einsum(
                "grqk,kgd->qgrd", probs, value_tile, preferred_element_type=jnp.float32
            )

        outs[query_part] = lax.cond(jnp.any(mask), output_update, keep_same, outs[query_part])
        return (tuple(outs), None)

    start_outs = tuple(
        (jnp.zeros((tile, KV_HEADS, repeat, HEAD), jnp.float32) for query_part in range(parts))
    )
    attended_wide = jnp.concatenate(lax.scan(output_step, start_outs, key_pieces)[0], 0).reshape(
        tokens, HEADS * HEAD
    )
    attended_low = attended_wide.astype(jnp.bfloat16)
    attn_rows = jnp.dot(attended_low, o_weight, preferred_element_type=jnp.float32).astype(
        jnp.bfloat16
    )
    resid = input_wide + attn_rows.astype(jnp.float32)
    scale_two = rms_scale(resid)
    normed_two = resid * scale_two
    normed2_low = (normed_two * gain_moe).astype(jnp.bfloat16)
    choice_ids = expert_ids[0].reshape(-1)
    onehot = (choice_ids[:, None] == jnp.arange(experts, dtype=jnp.int32)[None, :]).astype(
        jnp.int32
    )
    rank = jnp.sum((jnp.cumsum(onehot, 0) - 1) * onehot, 1)
    target = choice_ids * capacity + rank
    gates = gate_weights[0]
    outgoing = (
        jnp.zeros((experts * capacity, width), jnp.bfloat16)
        .at[target]
        .set(jnp.repeat(normed2_low, TOPK, axis=0))
    )
    arrived = to_experts(outgoing.reshape(count, exp_dev, capacity, width))[0]
    gate_full, up_full, down_full = (
        lax.all_gather(w_gate, "fsdp", axis=1, tiled=True),
        lax.all_gather(w_up, "fsdp", axis=1, tiled=True),
        lax.all_gather(w_down, "fsdp", axis=2, tiled=True),
    )
    gate_pre = jnp.einsum("erd,edf->erf", arrived, gate_full, preferred_element_type=jnp.float32)
    up_pre = jnp.einsum("erd,edf->erf", arrived, up_full, preferred_element_type=jnp.float32)
    sigma = jax.nn.sigmoid(gate_pre)
    activated = gate_pre * sigma
    hidden_low = (activated * up_pre).astype(jnp.bfloat16)
    expert_out = jnp.einsum(
        "erf,efd->erd", hidden_low, down_full, preferred_element_type=jnp.float32
    ).astype(jnp.bfloat16)
    returned = from_experts(expert_out[None]).reshape(experts * capacity, width)
    picked = returned[target].astype(jnp.float32).reshape(tokens, TOPK, width)
    result = resid + jnp.sum(gates[:, :, None] * picked, 1)
    grad_y = cotangent[0].astype(jnp.float32)
    grad_slots = (gates.reshape(-1)[:, None] * jnp.repeat(grad_y, TOPK, axis=0)).astype(
        jnp.bfloat16
    )
    grad_buffer = jnp.zeros((experts * capacity, width), jnp.bfloat16).at[target].set(grad_slots)
    grad_out = to_experts(grad_buffer.reshape(count, exp_dev, capacity, width))[0]
    grad_hidden = jnp.einsum(
        "erd,efd->erf", grad_out, down_full, preferred_element_type=jnp.float32
    )
    grad_gate = (grad_hidden * up_pre * (sigma * (1.0 + gate_pre * (1.0 - sigma)))).astype(
        jnp.bfloat16
    )
    grad_up = (grad_hidden * activated).astype(jnp.bfloat16)
    grad_in = jnp.einsum("erf,edf->erd", grad_gate, gate_full, preferred_element_type=jnp.float32)
    grad_in = (
        grad_in + jnp.einsum("erf,edf->erd", grad_up, up_full, preferred_element_type=jnp.float32)
    ).astype(jnp.bfloat16)
    down_terms = jnp.einsum(
        "erf,erd->efd", hidden_low, grad_out, preferred_element_type=jnp.float32
    )
    gate_terms = jnp.einsum("erd,erf->edf", arrived, grad_gate, preferred_element_type=jnp.float32)
    up_terms = jnp.einsum("erd,erf->edf", arrived, grad_up, preferred_element_type=jnp.float32)
    w_gate_grad, w_up_grad, w_down_grad = (
        lax.psum_scatter(
            gate_terms.astype(jnp.bfloat16), "fsdp", scatter_dimension=1, tiled=True
        ).astype(jnp.float32),
        lax.psum_scatter(
            up_terms.astype(jnp.bfloat16), "fsdp", scatter_dimension=1, tiled=True
        ).astype(jnp.float32),
        lax.psum_scatter(
            down_terms.astype(jnp.bfloat16), "fsdp", scatter_dimension=2, tiled=True
        ).astype(jnp.float32),
    )
    grad_back = from_experts(grad_in[None]).reshape(experts * capacity, width)
    grad_normed2 = jnp.sum(grad_back[target].astype(jnp.float32).reshape(tokens, TOPK, width), 1)
    gain_moe_part = jnp.sum(grad_normed2 * normed_two, 0)
    grad_resid = grad_y + norm_back(grad_normed2 * gain_moe, normed_two, scale_two)
    grad_attn_rows = grad_resid.astype(jnp.bfloat16)
    o_weight_grad = cross_rows(attended_low, grad_attn_rows)
    grad_o_low = cross_cols(grad_attn_rows, o_weight).astype(jnp.bfloat16)
    grad_o_tiles = grad_o_low.reshape(parts, tile, KV_HEADS, repeat, HEAD)
    delta_rows = jnp.sum(
        grad_o_low.astype(jnp.float32).reshape(parts, tile, KV_HEADS, repeat, HEAD)
        * attended_wide.reshape(parts, tile, KV_HEADS, repeat, HEAD),
        -1,
    )
    delta_tiles = jnp.transpose(delta_rows, (0, 2, 3, 1))

    def back_step(carry, piece):
        grads_q = list(carry)
        grad_k = jnp.zeros((tile, KV_HEADS, HEAD), jnp.float32)
        grad_v = jnp.zeros((tile, KV_HEADS, HEAD), jnp.float32)
        query_part = 0
        mask = tile_mask(query_part, piece[2][0], piece[3][0])

        def back_update(
            state, query_part=query_part, key_tile=piece[0][0], value_tile=piece[1][0], mask=mask
        ):
            grad_q_part, grad_k_part, grad_v_part = state
            scores = tile_scores(query_part, key_tile, mask)
            probs = jnp.exp(scores - log_total[query_part][..., None])
            probs_low = probs.astype(jnp.bfloat16)
            grad_probs = jnp.einsum(
                "qgrd,kgd->grqk",
                grad_o_tiles[query_part],
                value_tile,
                preferred_element_type=jnp.float32,
            )
            grad_scores = (probs * (grad_probs - delta_tiles[query_part][..., None])).astype(
                jnp.bfloat16
            )
            grad_q_part = grad_q_part + jnp.einsum(
                "grqk,kgd->qgrd", grad_scores, key_tile, preferred_element_type=jnp.float32
            )
            grad_k_part = jnp.einsum(
                "grqk,qgrd->kgd",
                grad_scores,
                q_tiles[query_part],
                preferred_element_type=jnp.float32,
            )
            grad_v_part = jnp.einsum(
                "grqk,qgrd->kgd",
                probs_low,
                grad_o_tiles[query_part],
                preferred_element_type=jnp.float32,
            )
            return (grad_q_part, grad_k_part, grad_v_part)

        grads_q[query_part], grad_k, grad_v = lax.cond(
            jnp.any(mask), back_update, keep_same, (grads_q[query_part], grad_k, grad_v)
        )
        key_terms = [
            jnp.concatenate([grad_k.reshape(tile, kv_width), grad_v.reshape(tile, kv_width)], 1)
        ]
        return (tuple(grads_q), jnp.concatenate(key_terms, 0))

    start_grads = tuple(
        (jnp.zeros((tile, KV_HEADS, repeat, HEAD), jnp.float32) for query_part in range(parts))
    )
    grads_q_final, key_terms_all = lax.scan(back_step, start_grads, key_pieces)
    grad_q_rot = grads_q_final[0].reshape(tokens, HEADS, HEAD) * scale
    grad_kv = lax.psum_scatter(
        key_terms_all.reshape(count * tokens, 2 * kv_width).astype(jnp.bfloat16),
        "ctx",
        scatter_dimension=0,
        tiled=True,
    ).astype(jnp.float32)
    grad_q_raw = (
        rotate(grad_q_rot, cosine, -sine).reshape(tokens, HEADS * HEAD).astype(jnp.bfloat16)
    )
    grad_k_raw = (
        rotate((grad_kv[:, :kv_width] * scale).reshape(tokens, KV_HEADS, HEAD), cosine, -sine)
        .reshape(tokens, kv_width)
        .astype(jnp.bfloat16)
    )
    grad_v_low = grad_kv[:, kv_width:].astype(jnp.bfloat16)
    q_weight_grad = cross_rows(normed_low, grad_q_raw)
    k_weight_grad = cross_rows(normed_low, grad_k_raw)
    v_weight_grad = cross_rows(normed_low, grad_v_low)
    grad_normed1 = (
        cross_cols(grad_q_raw, q_weight)
        + cross_cols(grad_k_raw, k_weight)
        + cross_cols(grad_v_low, v_weight)
    )
    gain_attn_part = jnp.sum(grad_normed1 * normed_one, 0)
    grad_input_attn = norm_back(grad_normed1 * gain_attn, normed_one, scale_one).astype(
        jnp.bfloat16
    )
    grad_rows_out = (grad_resid + grad_input_attn.astype(jnp.float32)).astype(jnp.bfloat16)
    gain_attn_grad, wq_grad, wk_grad, wv_grad, wo_grad, gain_moe_grad = (
        lax.psum_scatter(gain_attn_part, ("ctx", "fsdp"), scatter_dimension=0, tiled=True),
        lax.psum_scatter(q_weight_grad, ("ctx", "fsdp"), scatter_dimension=0, tiled=True),
        lax.psum_scatter(k_weight_grad, ("ctx", "fsdp"), scatter_dimension=0, tiled=True),
        lax.psum_scatter(v_weight_grad, ("ctx", "fsdp"), scatter_dimension=0, tiled=True),
        lax.psum_scatter(o_weight_grad, ("ctx", "fsdp"), scatter_dimension=1, tiled=True),
        lax.psum_scatter(gain_moe_part, ("ctx", "fsdp"), scatter_dimension=0, tiled=True),
    )
    return (
        result.astype(jnp.bfloat16)[None],
        grad_rows_out[None],
        gain_attn_grad,
        wq_grad,
        wk_grad,
        wv_grad,
        wo_grad,
        gain_moe_grad,
        w_gate_grad,
        w_up_grad,
        w_down_grad,
    )


def solution(mesh):
    return jax.shard_map(
        local,
        mesh=mesh,
        in_specs=(
            P("fsdp", "ctx", None),
            P("fsdp", None),
            P("fsdp", "ctx", None),
            P("fsdp", "ctx", None),
            P(("ctx", "fsdp")),
            P(("ctx", "fsdp"), None),
            P(("ctx", "fsdp"), None),
            P(("ctx", "fsdp"), None),
            P(None, ("ctx", "fsdp")),
            P(("ctx", "fsdp")),
            P("ctx", "fsdp", None),
            P("ctx", "fsdp", None),
            P("ctx", None, "fsdp"),
            P("fsdp", "ctx", None),
        ),
        out_specs=(
            P("fsdp", "ctx", None),
            P("fsdp", "ctx", None),
            P(("ctx", "fsdp")),
            P(("ctx", "fsdp"), None),
            P(("ctx", "fsdp"), None),
            P(("ctx", "fsdp"), None),
            P(None, ("ctx", "fsdp")),
            P(("ctx", "fsdp")),
            P("ctx", "fsdp", None),
            P("ctx", "fsdp", None),
            P("ctx", None, "fsdp"),
        ),
        check_vma=False,
    )
```

profile of v0, /device:TPU:0, one launch (start us, length us, event | category | flops | bytes accessed | tf_op | source)
XLA Modules:
  0.0 2049.2 jit_solution(6488295323399504661)
XLA Ops:
  10.8 42.1 %all-reduce.5 = (bf16[1536]{0:T(1024)(128)(2,1)S(1)}, bf16[1536]{0:T(1024)(128)(2,1)}) all-reduce(bf16[1536]{0:T(1024)(128)(2,1)S(1)} %dynamic-update-slice, bf16[1536]{0:T(1024)(128)(2,1)S(1)} %dynamic-update-slice.1), channel_id=1, replica_groups=mesh['ctx'=8,'fsdp'=4] {'ctx','fsdp'}, use_global_device_ids=true, to_apply=%add | all-reduce | flops 3072 | bytes 12288
  54.5 42.9 %all_gather.34 = bf16[1536,256]{1,0:T(8,128)(2,1)S(1)} all-gather(bf16[48,256]{1,0:T(8,128)(2,1)} %param.32), channel_id=1, replica_groups=mesh['ctx'=8,'fsdp'=4] {'ctx','fsdp'}, dimensions={0}, use_global_device_ids=true | all-gather | bytes 811008 | tf_op jit(solution)/shard_map/all_gather | solution.py:110
  100.3 40.3 %all_gather.37 = bf16[1536,256]{1,0:T(8,128)(2,1)S(1)} all-gather(bf16[48,256]{1,0:T(8,128)(2,1)S(1)} %copy-done.47), channel_id=1, replica_groups=mesh['ctx'=8,'fsdp'=4] {'ctx','fsdp'}, dimensions={0}, use_global_device_ids=true | all-gather | bytes 811008 | tf_op jit(solution)/shard_map/all_gather | solution.py:111
  198.4 179.7 %all-gather.10.cloned.1.call-done = bf16[1536,1536]{1,0:T(8,128)(2,1)} async-done(((bf16[48,1536]{1,0:T(8,128)(2,1)}), bf16[1536,1536]{1,0:T(8,128)(2,1)}) %all-gather.10.cloned.1.call-update) | async-done | bytes 4718608 | tf_op jit(solution)/shard_map/all_gather | solution.py:109
  391.1 16.1 while.40
  408.7 27.9 %while.41 = (s32[]{:T(128)}, f32[384,2,6,128]{3,0,2,1:T(8,128)S(1)}, s32[384]{0:T(512)S(1)}, s32[8,1,384]{2,1,0:T(1,128)}, s32[8,1,384]{2,1,0:T(1,128)}, /*index...) while((s32[]{:T(128)}, ...), condition=%wide.region_16.17_spmd, body=%wide.region_12.16_spmd.sunk | while | flops 914227200 | bytes 6624439 | solution.py:214
  474.9 62.3 %all-to-all-start = ((bf16[8,2,144,1536]{3,2,1,0:T(8,128)(2,1)}), bf16[8,2,144,1536]{3,2,1,0:T(8,128)(2,1)}, u32[]{:S(2)}, u32[]{:S(2)}) async-start(bf16[8,2,144,1536]{3,2,1,0:T(8,128)(2,1)} %bitcast.264), calls=%async_computation | async-start | bytes 14155776 | tf_op jit(solution)/shard_map/all_to_all | solution.py:67
  545.0 147.7 %all-to-all-done = bf16[8,2,144,1536]{3,2,1,0:T(8,128)(2,1)} async-done(((bf16[8,2,144,1536]{3,2,1,0:T(8,128)(2,1)}), bf16[8,2,144,1536]{3,2,1,0:T(8,128)(2,1)}, u32[]{:S(2)}, u32[]{:S(2)}) %all-to-all-start) | async-done | bytes 7077920 | tf_op jit(solution)/shard_map/all_to_all | solution.py:67
  721.7 16.0 multiply_convert_fusion.1
  759.4 35.4 %copy.138 = bf16[1,2,1152,1536]{3,1,0,2:T(2,128)(2,1)} copy(bf16[1,2,1152,1536]{3,2,1,0:T(8,128)(2,1)S(1)} %fusion.49) | data formatting | bytes 14155776 | tf_op jit(solution)/shard_map/broadcast_in_dim | solution.py:287
  808.4 35.2 %copy.134 = bf16[1,2,1152,1536]{3,1,0,2:T(2,128)(2,1)} copy(bf16[1,2,1152,1536]{3,2,1,0:T(8,128)(2,1)S(1)} %fusion.50) | data formatting | bytes 14155776 | tf_op jit(solution)/shard_map/broadcast_in_dim | solution.py:251
  843.6 110.6 %all-to-all-done.3 = bf16[1,2,1152,1536]{3,1,0,2:T(2,128)(2,1)} async-done(((bf16[1,2,1152,1536]{3,1,0,2:T(2,128)(2,1)}), bf16[1,2,1152,1536]{3,1,0,2:T(2,128)(2,1)}, u32[]{:S(2)}, u32[]{:S(2)}) %all-to-all-start.3) | async-done | bytes 7077920 | tf_op jit(solution)/shard_map/all_to_all | solution.py:71
  1005.1 108.0 %all-to-all-done.1 = bf16[1,2,1152,1536]{3,1,0,2:T(2,128)(2,1)} async-done(((bf16[1,2,1152,1536]{3,1,0,2:T(2,128)(2,1)}), bf16[1,2,1152,1536]{3,1,0,2:T(2,128)(2,1)}, u32[]{:S(2)}, u32[]{:S(2)}) %all-to-all-start.1) | async-done | bytes 7077920 | tf_op jit(solution)/shard_map/all_to_all | solution.py:71
  1120.4 14.7 gather_fusion
  1174.1 71.3 %while.42 = (s32[]{:T(128)}, f32[384,2,6,128]{3,0,2,1:T(8,128)S(1)}, bf16[8,384,512]{2,1,0:T(8,128)(2,1)}, s32[384]{0:T(512)S(1)}, s32[8,1,384]{2,1,0:T(1,128)},...) while((s32[]{:T(128)}, ...), condition=%wide.region_31.32_spmd, body=%wide.region_27.31_spmd.sunk | while | flops 2284584960 | bytes 50598240 | solution.py:353
  1297.5 105.1 %reduce-scatter.11.cloned.1.call-done = bf16[384,512]{1,0:T(8,128)(2,1)} async-done(((bf16[3072,512]{1,0:T(8,128)(2,1)}), bf16[384,512]{1,0:T(8,128)(2,1)}) %reduce-scatter.11.cloned.1.call-update) | async-done | bytes 393232 | tf_op jit(solution)/shard_map/reduce_scatter | solution.py:355
  1432.5 19.6 reduce-scatter.25.cloned.1.call-done
  1460.9 41.6 %reduce-scatter.21.cloned.1.call-done = bf16[2,384,768]{2,1,0:T(8,128)(2,1)} async-done(((bf16[2,1536,768]{2,1,0:T(8,128)(2,1)}), bf16[2,384,768]{2,1,0:T(8,128)(2,1)}) %reduce-scatter.21.cloned.1.call-update) | async-done | bytes 1179664 | tf_op jit(solution)/shard_map/reduce_scatter | solution.py:277
  1505.3 47.6 %reduce-scatter.23.cloned.1.call-done = bf16[2,384,768]{2,1,0:T(8,128)(2,1)} async-done(((bf16[2,1536,768]{2,1,0:T(8,128)(2,1)}), bf16[2,384,768]{2,1,0:T(8,128)(2,1)}) %reduce-scatter.23.cloned.1.call-update) | async-done | bytes 1179664 | tf_op jit(solution)/shard_map/reduce_scatter | solution.py:280
  1564.3 39.6 %all-reduce.4 = (f32[1536]{0:T(1024)}, f32[1536]{0:T(1024)}) all-reduce(f32[1536]{0:T(1024)} %get-tuple-element.497, f32[1536]{0:T(1024)} %get-tuple-element.495), channel_id=3, replica_groups=mesh['ctx'=8,'fsdp'=4] {'ctx','fsdp'}, use_global_device_ids=true, to_apply=%region_35.36.clone | all-reduce | flops 3072 | bytes 24576
  1610.1 46.4 %reduce-scatter.15.cloned.1.call-done = f32[48,256]{1,0:T(8,128)} async-done(((f32[1536,256]{1,0:T(8,128)}), f32[48,256]{1,0:T(8,128)}) %reduce-scatter.15.cloned.1.call-update) | async-done | bytes 49168 | tf_op jit(solution)/shard_map/reduce_scatter | solution.py:386
  1656.5 102.7 %reduce-scatter.17.cloned.1.call-done = f32[48,256]{1,0:T(8,128)} async-done(((f32[1536,256]{1,0:T(8,128)}), f32[48,256]{1,0:T(8,128)}) %reduce-scatter.17.cloned.1.call-update) | async-done | bytes 49168 | tf_op jit(solution)/shard_map/reduce_scatter | solution.py:387
  1759.2 141.9 %reduce-scatter.19.cloned.1.call-done = f32[1536,48]{0,1:T(8,128)} async-done(((f32[1536,1536]{0,1:T(8,128)}), f32[1536,48]{0,1:T(8,128)}) %reduce-scatter.19.cloned.1.call-update) | async-done | bytes 294928 | tf_op jit(solution)/shard_map/reduce_scatter | solution.py:388
  1901.1 141.1 %reduce-scatter.13.cloned.1.call-done = f32[48,1536]{1,0:T(8,128)} async-done(((f32[1536,1536]{1,0:T(8,128)}), f32[48,1536]{1,0:T(8,128)}) %reduce-scatter.13.cloned.1.call-update) | async-done | bytes 294928 | tf_op jit(solution)/shard_map/reduce_scatter | solution.py:385
  (400 shorter events, 518.0 us)
Async XLA Ops:
  7.2 183.8 %all-gather.8.cloned.1.call-start = ((), (), s32[]{:S(2)}) async-start(), calls=%async_computation.12 | async-start | bytes 1769472 | tf_op jit(solution)/shard_map/all_gather | solution.py:138
  52.9 331.9 %copy-start.32 = (f32[1536]{0:T(1024)}, f32[1536]{0:T(1024)S(1)}, u32[]{:S(2)}) copy-start(f32[1536]{0:T(1024)S(1)} %convert_element_type.210) | copy-start | bytes 18436
  100.3 94.3 %all-gather.12.cloned.1.call-start = ((), (), s32[]{:S(2)}) async-start(), calls=%async_computation.14 | async-start | bytes 1769472 | tf_op jit(solution)/shard_map/all_gather | solution.py:139
  142.8 235.4 %all-gather.10.cloned.1.call-start = ((), (), s32[]{:S(2)}) async-start(), calls=%async_computation.13 | async-start | bytes 4866048 | tf_op jit(solution)/shard_map/all_gather | solution.py:109
  143.5 299.9 %all-gather.14.cloned.1.call-start = ((), (), s32[]{:S(2)}) async-start(), calls=%async_computation.15 | async-start | bytes 4866048 | tf_op jit(solution)/shard_map/all_gather | solution.py:112
  184.5 290.3 %all-to-all-start.2 = ((bf16[8,2,144,1536]{3,2,1,0:T(8,128)(2,1)}), bf16[8,2,144,1536]{3,2,1,0:T(8,128)(2,1)}, u32[]{:S(2)}, u32[]{:S(2)}) async-start(bf16[8,2,144,1536]{3,2,1,0:T(8,128)(2,1)} %bitcast.263), calls=%async_computation.2 | async-start | bytes 14155776 | tf_op jit(solution)/shard_map/all_to_all | solution.py:67
  189.5 509.6 %all-gather.16.cloned.1.call-start = ((), (), s32[]{:S(2)}) async-start(), calls=%async_computation.16 | async-start | bytes 5898240 | tf_op jit(solution)/shard_map/all_gather | solution.py:239
  474.9 217.9 %all-to-all-start = ((bf16[8,2,144,1536]{3,2,1,0:T(8,128)(2,1)}), bf16[8,2,144,1536]{3,2,1,0:T(8,128)(2,1)}, u32[]{:S(2)}, u32[]{:S(2)}) async-start(bf16[8,2,144,1536]{3,2,1,0:T(8,128)(2,1)} %bitcast.264), calls=%async_computation | async-start | bytes 14155776 | tf_op jit(solution)/shard_map/all_to_all | solution.py:67
  537.2 173.4 %all-gather.18.cloned.1.call-start = ((), (), s32[]{:S(2)}) async-start(), calls=%async_computation.17 | async-start | bytes 5898240 | tf_op jit(solution)/shard_map/all_gather | solution.py:240
  537.8 183.9 %all-gather.20.cloned.1.call-start = ((), (), s32[]{:S(2)}) async-start(), calls=%async_computation.18 | async-start | bytes 5898240 | tf_op jit(solution)/shard_map/all_gather | solution.py:241
  794.7 159.4 %all-to-all-start.3 = ((bf16[1,2,1152,1536]{3,1,0,2:T(2,128)(2,1)}), bf16[1,2,1152,1536]{3,1,0,2:T(2,128)(2,1)}, u32[]{:S(2)}, u32[]{:S(2)}) async-start(bf16[1,2,1152,1536]{3,1,0,2:T(2,128)(2,1)} %copy.138), calls=%async_computation.3 | async-start | bytes 14155776 | tf_op jit(solution)/shard_map/all_to_all | solution.py:71
  843.6 115.5 %copy-start.49 = (f32[1,384,4]{1,2,0:T(4,128)S(1)}, f32[1,384,4]{1,2,0:T(4,128)}, u32[]{:S(2)}) copy-start(f32[1,384,4]{1,2,0:T(4,128)} %param.29) | copy-start | bytes 18436
  954.2 158.9 %all-to-all-start.1 = ((bf16[1,2,1152,1536]{3,1,0,2:T(2,128)(2,1)}), bf16[1,2,1152,1536]{3,1,0,2:T(2,128)(2,1)}, u32[]{:S(2)}, u32[]{:S(2)}) async-start(bf16[1,2,1152,1536]{3,1,0,2:T(2,128)(2,1)} %copy.134), calls=%async_computation.1 | async-start | bytes 14155776 | tf_op jit(solution)/shard_map/all_to_all | solution.py:71
  959.0 443.6 %reduce-scatter.11.cloned.1.call-start = ((), (), s32[]{:S(2)}) async-start(), calls=%async_computation.19 | async-start | bytes 3538944 | tf_op jit(solution)/shard_map/reduce_scatter | solution.py:355
  1245.5 206.6 %reduce-scatter.25.cloned.1.call-start = ((), (), s32[]{:S(2)}) async-start(), calls=%async_computation.26 | async-start | bytes 5898240
  1275.2 227.3 %reduce-scatter.21.cloned.1.call-start = ((), (), s32[]{:S(2)}) async-start(), calls=%async_computation.24 | async-start | bytes 5898240 | tf_op jit(solution)/shard_map/reduce_scatter | solution.py:277
  1286.3 266.6 %reduce-scatter.23.cloned.1.call-start = ((), (), s32[]{:S(2)}) async-start(), calls=%async_computation.25 | async-start | bytes 5898240 | tf_op jit(solution)/shard_map/reduce_scatter | solution.py:280
  1297.4 110.7 %copy-start.4 = (bf16[1,384,1536]{2,1,0:T(8,128)(2,1)S(1)}, bf16[1,384,1536]{2,1,0:T(8,128)(2,1)}, u32[]{:S(2)}) copy-start(bf16[1,384,1536]{2,1,0:T(8,128)(2,1)} %param.26) | copy-start | bytes 3538948
  1297.4 110.6 %copy-start.33 = (f32[1536]{0:T(1024)S(1)}, f32[1536]{0:T(1024)}, u32[]{:S(2)}) copy-start(f32[1536]{0:T(1024)} %copy-done.32) | copy-start | bytes 18436
  1297.4 110.6 %copy-start.39 = (f32[384]{0:T(512)S(1)}, f32[384]{0:T(512)}, u32[]{:S(2)}) copy-start(f32[384]{0:T(512)} %copy-done.37) | copy-start | bytes 4612
  1297.5 359.0 %reduce-scatter.15.cloned.1.call-start = ((), (), s32[]{:S(2)}) async-start(), calls=%async_computation.21 | async-start | bytes 1622016 | tf_op jit(solution)/shard_map/reduce_scatter | solution.py:386
  1410.0 349.2 %reduce-scatter.17.cloned.1.call-start = ((), (), s32[]{:S(2)}) async-start(), calls=%async_computation.22 | async-start | bytes 1622016 | tf_op jit(solution)/shard_map/reduce_scatter | solution.py:387
  1413.1 488.0 %reduce-scatter.19.cloned.1.call-start = ((), (), s32[]{:S(2)}) async-start(), calls=%async_computation.23 | async-start | bytes 9732096 | tf_op jit(solution)/shard_map/reduce_scatter | solution.py:388
  1421.9 620.3 %reduce-scatter.13.cloned.1.call-start = ((), (), s32[]{:S(2)}) async-start(), calls=%async_computation.20 | async-start | bytes 9732096 | tf_op jit(solution)/shard_map/reduce_scatter | solution.py:385
  (55 other events, 658.2 us)
Sparse Core Ops, SparseCore 0:
  100.4 42.9 all-gather.7
  146.1 43.0 all-gather.11
  192.1 186.0 all-gather.9
  380.9 62.4 all-gather.13
  444.8 36.2 all-gather.15
  539.3 37.9 all-gather.17
  578.9 37.3 all-gather.19
  1245.6 156.9 reduce-scatter.10
  1405.1 46.9 reduce-scatter.24
  1454.6 47.7 reduce-scatter.20
  1505.0 47.8 reduce-scatter.22
  1559.4 97.0 reduce-scatter.14
  1663.1 96.0 reduce-scatter.16
  1766.5 134.4 reduce-scatter.18
  1907.4 134.7 reduce-scatter.12
where the time goes:
time: 2060 us; the launch traced here: 2050 us
  waiting for transfers between devices  1200 us (58%)
  local copies, waits for them, and re-layouts  297 us (14%)
  blocking collectives  165 us (8%)
  matrix products  164 us (8%)
  other arithmetic  117 us (6%)
  starting transfers between devices  78.4 us (4%)
    all_to_all x2, waiting for transfers between devices, from_experts(): lax.all_to_all(buffer, 'ctx', split_axis=2, concat_axis=0, tiled=True)  219 us
    all_gather x1, waiting for transfers between devices, local(): lax.all_gather(wq, ('ctx', 'fsdp'), axis=0, tiled=True)  180 us
    all_to_all x2, waiting for transfers between devices, to_experts(): lax.all_to_all(buffer, 'ctx', split_axis=0, concat_axis=2, tiled=True)  148 us
    reduce_scatter x1, waiting for transfers between devices, local(): lax.psum_scatter(o_weight_grad, ('ctx', 'fsdp'), scatter_dimension=1, til...  142 us
    reduce_scatter x1, waiting for transfers between devices, local(): lax.psum_scatter(q_weight_grad, ('ctx', 'fsdp'), scatter_dimension=0, til...  141 us
    reduce_scatter x1, waiting for transfers between devices, local(): lax.psum_scatter(key_terms_all.reshape(count * tokens, 2 * kv_width).asty...  105 us
    reduce_scatter x1, waiting for transfers between devices, local(): lax.psum_scatter(v_weight_grad, ('ctx', 'fsdp'), scatter_dimension=0, til...  103 us
    unnamed x2, blocking collectives  81.7 us
  transfers between devices with their start and end apart: 19, of which 13 were waited for; matrix products, arithmetic and copies ran while one was open for 18% of the time, Pallas kernels for 0%

commit v1 on v0

v1 whole, which is shorter than its diff:
```python
import math

import jax
import jax.numpy as jnp
from jax import lax
from jax.experimental import pallas as pl
from jax.experimental.pallas import tpu as pltpu
from jax.sharding import PartitionSpec as P

HEADS = 12
KV_HEADS = 2
HEAD = 128
TOPK = 4
REPEAT = HEADS // KV_HEADS
HQ = HEADS * HEAD
KVW = KV_HEADS * HEAD
LANES = 128

EPS = 1e-06
ROPE_BASE = 10000.0
NEG = -1e30
BF = jnp.bfloat16
F32 = jnp.float32
NN = ((1,), (0,))
NT = ((1,), (1,))
TN = ((0,), (0,))
ANY = pl.BlockSpec(memory_space=pl.ANY)
MIB = 1024 * 1024


def mm(left, right, dims=NN):
    return lax.dot_general(left, right, (dims, ((), ())), preferred_element_type=F32)


def params(grid_rank, limit=56):
    return pltpu.CompilerParams(
        dimension_semantics=("arbitrary",) * grid_rank, vmem_limit_bytes=limit * MIB
    )


def cost(flops, size, exps=0):
    return pl.CostEstimate(flops=int(flops), bytes_accessed=int(size), transcendentals=int(exps))


def sds(shape, dtype):
    return jax.ShapeDtypeStruct(shape, dtype)


def whole(shape):
    return pl.BlockSpec(shape, lambda *_: (0,) * len(shape))


class Ring:
    def __init__(self, count):
        self.count = count
        self.low_pair = count == 8
        self.length = count // 2
        self.me = lax.axis_index("ctx")
        if self.low_pair:
            self.line, self.pair = self.me // 2, self.me % 2
        else:
            self.line, self.pair = self.me % self.length, self.me // self.length
        if self.length == 4:
            self.table = [[0, 1, 2, 3], [1, 0, 2, 3], [2, 3, 1, 0], [3, 2, 1, 0]]
        else:
            self.table = [
                [(place + step) % self.length for step in range(self.length)]
                for place in range(self.length)
            ]

    def index(self, line, pair):
        return line * 2 + pair if self.low_pair else pair * self.length + line

    def move(self, array, hops):
        pairs = [
            (self.index(source, side), self.index(target, side))
            for source, target in hops
            for side in (0, 1)
        ]
        return lax.ppermute(array, "ctx", pairs)

    def swap(self, array):
        pairs = [
            (self.index(place, side), self.index(place, 1 - side))
            for place in range(self.length)
            for side in (0, 1)
        ]
        return lax.ppermute(array, "ctx", pairs)

    def sources(self):
        line = jnp.asarray(self.table, jnp.int32)[self.line]
        side = jnp.stack([self.pair, 1 - self.pair]).astype(jnp.int32)
        return self.index(line[:, None], side[None, :]).reshape(-1).astype(jnp.int32)

    def gather(self, array):
        if self.length != 4:
            everything = lax.all_gather(array, "ctx", axis=0)
            order = self.sources()
            rows = [
                lax.dynamic_index_in_dim(everything, order[slot], 0, keepdims=False)
                for slot in range(self.count)
            ]
            return [(rows[2 * step], rows[2 * step + 1]) for step in range(self.length)]
        ends = [(1, 0), (2, 3)]
        middle = [(1, 2), (2, 1)]
        couples = [(0, 1), (1, 0), (2, 3), (3, 2)]
        first = self.move(array, couples)
        cross = self.move(array, middle)
        swapped = self.swap(array)
        outward = self.move(cross, ends)
        cross_two = self.move(first, middle)
        second = cross + outward
        outward_two = self.move(cross_two, ends)
        third = cross_two + outward_two
        return [
            (array, swapped),
            (first, self.swap(first)),
            (second, self.swap(second)),
            (third, self.swap(third)),
        ]

    def scatter(self, parts):
        if self.length != 4:
            order = self.sources()
            rows = jnp.stack([part for couple in parts for part in couple])
            placed = jnp.zeros_like(rows).at[order].set(rows)
            return [lax.psum_scatter(placed, "ctx", scatter_dimension=0, tiled=False)]
        inward = [(0, 1), (3, 2)]
        middle = [(1, 2), (2, 1)]
        couples = [(0, 1), (1, 0), (2, 3), (3, 2)]
        third = parts[3][0] + self.swap(parts[3][1])
        from_end = self.move(third, inward)
        second = parts[2][0] + self.swap(parts[2][1])
        from_end_two = self.move(second, inward)
        crossed = self.move(third + from_end, middle)
        first = parts[1][0] + self.swap(parts[1][1])
        crossed_two = self.move(second + from_end_two, middle)
        last = self.move(first + crossed, couples)
        swapped = self.swap(parts[0][1])
        return [parts[0][0], swapped, crossed_two, last]


def neighbour(array, axis_size, bit):
    pairs = [(index, index ^ (1 << bit)) for index in range(axis_size)]
    return lax.ppermute(array, "fsdp", pairs)


def gather_shards(array, axis_size):
    slots = {0: array}
    bits = axis_size.bit_length() - 1
    for bit in reversed(range(bits)):
        for slot in list(slots):
            slots[slot | (1 << bit)] = neighbour(slots[slot], axis_size, bit)
    return [slots[slot] for slot in range(axis_size)]


def scatter_shards(slots, axis_size):
    bits = axis_size.bit_length() - 1
    slots = dict(enumerate(slots))
    for bit in range(bits):
        far = [slot for slot in slots if slot >> bit & 1]
        near = {slot: value for slot, value in slots.items() if not slot >> bit & 1}
        for slot in far:
            arrived = neighbour(slots[slot], axis_size, bit)
            if bit == bits - 1:
                return near[0], arrived
            near[slot ^ (1 << bit)] = near[slot ^ (1 << bit)] + arrived
        slots = near
    return slots[0], jnp.zeros_like(slots[0])


def turn(values, cosine, sine):
    return values * cosine + pltpu.roll(values, HEAD // 2, 1) * sine


def qkv_kernel(x_ref, w_ref, g_ref, cos_ref, sin_ref, q_ref, kv_ref, low_ref, gain_ref):
    step = pl.program_id(0)
    blocks = HQ // 512

    @pl.when(step == 0)
    def _():
        gains = jnp.transpose(g_ref[...].astype(F32))
        gain_ref[...] = gains[0:8]
        wide = x_ref[...].astype(F32)
        scale = lax.rsqrt(jnp.mean(wide * wide, -1, keepdims=True) + EPS)
        low_ref[...] = (wide * scale * gains[0:1]).astype(BF)

    raw = mm(low_ref[...], w_ref[...])
    cosine, sine = cos_ref[...], sin_ref[...]

    def turned(count):
        return [
            turn(raw[:, head * HEAD : (head + 1) * HEAD], cosine, sine).astype(BF)
            for head in range(count)
        ]

    @pl.when(step < blocks)
    def _():
        for head, value in enumerate(turned(4)):
            q_ref[:, head * HEAD : (head + 1) * HEAD] = value

    @pl.when(step == blocks)
    def _():
        for head, value in enumerate(turned(KV_HEADS)):
            kv_ref[:, head * HEAD : (head + 1) * HEAD] = value
        kv_ref[:, KVW:] = raw[:, KVW:].astype(BF)


def qkv_call(x, w_full, cosine, sine):
    tokens, width = x.shape
    blocks = HQ // 512
    return pl.pallas_call(
        qkv_kernel,
        name="qkv",
        grid=(blocks + 1,),
        in_specs=[
            whole((tokens, width)),
            pl.BlockSpec((width, 512), lambda i: (0, i)),
            pl.BlockSpec((width, LANES), lambda i: (0, (HQ + 2 * KVW) // LANES)),
            whole((tokens, HEAD)),
            whole((tokens, HEAD)),
        ],
        out_specs=[
            pl.BlockSpec((tokens, 512), lambda i: (0, jnp.minimum(i, HQ // 512 - 1))),
            whole((tokens, 2 * KVW)),
            whole((tokens, width)),
            whole((8, width)),
        ],
        out_shape=[
            sds((tokens, HQ), BF),
            sds((tokens, 2 * KVW), BF),
            sds((tokens, width), BF),
            sds((8, width), F32),
        ],
        compiler_params=params(1),
        cost_estimate=cost(2 * tokens * width * 2048, 10 * MIB),
    )(x, w_full, w_full, cosine, sine)


def load_kv(order_ref, slots, kv_all, sems):
    copies = [
        pltpu.make_async_copy(slot, kv_all.at[order_ref[2 + place]], sems.at[place])
        for place, slot in enumerate(slots)
    ]
    for copy in copies:
        copy.start()
    for copy in copies:
        copy.wait()


def attn_kernel(count, order_ref, q_ref, start_ref, *rest):
    slots = rest[:count]
    out_ref, total_ref, kv_all, totals, sems = rest[count:]
    head = pl.program_id(0)
    tokens = q_ref.shape[0]
    scale = HEAD ** (-0.5)
    me, first = order_ref[0], order_ref[1]

    @pl.when(head == 0)
    def _():
        load_kv(order_ref, slots, kv_all, sems)
        totals[...] = jnp.zeros_like(totals)

    group = head // REPEAT
    q = q_ref[...]
    start = start_ref[:, 0:1]
    rows = me * tokens + lax.broadcasted_iota(jnp.int32, (tokens, 1), 0)
    lanes = lax.broadcasted_iota(jnp.int32, (1, tokens), 1)

    def visit(block, carry):
        peak, total, acc = carry
        key = kv_all[block, :, pl.ds(pl.multiple_of(group * HEAD, HEAD), HEAD)]
        value = kv_all[block, :, pl.ds(pl.multiple_of(KVW + group * HEAD, HEAD), HEAD)]
        index = block * tokens + lanes
        mask = (index >= start) & (index <= rows)
        scores = jnp.where(mask, mm(q, key, NT) * scale, NEG)
        new_peak = jnp.maximum(peak, jnp.max(scores, -1, keepdims=True))
        weights = jnp.exp(scores - new_peak)
        keep = jnp.exp(peak - new_peak)
        total = total * keep + jnp.sum(weights, -1, keepdims=True)
        acc = acc * keep + mm(weights.astype(BF), value)
        return new_peak, total, acc

    begin = (
        jnp.full((tokens, 1), NEG, F32),
        jnp.zeros((tokens, 1), F32),
        jnp.zeros((tokens, HEAD), F32),
    )
    state = visit(me, begin)
    peak, total, acc = lax.fori_loop(first, me, visit, state)
    out_ref[...] = (acc / total).astype(BF)
    here = lax.broadcasted_iota(jnp.int32, (tokens, LANES), 1) == head
    totals[...] = jnp.where(here, peak + jnp.log(total), totals[...])

    @pl.when(head == HEADS - 1)
    def _():
        total_ref[...] = jnp.transpose(totals[...])[0:16]


def attn_call(order, q, start, slots):
    tokens = q.shape[0]
    count = len(slots)
    grid = pltpu.PrefetchScalarGridSpec(
        num_scalar_prefetch=1,
        grid=(HEADS,),
        in_specs=[
            pl.BlockSpec((tokens, HEAD), lambda h, _: (0, h)),
            pl.BlockSpec((tokens, LANES), lambda h, _: (0, 0)),
        ]
        + [ANY] * count,
        out_specs=[
            pl.BlockSpec((tokens, HEAD), lambda h, _: (0, h)),
            pl.BlockSpec((16, tokens), lambda h, _: (0, 0)),
        ],
        scratch_shapes=[
            pltpu.VMEM((count, tokens, 2 * KVW), BF),
            pltpu.VMEM((tokens, LANES), F32),
            pltpu.SemaphoreType.DMA((count,)),
        ],
    )
    return pl.pallas_call(
        lambda *refs: attn_kernel(count, *refs),
        name="attention",
        grid_spec=grid,
        out_shape=[sds((tokens, HQ), BF), sds((16, tokens), F32)],
        compiler_params=params(1),
        cost_estimate=cost(4 * tokens * tokens * count * HQ, 6 * MIB),
    )(order, q, start, *slots)


def attn_back_kernel(count, order_ref, q_ref, do_ref, start_ref, total_ref, delta_ref, *rest):
    cos_ref, sin_ref = rest[:2]
    slots = rest[2 : 2 + count]
    dq_ref = rest[2 + count]
    outs = rest[3 + count : 3 + 2 * count]
    kv_all, d_k, d_v, packed, sems = rest[3 + 2 * count :]
    head = pl.program_id(0)
    tokens = q_ref.shape[0]
    scale = HEAD ** (-0.5)
    me, first = order_ref[0], order_ref[1]

    @pl.when(head == 0)
    def _():
        load_kv(order_ref, slots, kv_all, sems)
        d_k[...] = jnp.zeros_like(d_k)
        d_v[...] = jnp.zeros_like(d_v)

    group = head // REPEAT
    own = pl.ds(pl.multiple_of(group * HEAD, HEAD), HEAD)
    q = q_ref[...]
    grad = do_ref[...]
    start = start_ref[0:1, :]
    log_total = total_ref[pl.ds(head, 1), :]
    delta = delta_ref[pl.ds(head, 1), :]
    columns = me * tokens + lax.broadcasted_iota(jnp.int32, (1, tokens), 1)
    sublanes = lax.broadcasted_iota(jnp.int32, (tokens, 1), 0)

    def visit(block, d_q):
        key = kv_all[block, :, own]
        value = kv_all[block, :, pl.ds(pl.multiple_of(KVW + group * HEAD, HEAD), HEAD)]
        index = block * tokens + sublanes
        mask = (index >= start) & (index <= columns)
        scores = jnp.where(mask, mm(key, q, NT) * scale - log_total, NEG)
        probs = jnp.exp(scores)
        grad_probs = mm(value, grad, NT)
        grad_scores = (probs * (grad_probs - delta)).astype(BF)
        d_v[block, :, own] += mm(probs.astype(BF), grad)
        d_k[block, :, own] += mm(grad_scores, q)
        return d_q + mm(grad_scores, key, TN)

    d_q = lax.fori_loop(first, me + 1, visit, jnp.zeros((tokens, HEAD), F32))
    dq_ref[...] = turn(d_q * scale, cos_ref[...], -sin_ref[...]).astype(BF)

    @pl.when(head == HEADS - 1)
    def _():
        copies = []
        for place in range(count):
            block = order_ref[2 + place]
            packed[place, :, 0:KVW] = d_k[block].astype(BF)
            packed[place, :, KVW:] = d_v[block].astype(BF)
            copies.append(pltpu.make_async_copy(packed.at[place], outs[place], sems.at[place]))
            copies[-1].start()
        for copy in copies:
            copy.wait()


def attn_back_call(order, q, grad, start, log_total, delta, cosine, sine, slots):
    tokens = q.shape[0]
    count = len(slots)

    def column(h, _):
        return (0, h)

    def fixed(h, _):
        return (0, 0)

    grid = pltpu.PrefetchScalarGridSpec(
        num_scalar_prefetch=1,
        grid=(HEADS,),
        in_specs=[
            pl.BlockSpec((tokens, HEAD), column),
            pl.BlockSpec((tokens, HEAD), column),
            pl.BlockSpec((8, tokens), fixed),
            pl.BlockSpec((16, tokens), fixed),
            pl.BlockSpec((16, tokens), fixed),
            pl.BlockSpec((tokens, HEAD), fixed),
            pl.BlockSpec((tokens, HEAD), fixed),
        ]
        + [ANY] * count,
        out_specs=[pl.BlockSpec((tokens, HEAD), column)] + [ANY] * count,
        scratch_shapes=[
            pltpu.VMEM((count, tokens, 2 * KVW), BF),
            pltpu.VMEM((count, tokens, KVW), F32),
            pltpu.VMEM((count, tokens, KVW), F32),
            pltpu.VMEM((count, tokens, 2 * KVW), BF),
            pltpu.SemaphoreType.DMA((count,)),
        ],
    )
    return pl.pallas_call(
        lambda *refs: attn_back_kernel(count, *refs),
        name="attention_back",
        grid_spec=grid,
        out_shape=[sds((tokens, HQ), BF)] + [sds((tokens, 2 * KVW), BF)] * count,
        compiler_params=params(1),
        cost_estimate=cost(10 * tokens * tokens * count * HQ, 10 * MIB),
    )(order, q, grad, start, log_total, delta, cosine, sine, *slots)


def out_kernel(x_ref, a_ref, w_ref, gain_ref, rows_ref, low_ref):
    rows = mm(a_ref[...], w_ref[...], NT).astype(BF)
    rows_ref[...] = rows
    resid = x_ref[...].astype(F32) + rows.astype(F32)
    scale = lax.rsqrt(jnp.mean(resid * resid, -1, keepdims=True) + EPS)
    low_ref[...] = (resid * scale * gain_ref[1:2]).astype(BF)


def out_call(x, attended, wo_t, gains):
    tokens, width = x.shape
    tile = 128
    return pl.pallas_call(
        out_kernel,
        name="attention_out",
        grid=(tokens // tile,),
        in_specs=[
            pl.BlockSpec((tile, width), lambda i: (i, 0)),
            pl.BlockSpec((tile, HQ), lambda i: (i, 0)),
            whole((width, HQ)),
            whole((8, width)),
        ],
        out_specs=[pl.BlockSpec((tile, width), lambda i: (i, 0))] * 2,
        out_shape=[sds((tokens, width), BF)] * 2,
        compiler_params=params(1),
        cost_estimate=cost(2 * tokens * width * HQ, 10 * MIB),
    )(x, attended, wo_t, gains)


def weight_copies(shards, own, kinds, held, sems):
    size = shards[0].shape[2]
    groups = []
    for expert in range(shards[0].shape[1]):
        copies = []
        for slot, shard in enumerate(shards):
            rows = pl.ds(pl.multiple_of((own ^ slot) * size, 16), size)
            for place, kind in enumerate(kinds):
                copies.append(
                    pltpu.make_async_copy(
                        shard.at[kind, expert],
                        held.at[place, expert, rows],
                        sems.at[place, expert, slot],
                    )
                )
        groups.append(copies)
    return groups


def fetch_weights(shards, own, kinds, held, sems):
    groups = weight_copies(shards, own, kinds, held, sems)
    step = pl.program_id(0)

    @pl.when(step == 0)
    def _():
        for copies in groups:
            for copy in copies:
                copy.start()

    for expert, copies in enumerate(groups):

        @pl.when(step == expert)
        def _():
            for copy in copies:
                copy.wait()


def route_kernel(shards_of, capacity, order_ref, d0_ref, d1_ref, *rest):
    shards = rest[:shards_of]
    p0_ref, p1_ref, gate_ref, rows_ref, hid_ref, held, sems = rest[shards_of:]
    expert = pl.program_id(0)
    tokens = d0_ref.shape[0]
    width = rows_ref.shape[2]
    fetch_weights(shards, order_ref[0], (2,), held, sems)
    wanted = (order_ref[1] * held.shape[1] + expert).astype(F32)
    before = lax.broadcasted_iota(jnp.int32, (tokens, tokens), 0) < lax.broadcasted_iota(
        jnp.int32, (tokens, tokens), 1
    )
    before = jnp.where(before, 1.0, 0.0).astype(BF)
    places = lax.broadcasted_iota(jnp.int32, (capacity, tokens), 0).astype(F32)
    for side, (ref, p_ref) in enumerate(((d0_ref, p0_ref), (d1_ref, p1_ref))):
        info = jnp.transpose(ref[:, width:].astype(F32))
        chosen = jnp.where(info[0:TOPK] == wanted, 1.0, 0.0)
        gate = jnp.sum(
            chosen * (info[TOPK : 2 * TOPK] + info[2 * TOPK : 3 * TOPK] + info[3 * TOPK : 4 * TOPK]),
            0,
            keepdims=True,
        )
        named = jnp.sum(chosen, 0, keepdims=True)
        rank = mm(jnp.broadcast_to(named, (8, tokens)).astype(BF), before)[0:1]
        picks = jnp.where((places == rank) & (named > 0.5), 1.0, 0.0)
        weight = jnp.sum(picks * gate, 1, keepdims=True)
        picks = picks.astype(BF)
        p_ref[0] = picks
        span = slice(side * capacity, (side + 1) * capacity)
        gate_ref[0, span] = jnp.broadcast_to(weight, (capacity, LANES))
        rows_ref[0, span] = (mm(picks, ref[:, :width]) * weight).astype(BF)
    hid_ref[0] = mm(rows_ref[0], held[0, expert])


def route_call(order, grads, shards, capacity, width):
    tokens = grads[0].shape[0]
    _, experts, size, hidden = shards[0].shape
    rows = 2 * capacity
    by_expert = lambda e, _: (e, 0, 0)
    grid = pltpu.PrefetchScalarGridSpec(
        num_scalar_prefetch=1,
        grid=(experts,),
        in_specs=[pl.BlockSpec(grads[0].shape, lambda e, _: (0, 0))] * 2 + [ANY] * len(shards),
        out_specs=[pl.BlockSpec((1, capacity, tokens), by_expert)] * 2
        + [
            pl.BlockSpec((1, rows, LANES), by_expert),
            pl.BlockSpec((1, rows, width), by_expert),
            pl.BlockSpec((1, rows, hidden), by_expert),
        ],
        scratch_shapes=[
            pltpu.VMEM((1, experts, width, hidden), BF),
            pltpu.SemaphoreType.DMA((1, experts, len(shards))),
        ],
    )
    return pl.pallas_call(
        lambda *refs: route_kernel(len(shards), capacity, *refs),
        name="route",
        grid_spec=grid,
        out_shape=[sds((experts, capacity, tokens), BF)] * 2
        + [
            sds((experts, rows, LANES), F32),
            sds((experts, rows, width), BF),
            sds((experts, rows, hidden), F32),
        ],
        compiler_params=params(1),
        cost_estimate=cost(2 * experts * rows * width * (hidden + tokens), 14 * MIB),
    )(order, *grads, *shards)


def expert_kernel(shards_of, capacity, order_ref, x0_ref, x1_ref, p0_ref, p1_ref, gh_ref, *rest):
    shards = rest[:shards_of]
    rows_ref, hid_ref, gg_ref, gu_ref, out0_ref, out1_ref, held, slot, acc, sems = rest[shards_of:]
    expert = pl.program_id(0)
    hidden = gh_ref.shape[2]
    width = x0_ref.shape[1]
    fetch_weights(shards, order_ref[0], (0, 1), held, sems)
    for side, (ref, p_ref) in enumerate(((x0_ref, p0_ref), (x1_ref, p1_ref))):
        span = slice(side * capacity, (side + 1) * capacity)
        rows_ref[0, span] = mm(p_ref[0], ref[...]).astype(BF)
    rows = rows_ref[0]
    tile = 256
    for start in range(0, hidden, tile):
        span = slice(start, start + tile)
        gate = mm(rows, held[0, expert, :, span])
        up = mm(rows, held[1, expert, :, span])
        grad = gh_ref[0, :, span]
        sigma = 1.0 / (1.0 + jnp.exp(-gate))
        active = gate * sigma
        hid_ref[0, :, span] = (active * up).astype(BF)
        gg_ref[0, :, span] = (grad * up * (sigma * (1.0 + gate * (1.0 - sigma)))).astype(BF)
        gu_ref[0, :, span] = (grad * active).astype(BF)
    tile = 512
    for start in range(0, width, tile):
        span = slice(start, start + tile)
        slot[:, span] = (
            mm(gg_ref[0], held[0, expert, span, :], NT)
            + mm(gu_ref[0], held[1, expert, span, :], NT)
        ).astype(BF)
    for side, (p_ref, out_ref) in enumerate(((p0_ref, out0_ref), (p1_ref, out1_ref))):
        span = slice(side * capacity, (side + 1) * capacity)
        term = mm(p_ref[0], slot[span], TN)

        @pl.when(expert == 0)
        def _():
            acc[side] = term

        @pl.when(expert > 0)
        def _():
            acc[side] += term

        @pl.when(expert == pl.num_programs(0) - 1)
        def _():
            out_ref[...] = acc[side].astype(BF)


def expert_call(order, xs, picks, grad_hidden, shards, capacity):
    tokens, width = xs[0].shape
    _, experts, size, hidden = shards[0].shape
    rows = 2 * capacity
    by_expert = lambda e, _: (e, 0, 0)
    fixed = lambda e, _: (0, 0)
    grid = pltpu.PrefetchScalarGridSpec(
        num_scalar_prefetch=1,
        grid=(experts,),
        in_specs=[pl.BlockSpec((tokens, width), fixed)] * 2
        + [pl.BlockSpec((1, capacity, tokens), by_expert)] * 2
        + [pl.BlockSpec((1, rows, hidden), by_expert)]
        + [ANY] * len(shards),
        out_specs=[pl.BlockSpec((1, rows, width), by_expert)]
        + [pl.BlockSpec((1, rows, hidden), by_expert)] * 3
        + [pl.BlockSpec((tokens, width), fixed)] * 2,
        scratch_shapes=[
            pltpu.VMEM((2, experts, width, hidden), BF),
            pltpu.VMEM((rows, width), BF),
            pltpu.VMEM((2, tokens, width), F32),
            pltpu.SemaphoreType.DMA((2, experts, len(shards))),
        ],
    )
    return pl.pallas_call(
        lambda *refs: expert_kernel(len(shards), capacity, *refs),
        name="experts",
        grid_spec=grid,
        out_shape=[sds((experts, rows, width), BF)]
        + [sds((experts, rows, hidden), BF)] * 3
        + [sds((tokens, width), BF)] * 2,
        compiler_params=params(1),
        cost_estimate=cost(2 * experts * rows * width * (4 * hidden + 2 * tokens), 24 * MIB),
    )(order, *xs, *picks, grad_hidden, *shards)


def down_kernel(shards_of, capacity, order_ref, hid_ref, gate_ref, p0_ref, p1_ref, *rest):
    shards = rest[:shards_of]
    out0_ref, out1_ref, held, slot, acc, sems = rest[shards_of:]
    expert = pl.program_id(0)
    width = out0_ref.shape[1]
    fetch_weights(shards, order_ref[0], (2,), held, sems)
    tile = 512
    for start in range(0, width, tile):
        span = slice(start, start + tile)
        made = mm(hid_ref[0], held[0, expert, span, :], NT).astype(BF).astype(F32)
        slot[:, span] = (made * gate_ref[0, :, 0:1]).astype(BF)
    for side, (p_ref, out_ref) in enumerate(((p0_ref, out0_ref), (p1_ref, out1_ref))):
        span = slice(side * capacity, (side + 1) * capacity)
        term = mm(p_ref[0], slot[span], TN)

        @pl.when(expert == 0)
        def _():
            acc[side] = term

        @pl.when(expert > 0)
        def _():
            acc[side] += term

        @pl.when(expert == pl.num_programs(0) - 1)
        def _():
            out_ref[...] = acc[side].astype(BF)


def down_call(order, hid, gates, picks, shards, capacity, width):
    tokens = picks[0].shape[2]
    _, experts, size, hidden = shards[0].shape
    rows = 2 * capacity
    by_expert = lambda e, _: (e, 0, 0)
    fixed = lambda e, _: (0, 0)
    grid = pltpu.PrefetchScalarGridSpec(
        num_scalar_prefetch=1,
        grid=(experts,),
        in_specs=[
            pl.BlockSpec((1, rows, hidden), by_expert),
            pl.BlockSpec((1, rows, LANES), by_expert),
        ]
        + [pl.BlockSpec((1, capacity, tokens), by_expert)] * 2
        + [ANY] * len(shards),
        out_specs=[pl.BlockSpec((tokens, width), fixed)] * 2,
        scratch_shapes=[
            pltpu.VMEM((1, experts, width, hidden), BF),
            pltpu.VMEM((rows, width), BF),
            pltpu.VMEM((2, tokens, width), F32),
            pltpu.SemaphoreType.DMA((1, experts, len(shards))),
        ],
    )
    return pl.pallas_call(
        lambda *refs: down_kernel(len(shards), capacity, *refs),
        name="experts_down",
        grid_spec=grid,
        out_shape=[sds((tokens, width), BF)] * 2,
        compiler_params=params(1),
        cost_estimate=cost(2 * experts * rows * width * (hidden + tokens), 14 * MIB),
    )(order, hid, gates, *picks, *shards)


def weight_grad_kernel(chunks, shards_of, order_ref, *rest):
    xs, gs = rest[:chunks], rest[chunks : 2 * chunks]
    ggs, gus = rest[2 * chunks : 3 * chunks], rest[3 * chunks : 4 * chunks]
    hids = rest[4 * chunks : 5 * chunks]
    outs = rest[5 * chunks : 5 * chunks + shards_of]
    held, sems = rest[5 * chunks + shards_of :]
    expert = pl.program_id(0)
    width = xs[0].shape[2]
    size = outs[0].shape[2]
    own = order_ref[0]

    def copies(kind, which):
        return [
            pltpu.make_async_copy(
                held.at[kind, pl.ds(pl.multiple_of((own ^ slot) * size, 16), size)],
                out.at[kind, which],
                sems.at[kind, slot],
            )
            for slot, out in enumerate(outs)
        ]

    for kind, (lefts, rights) in enumerate(((xs, ggs), (xs, gus), (gs, hids))):

        @pl.when(expert > 0)
        def _():
            for copy in copies(kind, expert - 1):
                copy.wait()

        tile = 256

        @pl.loop(0, width // tile)
        def _(step):
            span = pl.ds(pl.multiple_of(step * tile, tile), tile)
            total = mm(lefts[0][0, :, span], rights[0][0], TN)
            for left, right in zip(lefts[1:], rights[1:]):
                total += mm(left[0, :, span], right[0], TN)
            held[kind, span] = total.astype(BF)

        for copy in copies(kind, expert):
            copy.start()

    @pl.when(expert == pl.num_programs(0) - 1)
    def _():
        for kind in range(3):
            for copy in copies(kind, expert):
                copy.wait()


def weight_grad_call(order, xs, gs, ggs, gus, hids, shards_of):
    chunks = len(xs)
    experts, rows, width = xs[0].shape
    hidden = ggs[0].shape[2]
    size = width // shards_of
    by_expert = lambda e, _: (e, 0, 0)
    grid = pltpu.PrefetchScalarGridSpec(
        num_scalar_prefetch=1,
        grid=(experts,),
        in_specs=[pl.BlockSpec((1, rows, width), by_expert)] * (2 * chunks)
        + [pl.BlockSpec((1, rows, hidden), by_expert)] * (3 * chunks),
        out_specs=[ANY] * shards_of,
        scratch_shapes=[
            pltpu.VMEM((3, width, hidden), BF),
            pltpu.SemaphoreType.DMA((3, shards_of)),
        ],
    )
    return pl.pallas_call(
        lambda *refs: weight_grad_kernel(chunks, shards_of, *refs),
        name="expert_weight_grads",
        grid_spec=grid,
        out_shape=[sds((3, experts, size, hidden), BF)] * shards_of,
        compiler_params=params(1),
        cost_estimate=cost(6 * experts * chunks * rows * width * hidden, 40 * MIB),
    )(order, *xs, *gs, *ggs, *gus, *hids)


def resid_back_kernel(
    terms, x_ref, rows_ref, dy_ref, gain_ref, w_ref, att_ref, *rest
):
    parts = rest[:terms]
    resid_ref, attn_ref, do_ref, delta_ref, gain_out, deltas = rest[terms:]
    step = pl.program_id(0)
    grad = parts[0][...].astype(F32)
    for part in parts[1:]:
        grad += part[...].astype(F32)
    resid = x_ref[...].astype(F32) + rows_ref[...].astype(F32)
    scale = lax.rsqrt(jnp.mean(resid * resid, -1, keepdims=True) + EPS)
    normed = resid * scale
    product = grad * normed
    partial = jnp.sum(product, 0, keepdims=True)

    @pl.when(step == 0)
    def _():
        gain_out[...] = jnp.broadcast_to(partial, gain_out.shape)

    @pl.when(step > 0)
    def _():
        gain_out[...] += partial

    gain = gain_ref[1:2]
    mean = jnp.mean(product * gain, -1, keepdims=True)
    total = dy_ref[...].astype(F32) + scale * (grad * gain - normed * mean)
    resid_ref[...] = total
    low = total.astype(BF)
    attn_ref[...] = low
    back = mm(low, w_ref[...]).astype(BF)
    do_ref[...] = back
    each = back.astype(F32) * att_ref[...].astype(F32)
    lanes = lax.broadcasted_iota(jnp.int32, deltas.shape, 1)
    made = jnp.zeros(deltas.shape, F32)
    for head in range(HEADS):
        value = jnp.sum(each[:, head * HEAD : (head + 1) * HEAD], -1, keepdims=True)
        made = jnp.where(lanes == head, value, made)
    deltas[...] = made
    delta_ref[...] = jnp.transpose(deltas[...])[0:16]


def resid_back_call(x, rows, dy, gains, wo_t, attended, parts):
    tokens, width = x.shape
    tile = 128
    by_row = lambda i: (i, 0)
    return pl.pallas_call(
        lambda *refs: resid_back_kernel(len(parts), *refs),
        name="resid_back",
        grid=(tokens // tile,),
        in_specs=[pl.BlockSpec((tile, width), by_row)] * 3
        + [whole((8, width)), whole((width, HQ)), pl.BlockSpec((tile, HQ), by_row)]
        + [pl.BlockSpec((tile, width), by_row)] * len(parts),
        out_specs=[pl.BlockSpec((tile, width), by_row)] * 2
        + [
            pl.BlockSpec((tile, HQ), by_row),
            pl.BlockSpec((16, tile), lambda i: (0, i)),
            whole((8, width)),
        ],
        out_shape=[
            sds((tokens, width), F32),
            sds((tokens, width), BF),
            sds((tokens, HQ), BF),
            sds((16, tokens), F32),
            sds((8, width), F32),
        ],
        scratch_shapes=[pltpu.VMEM((tile, LANES), F32)],
        compiler_params=params(1),
        cost_estimate=cost(2 * tokens * width * HQ, 16 * MIB),
    )(x, rows, dy, gains, wo_t, attended, *parts)


def cross_kernel(left_ref, right_ref, out_ref):
    out_ref[...] = mm(left_ref[...], right_ref[...], TN).astype(out_ref.dtype)


def cross_call(left, right, name):
    tokens, rows = left.shape
    columns = right.shape[1]
    tile = 512 if rows % 512 == 0 else rows
    return pl.pallas_call(
        cross_kernel,
        name=name,
        grid=(rows // tile,),
        in_specs=[pl.BlockSpec((tokens, tile), lambda i: (0, i)), whole((tokens, columns))],
        out_specs=pl.BlockSpec((tile, columns), lambda i: (i, 0)),
        out_shape=sds((rows, columns), BF),
        compiler_params=params(1),
        cost_estimate=cost(2 * tokens * rows * columns, 8 * MIB),
    )(left, right)


def input_q_kernel(dq_ref, w_ref, out_ref):
    out_ref[...] = mm(dq_ref[...], w_ref[...], NT)


def input_q_call(d_q, w_full):
    tokens = d_q.shape[0]
    width = w_full.shape[0]
    tile = 512
    return pl.pallas_call(
        input_q_kernel,
        name="input_grad_q",
        grid=(width // tile,),
        in_specs=[whole((tokens, HQ)), pl.BlockSpec((tile, HQ), lambda i: (i, 0))],
        out_specs=pl.BlockSpec((tokens, tile), lambda i: (0, i)),
        out_shape=sds((tokens, width), F32),
        compiler_params=params(1),
        cost_estimate=cost(2 * tokens * width * HQ, 9 * MIB),
    )(d_q, w_full)


def final_kernel(
    terms, x_ref, low_ref, resid_ref, gq_ref, gain_ref, moe_ref, w_ref, cos_ref, sin_ref, *rest
):
    parts = rest[:terms]
    grad_ref, out_ref = rest[terms:]
    scale_k = HEAD ** (-0.5)
    total = parts[0][...].astype(F32)
    for part in parts[1:]:
        total += part[...].astype(F32)
    cosine, sine = cos_ref[...], -sin_ref[...]
    pieces = [
        turn(total[:, head * HEAD : (head + 1) * HEAD] * scale_k, cosine, sine).astype(BF)
        for head in range(KV_HEADS)
    ]
    low = jnp.concatenate(pieces + [total[:, KVW:].astype(BF)], 1)
    out_ref[:, 0 : 2 * KVW] = mm(low_ref[...], low, TN).astype(BF)
    wide = x_ref[...].astype(F32)
    scale = lax.rsqrt(jnp.mean(wide * wide, -1, keepdims=True) + EPS)
    normed = wide * scale
    grad = gq_ref[...] + mm(low, w_ref[...], NT)
    product = grad * normed
    gain_part = jnp.sum(product, 0, keepdims=True)
    gain = gain_ref[0:1]
    mean = jnp.mean(product * gain, -1, keepdims=True)
    own = (scale * (grad * gain - normed * mean)).astype(BF)
    grad_ref[...] = (resid_ref[...] + own.astype(F32)).astype(BF)
    width = x_ref.shape[1]
    lines = lax.broadcasted_iota(jnp.int32, (LANES, width), 0)
    both = jnp.where(lines == 0, gain_part, jnp.where(lines == 1, moe_ref[0:1], 0.0))
    out_ref[:, 2 * KVW :] = jnp.transpose(both).astype(BF)


def final_call(x, low, resid, grad_q, gains, moe_part, w_full, cosine, sine, parts):
    tokens, width = x.shape
    columns = 2 * KVW + LANES
    return pl.pallas_call(
        lambda *refs: final_kernel(len(parts), *refs),
        name="final",
        grid=(1,),
        in_specs=[whole((tokens, width))] * 4
        + [whole((8, width))] * 2
        + [pl.BlockSpec((width, 2 * KVW), lambda i: (0, HQ // (2 * KVW)))]
        + [whole((tokens, HEAD))] * 2
        + [whole((tokens, 2 * KVW))] * len(parts),
        out_specs=[whole((tokens, width)), whole((width, columns))],
        out_shape=[sds((tokens, width), BF), sds((width, columns), BF)],
        compiler_params=params(1),
        cost_estimate=cost(4 * tokens * width * 2 * KVW, 14 * MIB),
    )(x, low, resid, grad_q, gains, moe_part, w_full, cosine, sine, *parts)


def hold_kernel(count, *refs):
    del count, refs


def hold(arrays, until):
    count = len(arrays)
    return pl.pallas_call(
        lambda *refs: hold_kernel(count, *refs),
        name="hold",
        in_specs=[ANY] * (count + 1),
        out_specs=[ANY] * count,
        out_shape=[sds(array.shape, array.dtype) for array in arrays],
        input_output_aliases={place: place for place in range(count)},
    )(*arrays, until)


def local(
    layer_input,
    lengths,
    expert_ids,
    gate_weights,
    attn_gain,
    wq,
    wk,
    wv,
    wo,
    moe_gain,
    w_gate,
    w_up,
    w_down,
    cotangent,
):
    count = lax.axis_size("ctx")
    shards_of = lax.axis_size("fsdp")
    both = ("ctx", "fsdp")
    ring = Ring(count)
    me = lax.axis_index("ctx").astype(jnp.int32)
    own = lax.axis_index("fsdp").astype(jnp.int32)
    x = layer_input[0]
    dy = cotangent[0]
    tokens, width = x.shape
    exp_dev = w_gate.shape[0]
    experts = exp_dev * count
    capacity = 3 * tokens * TOPK // (2 * experts)

    rows = wq.shape[0]
    gains_part = jnp.concatenate(
        [attn_gain[:, None], moe_gain[:, None], jnp.zeros((rows, LANES - 2), BF)], 1
    )
    w_full = lax.all_gather(
        jnp.concatenate([wq, wk, wv, gains_part], 1), both, axis=0, tiled=True
    )
    wo_t = lax.all_gather(wo.T, both, axis=0, tiled=True)

    shards = gather_shards(
        jnp.stack([w_gate, w_up, jnp.swapaxes(w_down, 1, 2)]), shards_of
    )
    gates = gate_weights[0]
    gate_high = gates.astype(BF)
    rest = gates - gate_high.astype(F32)
    gate_mid = rest.astype(BF)
    gate_low = (rest - gate_mid.astype(F32)).astype(BF)
    info = jnp.concatenate(
        [
            dy,
            expert_ids[0].astype(BF),
            gate_high,
            gate_mid,
            gate_low,
            jnp.zeros((tokens, LANES - 4 * TOPK), BF),
        ],
        1,
    )
    grads = ring.gather(info)

    ends = jnp.cumsum(lengths[0])
    index = me * tokens + jnp.arange(tokens, dtype=jnp.int32)
    after = (index[:, None] >= ends[None, :]).astype(jnp.int32)
    start = jnp.sum(after * lengths[0][None, :], 1)
    half = HEAD // 2
    freq = jnp.exp(jnp.arange(half, dtype=F32) * (-2.0 * math.log(ROPE_BASE) / HEAD))
    angle = (index - start).astype(F32)[:, None] * freq[None, :]
    cosine = jnp.cos(angle)
    sine = jnp.sin(angle)
    cosine = jnp.concatenate([cosine, cosine], 1)
    sine = jnp.concatenate([-sine, sine], 1)
    start_column = jnp.broadcast_to(start[:, None], (tokens, LANES))
    start_row = jnp.broadcast_to(start[None, :], (8, tokens))
    order = jnp.concatenate([me[None], (start[0] // tokens)[None], ring.sources()])
    places = jnp.stack([own, me])

    q, kv, low_one, gains = qkv_call(x, w_full, cosine, sine)
    kv_slots = [part for couple in ring.gather(kv) for part in couple]
    attended, log_total = attn_call(order, q, start_column, kv_slots)
    attn_rows, low_two = out_call(x, attended, wo_t, gains)

    routed = [route_call(places, couple, shards, capacity, width) for couple in grads]
    parts, made = [], []
    for couple, (pick0, pick1, _, _, grad_hidden) in zip(ring.gather(low_two), routed):
        found = expert_call(places, couple, (pick0, pick1), grad_hidden, shards, capacity)
        made.append(found[:4])
        parts.append((found[4], found[5]))
    grad_parts = ring.scatter(parts)

    resid, grad_attn, grad_out, delta, moe_part = resid_back_call(
        x, attn_rows, dy, gains, wo_t, attended, grad_parts
    )
    back = attn_back_call(
        order, q, grad_out, start_row, log_total, delta, cosine, sine, kv_slots
    )
    d_q, kv_parts = back[0], back[1:]
    kv_terms = ring.scatter(
        [(kv_parts[2 * step], kv_parts[2 * step + 1]) for step in range(count // 2)]
    )

    y_parts = []
    for (pick0, pick1, gate_rows, _, _), (_, hid, _, _) in zip(routed, made):
        y_parts.append(
            down_call(places, hid, gate_rows, (pick0, pick1), shards, capacity, width)
        )
    flat = hold([part for couple in y_parts for part in couple], resid)
    y_terms = ring.scatter(
        [(flat[2 * step], flat[2 * step + 1]) for step in range(count // 2)]
    )
    moe = y_terms[0].astype(F32)
    for term in y_terms[1:]:
        moe = moe + term.astype(F32)
    output = (x.astype(F32) + attn_rows.astype(F32) + moe).astype(BF)

    grad_shards = weight_grad_call(
        places,
        [entry[0] for entry in made],
        [entry[3] for entry in routed],
        [entry[2] for entry in made],
        [entry[3] for entry in made],
        [entry[1] for entry in made],
        shards_of,
    )
    near, arrived = scatter_shards(grad_shards, shards_of)
    expert_grads = near.astype(F32) + arrived.astype(F32)

    wo_grad = lax.psum_scatter(
        cross_call(grad_attn, attended, "wo_grad"), both, scatter_dimension=0, tiled=True
    ).astype(F32)
    wq_grad = lax.psum_scatter(
        cross_call(low_one, d_q, "wq_grad"), both, scatter_dimension=0, tiled=True
    ).astype(F32)
    grad_q = input_q_call(d_q, w_full)
    input_grad, tail = final_call(
        x, low_one, resid, grad_q, gains, moe_part, w_full, cosine, sine, kv_terms
    )
    tail = lax.psum_scatter(tail, both, scatter_dimension=0, tiled=True).astype(F32)
    return (
        output[None],
        input_grad[None],
        tail[:, 2 * KVW],
        wq_grad,
        tail[:, 0:KVW],
        tail[:, KVW : 2 * KVW],
        wo_grad.T,
        tail[:, 2 * KVW + 1],
        expert_grads[0],
        expert_grads[1],
        jnp.swapaxes(expert_grads[2], 1, 2),
    )


def solution(mesh):
    return jax.shard_map(
        local,
        mesh=mesh,
        in_specs=(
            P("fsdp", "ctx", None),
            P("fsdp", None),
            P("fsdp", "ctx", None),
            P("fsdp", "ctx", None),
            P(("ctx", "fsdp")),
            P(("ctx", "fsdp"), None),
            P(("ctx", "fsdp"), None),
            P(("ctx", "fsdp"), None),
            P(None, ("ctx", "fsdp")),
            P(("ctx", "fsdp")),
            P("ctx", "fsdp", None),
            P("ctx", "fsdp", None),
            P("ctx", None, "fsdp"),
            P("fsdp", "ctx", None),
        ),
        out_specs=(
            P("fsdp", "ctx", None),
            P("fsdp", "ctx", None),
            P(("ctx", "fsdp")),
            P(("ctx", "fsdp"), None),
            P(("ctx", "fsdp"), None),
            P(("ctx", "fsdp"), None),
            P(None, ("ctx", "fsdp")),
            P(("ctx", "fsdp")),
            P("ctx", "fsdp", None),
            P("ctx", "fsdp", None),
            P("ctx", None, "fsdp"),
        ),
        check_vma=False,
    )
```

time: 2060 us -> 1130 us (0.55)
  waiting for transfers between devices: 1200 us -> 538 us
  Pallas kernels: 0 us -> 283 us
  local copies, waits for them, and re-layouts: 297 us -> 26.3 us
  blocking collectives: 165 us -> 0 us
  matrix products: 164 us -> 0 us
  starting transfers between devices: 78.4 us -> 215 us
  other arithmetic: 117 us -> 39.2 us
    reduce_scatter x7 -> x3, waiting for transfers between devices: 626 us -> 104 us  [the longest x1 104 us: local(): lax.psum_scatter(cross_call(grad_attn, attended, 'wo_grad'), both, scatte...]
    all_to_all x4 -> x0, waiting for transfers between devices: 366 us -> none  [the longest x2 219 us: from_experts(): lax.all_to_all(buffer, 'ctx', split_axis=2, concat_axis=0, tiled=True)]
    ppermute x0 -> x60, waiting for transfers between devices: none -> 363 us  [the longest x30 206 us: move(): return lax.ppermute(array, 'ctx', pairs)]
    pallas_call x0 -> x23, Pallas kernels: none -> 283 us  [the longest x4 67.3 us: expert_call(): pl.pallas_call(lambda *refs: expert_kernel(len(shards), capacity, *refs),...]
    ppermute x0 -> x60, starting transfers between devices: none -> 215 us  [the longest x30 151 us: move(): return lax.ppermute(array, 'ctx', pairs)]
    dot_general x28 -> x0, matrix products: 164 us -> none  [the longest x4 18.7 us: cross_rows(): lax.dot_general(left, right, (((0,), (0,)), ((), ())), preferred_element_...]
    all_gather x7 -> x2, waiting for transfers between devices: 182 us -> 70 us  [the longest x1 70 us: local(): lax.all_gather(jnp.concatenate([wq, wk, wv, gains_part], 1), both, axis=0...]
    all_gather x2 -> x0, blocking collectives: 83.2 us -> none  [the longest x1 42.9 us: local(): lax.all_gather(wk, ('ctx', 'fsdp'), axis=0, tiled=True)]
  transfers between devices with their start and end apart: 19 -> 65, of which waited for: 13 -> 30; matrix products, arithmetic and copies ran while one was open for 18% -> 5% of each run, Pallas kernels for 0% -> 22%
where the time goes in v1:
time: 1130 us; the launch traced here: 1120 us
  waiting for transfers between devices  538 us (48%)
  Pallas kernels  283 us (25%)
  starting transfers between devices  215 us (19%)
  other arithmetic  39.2 us (3%)
  local copies, waits for them, and re-layouts  26.3 us (2%)
  between operations  16.7 us (1%)
    ppermute x30, waiting for transfers between devices, move(): return lax.ppermute(array, 'ctx', pairs)  206 us
    ppermute x24, waiting for transfers between devices, swap(): return lax.ppermute(array, 'ctx', pairs)  158 us
    ppermute x30, starting transfers between devices, move(): return lax.ppermute(array, 'ctx', pairs)  151 us
    reduce_scatter x1, waiting for transfers between devices, local(): lax.psum_scatter(cross_call(grad_attn, attended, 'wo_grad'), both, scatte...  104 us
    all_gather x1, waiting for transfers between devices, local(): lax.all_gather(jnp.concatenate([wq, wk, wv, gains_part], 1), both, axis=0...  70 us
    pallas_call x4, Pallas kernels, expert_call(): pl.pallas_call(lambda *refs: expert_kernel(len(shards), capacity, *refs),...  67.3 us
    ppermute x24, starting transfers between devices, swap(): return lax.ppermute(array, 'ctx', pairs)  61.2 us
    pallas_call x4, Pallas kernels, route_call(): pl.pallas_call(lambda *refs: route_kernel(len(shards), capacity, *refs),...  48.9 us
  transfers between devices with their start and end apart: 65, of which 30 were waited for; matrix products, arithmetic and copies ran while one was open for 5% of the time, Pallas kernels for 22%

profile of v1, /device:TPU:0, one launch (start us, length us, event | category | flops | bytes accessed | tf_op | source)
XLA Modules:
  0.0 1118.9 jit_solution(4888100801609214437)
XLA Ops:
  21.5 70.0 %all-gather.3.cloned.1.call-done.w_ref.g_ref.refs_6_ = bf16[1536,2176]{1,0:T(8,128)(2,1)} async-done(((bf16[48,2176]{1,0:T(8,128)(2,1)}), bf16[1536,2176]{1,0:T(8,128)(2,1)}) %all-gather.3.cloned.1.call-update) | async-done | bytes 6684688 | tf_op jit(solution)/shard_map/all_gather | solution.py:990
  171.2 14.3 %attention.1 = (bf16[384,1536]{1,0:T(8,128)(2,1)}, f32[16,384]{1,0:T(8,128)}) custom-call(s32[10]{0:T(128)} %pad_add_fusion.1.refs_0_, bf16[384,1536]{1,0:T(8,128)(2,1)} %get-tuple-element.99.refs_1_, s32[384,128]{1,0:T(8,128)} %broadcast_in_dim.46.refs_2_, bf16[384,512]{1,0:T(8,128)(2,1)} %get-tuple-element.100.refs_3_.refs_8_, ...), custom_call_target="tpu_custom_call" | custom-call | flops 7247757312 | bytes 6291456 | tf_op jit(solution)/shard_map/attention/pallas_call | solution.py:321
  194.2 26.1 %collective-permute-start.14 = (bf16[384,1536]{1,0:T(8,128)(2,1)}, bf16[384,1536]{1,0:T(8,128)(2,1)S(1)}, u32[]{:S(2)}, u32[]{:S(2)}) collective-permute-start(bf16[384,1536]{1,0:T(8,128)(2,1)} %get-tuple-element.104.refs_1_), channel_id=1, source_target_pairs={{0,8},{4,12},{8,0},{12,4},{16,24},{20,28},{24,16},{28,20},{1,9},{5... | collective-permute-start | bytes 3538952 | tf_op jit(solution)/shard_map/ppermute | solution.py:80
  221.1 23.3 %collective-permute-done.14.refs_1_ = bf16[384,1536]{1,0:T(8,128)(2,1)S(1)} collective-permute-done((bf16[384,1536]{1,0:T(8,128)(2,1)}, bf16[384,1536]{1,0:T(8,128)(2,1)S(1)}, u32[]{:S(2)}, u32[]{:S(2)}) %collective-permute-start.14) | collective-permute-done | bytes 1179680 | tf_op jit(solution)/shard_map/ppermute | solution.py:80
  250.1 43.7 %collective-permute-done.28 = bf16[384,1664]{1,0:T(8,128)(2,1)S(1)} collective-permute-done((bf16[384,1664]{1,0:T(8,128)(2,1)}, bf16[384,1664]{1,0:T(8,128)(2,1)S(1)}, u32[]{:S(2)}, u32[]{:S(2)}) %collective-permute-start.28) | collective-permute-done | bytes 1277984 | tf_op jit(solution)/shard_map/ppermute | solution.py:80
  299.1 25.1 %collective-permute-done.25 = bf16[384,1536]{1,0:T(8,128)(2,1)S(1)} collective-permute-done((bf16[384,1536]{1,0:T(8,128)(2,1)S(1)}, bf16[384,1536]{1,0:T(8,128)(2,1)S(1)}, u32[]{:S(2)}, u32[]{:S(2)}) %collective-permute-start.25) | collective-permute-done | bytes 1179680 | tf_op jit(solution)/shard_map/ppermute | solution.py:80
  333.4 18.2 %collective-permute-done.22 = bf16[384,1664]{1,0:T(8,128)(2,1)S(1)} collective-permute-done((bf16[384,1664]{1,0:T(8,128)(2,1)S(1)}, bf16[384,1664]{1,0:T(8,128)(2,1)S(1)}, u32[]{:S(2)}, u32[]{:S(2)}) %collective-permute-start.22) | collective-permute-done | bytes 1277984 | tf_op jit(solution)/shard_map/ppermute | solution.py:80
  391.2 16.8 %experts.7 = (bf16[2,288,1536]{2,1,0:T(8,128)(2,1)}, bf16[2,288,768]{2,1,0:T(8,128)(2,1)}, bf16[2,288,768]{2,1,0:T(8,128)(2,1)}, bf16[2,288,768]{2,1,0:T(8,128)(...) custom-call(s32[2]{0:T(128)} %pad_add_fusion.2.refs_0_, bf16[384,1536]{1,0:T(8,128)(2,1)} %add.154.refs_1_, ...), custom_call_target="tpu_custom_call" | custom-call | flops 6794772480 | bytes 25165824 | tf_op jit(solution)/shard_map/experts/pallas_call | solution.py:631
  434.1 16.9 %experts.6 = (bf16[2,288,1536]{2,1,0:T(8,128)(2,1)}, bf16[2,288,768]{2,1,0:T(8,128)(2,1)}, bf16[2,288,768]{2,1,0:T(8,128)(2,1)}, bf16[2,288,768]{2,1,0:T(8,128)(...) custom-call(s32[2]{0:T(128)} %pad_add_fusion.2.refs_0_, bf16[384,1536]{1,0:T(8,128)(2,1)} %add.152.refs_1_, ...), custom_call_target="tpu_custom_call" | custom-call | flops 6794772480 | bytes 25165824 | tf_op jit(solution)/shard_map/experts/pallas_call | solution.py:631
  469.4 16.3 %collective-permute-done.17.refs_2_ = bf16[384,1664]{1,0:T(8,128)(2,1)S(1)} collective-permute-done((bf16[384,1664]{1,0:T(8,128)(2,1)}, bf16[384,1664]{1,0:T(8,128)(2,1)S(1)}, u32[]{:S(2)}, u32[]{:S(2)}) %collective-permute-start.17) | collective-permute-done | bytes 1277984 | tf_op jit(solution)/shard_map/ppermute | solution.py:88
  486.8 23.3 %route.5 = (bf16[2,144,384]{2,1,0:T(8,128)(2,1)}, bf16[2,144,384]{2,1,0:T(8,128)(2,1)}, f32[2,288,128]{2,1,0:T(8,128)}, bf16[2,288,1536]{2,1,0:T(8,128)(2,1)}, f32[2,288,768]{2,1,0:T(8,128)}) custom-call(s32[2]{0:T(128)} %pad_add_fusion.2.refs_0_, bf16[384,1664]{1,0:T(8,128)(2,1)} %collective-permute-done.16.refs_1_, bf16[384,1664]{1,0:T(8,128)(2,1)} %copy-done.12, ...), custom_call_target="tpu_custom_call" | custom-call | flops 2038431744 | bytes 14680064 | tf_op jit(solution)/shard_map/route/pallas_call | solution.py:547
  512.1 16.9 %experts.5 = (bf16[2,288,1536]{2,1,0:T(8,128)(2,1)}, bf16[2,288,768]{2,1,0:T(8,128)(2,1)}, bf16[2,288,768]{2,1,0:T(8,128)(2,1)}, bf16[2,288,768]{2,1,0:T(8,128)(...) custom-call(s32[2]{0:T(128)} %pad_add_fusion.2.refs_0_, bf16[384,1536]{1,0:T(8,128)(2,1)} %copy-done.32, ...), custom_call_target="tpu_custom_call" | custom-call | flops 6794772480 | bytes 25165824 | tf_op jit(solution)/shard_map/experts/pallas_call | solution.py:631
  548.4 15.2 %collective-permute-done.10.refs_2_ = bf16[384,1664]{1,0:T(8,128)(2,1)S(1)} collective-permute-done((bf16[384,1664]{1,0:T(8,128)(2,1)}, bf16[384,1664]{1,0:T(8,128)(2,1)S(1)}, u32[]{:S(2)}, u32[]{:S(2)}) %collective-permute-start.10) | collective-permute-done | bytes 1277984 | tf_op jit(solution)/shard_map/ppermute | solution.py:88
  573.1 15.9 %collective-permute-done.9.refs_2_ = bf16[384,1536]{1,0:T(8,128)(2,1)} collective-permute-done((bf16[384,1536]{1,0:T(8,128)(2,1)}, bf16[384,1536]{1,0:T(8,128)(2,1)}, u32[]{:S(2)}, u32[]{:S(2)}) %collective-permute-start.9) | collective-permute-done | bytes 1179680 | tf_op jit(solution)/shard_map/ppermute | solution.py:88
  589.0 16.8 %experts.4 = (bf16[2,288,1536]{2,1,0:T(8,128)(2,1)}, bf16[2,288,768]{2,1,0:T(8,128)(2,1)}, bf16[2,288,768]{2,1,0:T(8,128)(2,1)}, bf16[2,288,768]{2,1,0:T(8,128)(...) custom-call(s32[2]{0:T(128)} %pad_add_fusion.2.refs_0_, bf16[384,1536]{1,0:T(8,128)(2,1)} %get-tuple-element.104.refs_1_, ...), custom_call_target="tpu_custom_call" | custom-call | flops 6794772480 | bytes 25165824 | tf_op jit(solution)/shard_map/experts/pallas_call | solution.py:631
  650.8 17.6 %attention_back.1 = (bf16[384,1536]{1,0:T(8,128)(2,1)}, bf16[384,512]{1,0:T(8,128)(2,1)}, bf16[384,512]{1,0:T(8,128)(2,1)}, bf16[384,512]{1,0:T(8,128)(2,1)}, bf...) custom-call(s32[10]{0:T(128)} %pad_add_fusion.1.refs_0_, ...), custom_call_target="tpu_custom_call" | custom-call | flops 18119393280 | bytes 10485760 | tf_op jit(solution)/shard_map/attention_back/pallas_call | solution.py:419
  685.3 24.7 %collective-permute-start.54 = (bf16[384,512]{1,0:T(8,128)(2,1)S(1)}, bf16[384,512]{1,0:T(8,128)(2,1)S(1)}, u32[]{:S(2)}, u32[]{:S(2)}) collective-permute-start(bf16[384,512]{1,0:T(8,128)(2,1)S(1)} %add.175), channel_id=1, source_target_pairs={{0,8},{4,12},{24,16},{28,20},{1,9},{5,13},{25,17},{29,21},{2,10},{... | collective-permute-start | bytes 1179656 | tf_op jit(solution)/shard_map/ppermute | solution.py:80
  722.7 36.5 %collective-permute-start.56 = (bf16[384,512]{1,0:T(8,128)(2,1)S(1)}, bf16[384,512]{1,0:T(8,128)(2,1)S(1)}, u32[]{:S(2)}, u32[]{:S(2)}) collective-permute-start(bf16[384,512]{1,0:T(8,128)(2,1)S(1)} %add_add_fusion.2), channel_id=1, source_target_pairs={{0,8},{4,12},{8,0},{12,4},{16,24},{20,28},{24,16},{28,20},{1,9},{5... | collective-permute-start | bytes 1179656 | tf_op jit(solution)/shard_map/ppermute | solution.py:80
  780.6 44.1 %expert_weight_grads.1 = (bf16[3,2,384,768]{3,2,1,0:T(8,128)(2,1)}, bf16[3,2,384,768]{3,2,1,0:T(8,128)(2,1)}, bf16[3,2,384,768]{3,2,1,0:T(8,128)(2,1)}, bf16[3,2,384,768]{3,2,1,0:T(8,128)(2,1)}) custom-call(s32[2]{0:T(128)} %pad_add_fusion.2.refs_0_, bf16[2,288,1536]{2,1,0:T(8,128)(2,1)} %get-tuple-element.167.refs_1_, ...), custom_call_target="tpu_custom_call" | custom-call | flops 16307453952 | bytes 41943040 | tf_op jit(solution)/shard_map/expert_weight_grads/pallas_call | solution.py:769
  875.7 15.6 %collective-permute-done.44 = bf16[384,1536]{1,0:T(8,128)(2,1)} collective-permute-done((bf16[384,1536]{1,0:T(8,128)(2,1)}, bf16[384,1536]{1,0:T(8,128)(2,1)}, u32[]{:S(2)}, u32[]{:S(2)}) %collective-permute-start.44) | collective-permute-done | bytes 1179680 | tf_op jit(solution)/shard_map/ppermute | solution.py:88
  896.5 19.7 %collective-permute-done.40 = bf16[384,1536]{1,0:T(8,128)(2,1)S(1)} collective-permute-done((bf16[384,1536]{1,0:T(8,128)(2,1)S(1)}, bf16[384,1536]{1,0:T(8,128)(2,1)S(1)}, u32[]{:S(2)}, u32[]{:S(2)}) %collective-permute-start.40) | collective-permute-done | bytes 1179680 | tf_op jit(solution)/shard_map/ppermute | solution.py:88
  923.9 35.6 %collective-permute-done.41 = bf16[384,1536]{1,0:T(8,128)(2,1)S(1)} collective-permute-done((bf16[384,1536]{1,0:T(8,128)(2,1)S(1)}, bf16[384,1536]{1,0:T(8,128)(2,1)S(1)}, u32[]{:S(2)}, u32[]{:S(2)}) %collective-permute-start.41) | collective-permute-done | bytes 1179680 | tf_op jit(solution)/shard_map/ppermute | solution.py:80
  977.0 12.7 %collective-permute-done.39 = bf16[384,1536]{1,0:T(8,128)(2,1)} collective-permute-done((bf16[384,1536]{1,0:T(8,128)(2,1)}, bf16[384,1536]{1,0:T(8,128)(2,1)}, u32[]{:S(2)}, u32[]{:S(2)}) %collective-permute-start.39) | collective-permute-done | bytes 1179680 | tf_op jit(solution)/shard_map/ppermute | solution.py:88
  1006.7 103.9 %reduce-scatter.8.cloned.1.call-done = bf16[48,1536]{1,0:T(8,128)(2,1)} async-done(((bf16[1536,1536]{1,0:T(8,128)(2,1)}), bf16[48,1536]{1,0:T(8,128)(2,1)}) %reduce-scatter.8.cloned.1.call-update) | async-done | bytes 147472 | tf_op jit(solution)/shard_map/reduce_scatter | solution.py:1082
  (272 shorter events, 433.0 us)
Async XLA Ops:
  7.2 84.2 %all-gather.3.cloned.1.call-start = ((), (), s32[]{:S(2)}) async-start(), calls=%async_computation.3 | async-start | bytes 6893568 | tf_op jit(solution)/shard_map/all_gather | solution.py:990
  10.6 174.9 %all-gather.5.cloned.1.call-start = ((), (), s32[]{:S(2)}) async-start(), calls=%async_computation.4 | async-start | bytes 4866048 | tf_op jit(solution)/shard_map/all_gather | solution.py:993
  11.3 962.7 %reduce-scatter.4.cloned.1.call-start = ((), (), s32[]{:S(2)}) async-start(), calls=%async_computation.5 | async-start | bytes 2027520 | tf_op jit(solution)/shard_map/reduce_scatter | solution.py:1092
  15.0 136.2 %collective-permute-start.16 = (bf16[384,1664]{1,0:T(8,128)(2,1)}, bf16[384,1664]{1,0:T(8,128)(2,1)}, u32[]{:S(2)}, u32[]{:S(2)}) collective-permute-start(bf16[384,1664]{1,0:T(8,128)(2,1)} %concatenate.19.refs_1_), channel_id=1, source_target_pairs={{0,8},{4,12},{8,0},{12,4},{16,24},{20,28},{24,16},{28,20},{1,9},{5... | collective-permute-start | bytes 3833864 | tf_op jit(solution)/shard_map/ppermute | solution.py:80
  102.0 144.6 %collective-permute-start.12 = (bf16[3,2,384,768]{3,2,1,0:T(8,128)(2,1)S(1)}, bf16[3,2,384,768]{3,2,1,0:T(8,128)(2,1)}, u32[]{:S(2)}, u32[]{:S(2)}) collective-permute-start(bf16[3,2,384,768]{3,2,1,0:T(8,128)(2,1)S(1)} %pad_maximum_fusion.refs_3_.refs_6_.refs_5_), channel_id=1, source_target_pairs={{0,2},{1,3},{2,0},{3,1},{4,6},{5,7},{6,4},{7,5},{8,10},{9,11},{10,... | collective-permute-start | bytes 10616840 | tf_op jit(solution)/shard_map/ppermute | solution.py:145
  154.7 90.4 %collective-permute-start.27 = (bf16[384,1664]{1,0:T(8,128)(2,1)}, bf16[384,1664]{1,0:T(8,128)(2,1)}, u32[]{:S(2)}, u32[]{:S(2)}) collective-permute-start(bf16[384,1664]{1,0:T(8,128)(2,1)} %collective-permute-done.16.refs_1_), channel_id=1, source_target_pairs={{8,16},{12,20},{16,8},{20,12},{9,17},{13,21},{17,9},{21,13},{10,18... | collective-permute-start | bytes 3833864 | tf_op jit(solution)/shard_map/ppermute | solution.py:80
  246.5 135.9 %collective-permute-start.11 = (bf16[3,2,384,768]{3,2,1,0:T(8,128)(2,1)S(1)}, bf16[3,2,384,768]{3,2,1,0:T(8,128)(2,1)}, u32[]{:S(2)}, u32[]{:S(2)}) collective-permute-start(bf16[3,2,384,768]{3,2,1,0:T(8,128)(2,1)S(1)} %pad_maximum_fusion.refs_3_.refs_6_.refs_5_), channel_id=1, source_target_pairs={{0,1},{1,0},{2,3},{3,2},{4,5},{5,4},{6,7},{7,6},{8,9},{9,8},{10,11... | collective-permute-start | bytes 10616840 | tf_op jit(solution)/shard_map/ppermute | solution.py:145
  246.6 135.8 %collective-permute-start.13 = (bf16[3,2,384,768]{3,2,1,0:T(8,128)(2,1)}, bf16[3,2,384,768]{3,2,1,0:T(8,128)(2,1)}, u32[]{:S(2)}, u32[]{:S(2)}) collective-permute-start(bf16[3,2,384,768]{3,2,1,0:T(8,128)(2,1)} %collective-permute-done.12.refs_5_.refs_8_.refs_7_), channel_id=1, source_target_pairs={{0,1},{1,0},{2,3},{3,2},{4,5},{5,4},{6,7},{7,6},{8,9},{9,8},{10,11... | collective-permute-start | bytes 10616840 | tf_op jit(solution)/shard_map/ppermute | solution.py:145
  248.8 75.4 %collective-permute-start.25 = (bf16[384,1536]{1,0:T(8,128)(2,1)S(1)}, bf16[384,1536]{1,0:T(8,128)(2,1)S(1)}, u32[]{:S(2)}, u32[]{:S(2)}) collective-permute-start(bf16[384,1536]{1,0:T(8,128)(2,1)S(1)} %collective-permute-done.24), channel_id=1, source_target_pairs={{8,0},{12,4},{16,24},{20,28},{9,1},{13,5},{17,25},{21,29},{10,2},{... | collective-permute-start | bytes 3538952 | tf_op jit(solution)/shard_map/ppermute | solution.py:80
  295.1 76.3 %collective-permute-start.19 = (bf16[384,1536]{1,0:T(8,128)(2,1)}, bf16[384,1536]{1,0:T(8,128)(2,1)}, u32[]{:S(2)}, u32[]{:S(2)}) collective-permute-start(bf16[384,1536]{1,0:T(8,128)(2,1)} %collective-permute-done.18), channel_id=1, source_target_pairs={{8,0},{12,4},{16,24},{20,28},{9,1},{13,5},{17,25},{21,29},{10,2},{... | collective-permute-start | bytes 3538952 | tf_op jit(solution)/shard_map/ppermute | solution.py:80
  324.2 58.2 %collective-permute-start.29 = (bf16[384,1664]{1,0:T(8,128)(2,1)}, bf16[384,1664]{1,0:T(8,128)(2,1)}, u32[]{:S(2)}, u32[]{:S(2)}) collective-permute-start(bf16[384,1664]{1,0:T(8,128)(2,1)} %add.155.refs_1_), channel_id=1, source_target_pairs={{0,4},{4,0},{8,12},{12,8},{16,20},{20,16},{24,28},{28,24},{1,5},{5... | collective-permute-start | bytes 3833864 | tf_op jit(solution)/shard_map/ppermute | solution.py:88
  410.1 75.6 %collective-permute-start.17 = (bf16[384,1664]{1,0:T(8,128)(2,1)}, bf16[384,1664]{1,0:T(8,128)(2,1)S(1)}, u32[]{:S(2)}, u32[]{:S(2)}) collective-permute-start(bf16[384,1664]{1,0:T(8,128)(2,1)} %collective-permute-done.16.refs_1_), channel_id=1, source_target_pairs={{0,4},{4,0},{8,12},{12,8},{16,20},{20,16},{24,28},{28,24},{1,5},{5... | collective-permute-start | bytes 3833864 | tf_op jit(solution)/shard_map/ppermute | solution.py:88
  419.7 92.4 %collective-permute-start.15 = (bf16[384,1536]{1,0:T(8,128)(2,1)S(1)}, bf16[384,1536]{1,0:T(8,128)(2,1)}, u32[]{:S(2)}, u32[]{:S(2)}) collective-permute-start(bf16[384,1536]{1,0:T(8,128)(2,1)S(1)} %copy-done.33), channel_id=1, source_target_pairs={{0,4},{4,0},{8,12},{12,8},{16,20},{20,16},{24,28},{28,24},{1,5},{5... | collective-permute-start | bytes 3538952 | tf_op jit(solution)/shard_map/ppermute | solution.py:88
  450.9 85.3 %collective-permute-start.31 = (bf16[384,1536]{1,0:T(8,128)(2,1)}, bf16[384,1536]{1,0:T(8,128)(2,1)S(1)}, u32[]{:S(2)}, u32[]{:S(2)}) collective-permute-start(bf16[384,1536]{1,0:T(8,128)(2,1)} %get-tuple-element.136), channel_id=1, source_target_pairs={{0,4},{4,0},{8,12},{12,8},{16,20},{20,16},{24,28},{28,24},{1,5},{5... | collective-permute-start | bytes 3538952 | tf_op jit(solution)/shard_map/ppermute | solution.py:88
  458.6 88.8 %collective-permute-start.36 = (bf16[384,1536]{1,0:T(8,128)(2,1)S(1)}, bf16[384,1536]{1,0:T(8,128)(2,1)S(1)}, u32[]{:S(2)}, u32[]{:S(2)}) collective-permute-start(bf16[384,1536]{1,0:T(8,128)(2,1)S(1)} %add.159), channel_id=1, source_target_pairs={{0,8},{4,12},{24,16},{28,20},{1,9},{5,13},{25,17},{29,21},{2,10},{... | collective-permute-start | bytes 3538952 | tf_op jit(solution)/shard_map/ppermute | solution.py:80
  467.4 96.3 %collective-permute-start.10 = (bf16[384,1664]{1,0:T(8,128)(2,1)}, bf16[384,1664]{1,0:T(8,128)(2,1)S(1)}, u32[]{:S(2)}, u32[]{:S(2)}) collective-permute-start(bf16[384,1664]{1,0:T(8,128)(2,1)} %concatenate.19.refs_1_), channel_id=1, source_target_pairs={{0,4},{4,0},{8,12},{12,8},{16,20},{20,16},{24,28},{28,24},{1,5},{5... | collective-permute-start | bytes 3833864 | tf_op jit(solution)/shard_map/ppermute | solution.py:88
  510.0 79.0 %collective-permute-start.9 = (bf16[384,1536]{1,0:T(8,128)(2,1)}, bf16[384,1536]{1,0:T(8,128)(2,1)}, u32[]{:S(2)}, u32[]{:S(2)}) collective-permute-start(bf16[384,1536]{1,0:T(8,128)(2,1)} %get-tuple-element.104.refs_1_), channel_id=1, source_target_pairs={{0,4},{4,0},{8,12},{12,8},{16,20},{20,16},{24,28},{28,24},{1,5},{5... | collective-permute-start | bytes 3538952 | tf_op jit(solution)/shard_map/ppermute | solution.py:88
  536.6 71.4 %collective-permute-start.32 = (bf16[384,1536]{1,0:T(8,128)(2,1)S(1)}, bf16[384,1536]{1,0:T(8,128)(2,1)S(1)}, u32[]{:S(2)}, u32[]{:S(2)}) collective-permute-start(bf16[384,1536]{1,0:T(8,128)(2,1)S(1)} %add.156), channel_id=1, source_target_pairs={{0,8},{4,12},{24,16},{28,20},{1,9},{5,13},{25,17},{29,21},{2,10},{... | collective-permute-start | bytes 3538952 | tf_op jit(solution)/shard_map/ppermute | solution.py:80
  545.3 69.0 %collective-permute-start.34 = (bf16[384,1536]{1,0:T(8,128)(2,1)}, bf16[384,1536]{1,0:T(8,128)(2,1)}, u32[]{:S(2)}, u32[]{:S(2)}) collective-permute-start(bf16[384,1536]{1,0:T(8,128)(2,1)} %get-tuple-element.138), channel_id=1, source_target_pairs={{0,4},{4,0},{8,12},{12,8},{16,20},{20,16},{24,28},{28,24},{1,5},{5... | collective-permute-start | bytes 3538952 | tf_op jit(solution)/shard_map/ppermute | solution.py:88
  547.7 66.7 %collective-permute-start.37 = (bf16[384,1536]{1,0:T(8,128)(2,1)S(1)}, bf16[384,1536]{1,0:T(8,128)(2,1)S(1)}, u32[]{:S(2)}, u32[]{:S(2)}) collective-permute-start(bf16[384,1536]{1,0:T(8,128)(2,1)S(1)} %add.160), channel_id=1, source_target_pairs={{8,16},{12,20},{16,8},{20,12},{9,17},{13,21},{17,9},{21,13},{10,18... | collective-permute-start | bytes 3538952 | tf_op jit(solution)/shard_map/ppermute | solution.py:80
  774.6 230.5 %reduce-scatter.6.cloned.1.call-start = ((), (), s32[]{:S(2)}) async-start(), calls=%async_computation.6 | async-start | bytes 4866048 | tf_op jit(solution)/shard_map/reduce_scatter | solution.py:1085
  780.5 330.0 %reduce-scatter.8.cloned.1.call-start = ((), (), s32[]{:S(2)}) async-start(), calls=%async_computation.7 | async-start | bytes 4866048 | tf_op jit(solution)/shard_map/reduce_scatter | solution.py:1082
  870.2 97.8 %collective-permute-start.57 = (bf16[3,2,384,768]{3,2,1,0:T(8,128)(2,1)}, bf16[3,2,384,768]{3,2,1,0:T(8,128)(2,1)S(1)}, u32[]{:S(2)}, u32[]{:S(2)}) collective-permute-start(bf16[3,2,384,768]{3,2,1,0:T(8,128)(2,1)} %get-tuple-element.184), channel_id=1, source_target_pairs={{0,1},{1,0},{2,3},{3,2},{4,5},{5,4},{6,7},{7,6},{8,9},{9,8},{10,11... | collective-permute-start | bytes 10616840 | tf_op jit(solution)/shard_map/ppermute | solution.py:145
  875.2 92.8 %collective-permute-start.59 = (bf16[3,2,384,768]{3,2,1,0:T(8,128)(2,1)S(1)}, bf16[3,2,384,768]{3,2,1,0:T(8,128)(2,1)S(1)}, u32[]{:S(2)}, u32[]{:S(2)}) collective-permute-start(bf16[3,2,384,768]{3,2,1,0:T(8,128)(2,1)S(1)} %add.179), channel_id=1, source_target_pairs={{0,2},{1,3},{2,0},{3,1},{4,6},{5,7},{6,4},{7,5},{8,10},{9,11},{10,... | collective-permute-start | bytes 10616840 | tf_op jit(solution)/shard_map/ppermute | solution.py:145
  (80 other events, 1839.6 us)
Sparse Core Ops, SparseCore 0:
  11.5 79.8 all-gather.2
  94.3 77.6 all-gather.4
  774.7 96.7 reduce-scatter.3
  876.8 121.5 reduce-scatter.5
  1004.6 105.9 reduce-scatter.7

commit v2 on v1

v2 whole, which is shorter than its diff:
```python
import math

import jax
import jax.numpy as jnp
from jax import lax
from jax.experimental import pallas as pl
from jax.experimental.pallas import tpu as pltpu
from jax.sharding import PartitionSpec as P

HEADS = 12
KV_HEADS = 2
HEAD = 128
TOPK = 4
REPEAT = HEADS // KV_HEADS
HQ = HEADS * HEAD
KVW = KV_HEADS * HEAD
LANES = 128

EPS = 1e-06
ROPE_BASE = 10000.0
NEG = -1e30
BF = jnp.bfloat16
F32 = jnp.float32
NN = ((1,), (0,))
NT = ((1,), (1,))
TN = ((0,), (0,))
ANY = pl.BlockSpec(memory_space=pl.ANY)
MIB = 1024 * 1024
SCALE = 0.4


def mm(left, right, dims=NN):
    return lax.dot_general(left, right, (dims, ((), ())), preferred_element_type=F32)


def params(grid_rank, limit=56):
    return pltpu.CompilerParams(
        dimension_semantics=("arbitrary",) * grid_rank, vmem_limit_bytes=limit * MIB
    )


def busy(microseconds):
    return pl.CostEstimate(
        flops=int(microseconds * SCALE * 1.15e9), bytes_accessed=1024, transcendentals=0
    )


def sds(shape, dtype):
    return jax.ShapeDtypeStruct(shape, dtype)


def whole(shape):
    return pl.BlockSpec(shape, lambda *_: (0,) * len(shape))


def without(kernel, place, extra):
    def run(*refs):
        kernel(*refs[:place], *refs[place + extra :])

    return run


class Ring:
    def __init__(self, count):
        self.count = count
        self.low_pair = count == 8
        self.length = count // 2
        self.me = lax.axis_index("ctx")
        if self.low_pair:
            self.line, self.pair = self.me // 2, self.me % 2
        else:
            self.line, self.pair = self.me % self.length, self.me // self.length
        if self.length == 4:
            self.table = [[0, 1, 2, 3], [1, 0, 2, 3], [2, 3, 1, 0], [3, 2, 1, 0]]
        else:
            self.table = [
                [(place + step) % self.length for step in range(self.length)]
                for place in range(self.length)
            ]

    def index(self, line, pair):
        return line * 2 + pair if self.low_pair else pair * self.length + line

    def move(self, array, hops):
        pairs = [
            (self.index(source, side), self.index(target, side))
            for source, target in hops
            for side in (0, 1)
        ]
        return lax.ppermute(array, "ctx", pairs)

    def swap(self, array):
        pairs = [
            (self.index(place, side), self.index(place, 1 - side))
            for place in range(self.length)
            for side in (0, 1)
        ]
        return lax.ppermute(array, "ctx", pairs)

    def sources(self):
        line = jnp.asarray(self.table, jnp.int32)[self.line]
        side = jnp.stack([self.pair, 1 - self.pair]).astype(jnp.int32)
        return self.index(line[:, None], side[None, :]).reshape(-1).astype(jnp.int32)

    def spread(self, array):
        everything = lax.all_gather(array, "ctx", axis=0)
        order = self.sources()
        rows = [
            lax.dynamic_index_in_dim(everything, order[slot], 0, keepdims=False)
            for slot in range(self.count)
        ]
        return [(rows[2 * step], rows[2 * step + 1]) for step in range(self.length)]

    def gather(self, array, late=()):
        if self.length != 4:
            yield
            for couple in self.spread(array):
                yield couple
            return
        ends = [(1, 0), (2, 3)]
        middle = [(1, 2), (2, 1)]
        couples = [(0, 1), (1, 0), (2, 3), (3, 2)]
        first = self.move(array, couples)
        cross = self.move(array, middle)
        swapped = self.swap(array)
        until = yield
        first, cross = hold([first, cross], until, swapped)
        swapped = hold([swapped], cross)[0]
        outward = self.move(cross, ends)
        cross_two = self.move(first, middle)
        swapped_first = self.swap(first)
        until = yield (array, swapped)
        outward, cross_two = hold([outward, cross_two], until, swapped_first)
        second = cross + outward
        if late:
            cross_two, second = hold([cross_two, second], late[0])
        outward_two = self.move(cross_two, ends)
        swapped_second = self.swap(second)
        until = yield (first, swapped_first)
        outward_two = hold([outward_two], until, swapped_second)[0]
        third = cross_two + outward_two
        swapped_third = self.swap(third)
        yield (second, swapped_second)
        yield (third, swapped_third)

    def gather_now(self, array):
        run = self.gather(array)
        next(run)
        return [run.send(None) for _ in range(self.length)]

    def scatter(self, parts):
        if self.length != 4:
            order = self.sources()
            rows = jnp.stack([part for couple in parts for part in couple])
            placed = jnp.zeros_like(rows).at[order].set(rows)
            total = lax.psum_scatter(placed, "ctx", scatter_dimension=0, tiled=False)
            for _ in range(4):
                yield total
            yield [total]
            return
        inward = [(0, 1), (3, 2)]
        middle = [(1, 2), (2, 1)]
        couples = [(0, 1), (1, 0), (2, 3), (3, 2)]
        swapped = [self.swap(part[1]) for part in parts]
        until = yield parts[3][1]
        third = parts[3][0] + hold([swapped[3]], until)[0]
        from_end = self.move(third, inward)
        until = yield third
        from_end, arrived = hold([from_end, swapped[2]], until)
        sent = third + from_end
        crossed = self.move(sent, middle)
        second = parts[2][0] + arrived
        from_end_two = self.move(second, inward)
        until = yield second
        crossed, from_end_two, arrived = hold([crossed, from_end_two, swapped[1]], until)
        sent = parts[1][0] + arrived + crossed
        last = self.move(sent, couples)
        crossed_two = self.move(second + from_end_two, middle)
        until = yield sent
        last, crossed_two, arrived = hold([last, crossed_two, swapped[0]], until)
        yield [parts[0][0], arrived, crossed_two, last]

    def scatter_pairs(self, parts, pairs):
        if self.length != 4:
            flat = [pair[place] for pair in pairs for place in range(self.length // 2)]
            yield from self.scatter(list(zip(parts, reversed(flat))))
            return
        inward = [(0, 1), (3, 2)]
        middle = [(1, 2), (2, 1)]
        couples = [(0, 1), (1, 0), (2, 3), (3, 2)]
        swapped = [self.swap(pair) for pair in pairs]
        until = yield pairs[0]
        arrived = hold([swapped[0]], until)[0]
        third = parts[3] + arrived[0]
        second = parts[2] + arrived[1]
        from_end = self.move(third, inward)
        from_end_two = self.move(second, inward)
        until = yield second
        from_end, from_end_two, arrived = hold([from_end, from_end_two, swapped[1]], until)
        crossed = self.move(third + from_end, middle)
        sent = second + from_end_two
        crossed_two = self.move(sent, middle)
        until = yield sent
        crossed = hold([crossed], until)[0]
        sent = parts[1] + arrived[0] + crossed
        last = self.move(sent, couples)
        until = yield sent
        last, crossed_two = hold([last, crossed_two], until)
        yield [parts[0], arrived[1], crossed_two, last]

    def scatter_now(self, parts):
        run = self.scatter(parts)
        next(run)
        made = [run.send(None) for _ in range(4)]
        return made[-1]


def neighbour(array, axis_size, bit):
    pairs = [(index, index ^ (1 << bit)) for index in range(axis_size)]
    return lax.ppermute(array, "fsdp", pairs)


def gather_shards(array, axis_size, until=None):
    slots = {0: array}
    bits = axis_size.bit_length() - 1
    for bit in reversed(range(bits)):
        for slot in list(slots):
            taken = slots[slot]
            if slot and bit == 0 and until is not None:
                taken = slots[slot] = hold([taken], until)[0]
            slots[slot | (1 << bit)] = neighbour(taken, axis_size, bit)
    return [slots[slot] for slot in range(axis_size)]


def scatter_all_across(near, far, axis_size):
    arrived = neighbour(far, axis_size, 0)
    sent = near[1] + arrived[1]
    return near[0] + arrived[0] + neighbour(sent, axis_size, 1), sent


def scatter_all_along(terms, ring):
    swapped = ring.swap(terms[1])
    swapped = hold([swapped], (yield))[0]
    lines = terms[0] + swapped
    ends = ring.move(lines[2:4], [(0, 1), (3, 2)])
    ends = hold([ends], (yield))[0]
    middle = ring.move(lines[2:4] + ends, [(1, 2), (2, 1)])
    middle = hold([middle], (yield))[0]
    last = ring.move(lines[1] + middle[1], [(0, 1), (1, 0), (2, 3), (3, 2)])
    last = hold([last], (yield))[0]
    yield lines[0].astype(F32) + middle[0].astype(F32) + last.astype(F32)


def turn(values, cosine, sine):
    return values * cosine + pltpu.roll(values, HEAD // 2, 1) * sine


def qkv_kernel(x_ref, w_ref, g_ref, cos_ref, sin_ref, q_ref, kv_ref, low_ref, gain_ref):
    step = pl.program_id(0)
    blocks = HQ // 512

    @pl.when(step == 0)
    def _():
        gains = jnp.transpose(g_ref[...].astype(F32))
        gain_ref[...] = gains[0:8]
        wide = x_ref[...].astype(F32)
        scale = lax.rsqrt(jnp.mean(wide * wide, -1, keepdims=True) + EPS)
        low_ref[...] = (wide * scale * gains[0:1]).astype(BF)

    raw = mm(low_ref[...], w_ref[...])
    cosine, sine = cos_ref[...], sin_ref[...]

    def turned(count):
        return [
            turn(raw[:, head * HEAD : (head + 1) * HEAD], cosine, sine).astype(BF)
            for head in range(count)
        ]

    @pl.when(step < blocks)
    def _():
        for head, value in enumerate(turned(4)):
            q_ref[:, head * HEAD : (head + 1) * HEAD] = value

    @pl.when(step == blocks)
    def _():
        for head, value in enumerate(turned(KV_HEADS)):
            kv_ref[:, head * HEAD : (head + 1) * HEAD] = value
        kv_ref[:, KVW:] = raw[:, KVW:].astype(BF)


def qkv_call(x, w_full, cosine, sine, after=()):
    tokens, width = x.shape
    blocks = HQ // 512
    return pl.pallas_call(
        without(qkv_kernel, 5, len(after)),
        name="qkv",
        grid=(blocks + 1,),
        in_specs=[
            whole((tokens, width)),
            pl.BlockSpec((width, 512), lambda i: (0, i)),
            pl.BlockSpec((width, LANES), lambda i: (0, (2 * HQ + 2 * KVW) // LANES)),
            whole((tokens, HEAD)),
            whole((tokens, HEAD)),
        ]
        + [ANY] * len(after),
        out_specs=[
            pl.BlockSpec((tokens, 512), lambda i: (0, jnp.minimum(i, HQ // 512 - 1))),
            whole((tokens, 2 * KVW)),
            whole((tokens, width)),
            whole((8, width)),
        ],
        out_shape=[
            sds((tokens, HQ), BF),
            sds((tokens, 2 * KVW), BF),
            sds((tokens, width), BF),
            sds((8, width), F32),
        ],
        compiler_params=params(1),
        cost_estimate=busy(9),
    )(x, w_full, w_full, cosine, sine, *after)


HEADER = 5
SEQS = 3
COUPLE = 2
COUPLES = HEADS // COUPLE
LOG2E = math.log2(math.e)


def load_kv(slots, kv_all, sems):
    copies = [
        pltpu.make_async_copy(slot, kv_all.at[place], sems.at[place])
        for place, slot in enumerate(slots)
    ]
    for copy in copies:
        copy.start()
    for copy in copies:
        copy.wait()


def sequence_of(order_ref, index):
    ends = [order_ref[2 + place] for place in range(SEQS - 1)]
    return sum((index >= end).astype(jnp.int32) for end in ends)


def extend_queries(order_ref, q_ref, wide):
    tokens = q_ref.shape[0]
    rows = order_ref[0] * tokens + lax.broadcasted_iota(jnp.int32, (tokens, LANES), 0)
    lanes = lax.broadcasted_iota(jnp.int32, (tokens, LANES), 1)
    other = (lanes < SEQS) & (lanes != sequence_of(order_ref, rows))
    extra = jnp.where(other | (lanes > SEQS + order_ref[0]), NEG, 0.0).astype(BF)
    for place in range(COUPLE):
        span = slice(place * tokens, (place + 1) * tokens)
        wide[span, 0:HEAD] = q_ref[:, place * HEAD : (place + 1) * HEAD]
        wide[span, HEAD:] = extra


def extend_keys(order_ref, base, kv_all, groups, wide, turned, which):
    count, tokens, columns = kv_all.shape
    lanes = lax.broadcasted_iota(jnp.int32, (tokens, LANES), 1)
    sublanes = lax.broadcasted_iota(jnp.int32, (tokens, LANES), 0)
    for slot in range(count):
        block = order_ref[HEADER + base + slot]
        mine = lanes == sequence_of(order_ref, block * tokens + sublanes)
        unit = jnp.where(mine | (lanes == SEQS + block), 1.0, 0.0).astype(BF)
        for group in range(groups):
            span = slice(group * HEAD, (group + 1) * HEAD)
            wide[group, slot, :, 0:HEAD] = kv_all[slot, :, span]
            wide[group, slot, :, HEAD:] = unit
            start = which * groups * HEAD + group * HEAD
            taken = kv_all[slot, :, start : start + HEAD].astype(F32)
            turned[
                group * HEAD : (group + 1) * HEAD, slot * tokens : (slot + 1) * tokens
            ] = jnp.transpose(taken).astype(BF)


def causal(scores):
    tokens = scores.shape[0]
    keys = lax.broadcasted_iota(jnp.int32, (tokens, tokens), 0)
    queries = lax.broadcasted_iota(jnp.int32, (tokens, tokens), 1)
    kept = jnp.concatenate([keys <= queries] * COUPLE, 1)
    return jnp.where(kept, scores, NEG)


def attn_kernel(count, base, last, order_ref, q_ref, *rest):
    slots, rest = rest[:count], rest[count:]
    if base:
        acc_in, stat_in, *rest = rest
    if last:
        out_ref, total_ref, *rest = rest
    else:
        acc_out, stat_out, *rest = rest
    kv_all, keys, values, queries, spread, acc, stat, sems = rest
    step = pl.program_id(0)
    tokens = q_ref.shape[0]
    factor = HEAD ** (-0.5) * LOG2E

    @pl.when(step == 0)
    def _():
        load_kv(slots, kv_all, sems)
        extend_keys(order_ref, base, kv_all, KV_HEADS, keys, values, 1)

    group = step * COUPLE // REPEAT
    extend_queries(order_ref, q_ref, queries)
    if base:
        acc[...] = acc_in[0]
        stat[...] = stat_in[0]
    else:
        acc[...] = jnp.zeros_like(acc)
        stat[...] = jnp.zeros_like(stat)
        stat[0:1] = jnp.full((1, COUPLE * tokens), NEG, F32)

    scores = []
    new_peak = stat[0:1]
    for slot in range(count):
        made = mm(keys[group, slot], queries[...], NT)
        if base + slot == 0:
            made = causal(made)
        new_peak = jnp.maximum(new_peak, jnp.max(made, 0, keepdims=True))
        scores.append(made)
    keep = jnp.exp2((stat[0:1] - new_peak) * factor)
    total = stat[1:2] * keep
    added = acc[...] * keep
    for slot in range(count):
        weights = jnp.exp2((scores[slot] - new_peak) * factor)
        total += jnp.sum(weights, 0, keepdims=True)
        spread[slot * tokens : (slot + 1) * tokens] = weights.astype(BF)
    own = pl.ds(pl.multiple_of(group * HEAD, HEAD), HEAD)
    added += mm(values[own, :], spread[...])
    stat[0:1] = new_peak
    stat[1:2] = total
    acc[...] = added

    if last:
        made = acc[...] / stat[1:2]
        log_total = stat[0:1] * factor + jnp.log(stat[1:2]) * LOG2E
        for place in range(COUPLE):
            span = slice(place * tokens, (place + 1) * tokens)
            out_ref[:, place * HEAD : (place + 1) * HEAD] = jnp.transpose(made[:, span]).astype(BF)
            total_ref[0, place : place + 1] = log_total[:, span]
    else:
        acc_out[0] = acc[...]
        stat_out[0] = stat[...]


def attn_call(order, q, slots, base, last, state=(), after=()):
    tokens = q.shape[0]
    count = len(slots)
    wide = COUPLE * tokens
    column = lambda h, _: (0, h)
    by_step = lambda h, _: (h, 0, 0)
    if last:
        out_specs = [
            pl.BlockSpec((tokens, COUPLE * HEAD), column),
            pl.BlockSpec((1, 8, tokens), by_step),
        ]
        out_shape = [sds((tokens, HQ), BF), sds((COUPLES, 8, tokens), F32)]
    else:
        out_specs = [
            pl.BlockSpec((1, HEAD, wide), by_step),
            pl.BlockSpec((1, 8, wide), by_step),
        ]
        out_shape = [sds((COUPLES, HEAD, wide), F32), sds((COUPLES, 8, wide), F32)]
    state_specs = [
        pl.BlockSpec((1, HEAD, wide), by_step),
        pl.BlockSpec((1, 8, wide), by_step),
    ]
    grid = pltpu.PrefetchScalarGridSpec(
        num_scalar_prefetch=1,
        grid=(COUPLES,),
        in_specs=[pl.BlockSpec((tokens, COUPLE * HEAD), column)]
        + [ANY] * count
        + (state_specs if base else [])
        + [ANY] * len(after),
        out_specs=out_specs,
        scratch_shapes=[
            pltpu.VMEM((count, tokens, 2 * KVW), BF),
            pltpu.VMEM((KV_HEADS, count, tokens, 2 * HEAD), BF),
            pltpu.VMEM((KV_HEADS * HEAD, count * tokens), BF),
            pltpu.VMEM((wide, 2 * HEAD), BF),
            pltpu.VMEM((count * tokens, wide), BF),
            pltpu.VMEM((HEAD, wide), F32),
            pltpu.VMEM((8, wide), F32),
            pltpu.SemaphoreType.DMA((count,)),
        ],
    )
    return pl.pallas_call(
        without(
            lambda *refs: attn_kernel(count, base, last, *refs),
            2 + count + len(state),
            len(after),
        ),
        name="attention",
        grid_spec=grid,
        out_shape=out_shape,
        compiler_params=params(1),
        cost_estimate=busy(18),
    )(order, q, *slots, *state, *after)


def attn_back_kernel(count, group, order_ref, q_ref, do_ref, total_ref, delta_ref, *rest):
    cos_ref, sin_ref = rest[:2]
    slots, rest = rest[2 : 2 + count], rest[2 + count :]
    if group:
        rest = rest[count:]
    dq_ref, rest = rest[0], rest[1:]
    outs, rest = rest[:count], rest[count:]
    kv_all, keys, turned, queries, grads, spread, d_k, d_v, packed, sems = rest
    step = pl.program_id(0)
    tokens = q_ref.shape[0]
    scale = HEAD ** (-0.5)

    @pl.when(step == 0)
    def _():
        for part in range(2):
            columns = slice(part * KVW + group * HEAD, part * KVW + (group + 1) * HEAD)
            load_kv(
                [slot.at[:, columns] for slot in slots],
                kv_all.at[:, :, part * HEAD : (part + 1) * HEAD],
                sems,
            )
        extend_keys(order_ref, 0, kv_all, 1, keys, turned, 0)
        d_k[...] = jnp.zeros_like(d_k)
        d_v[...] = jnp.zeros_like(d_v)

    extend_queries(order_ref, q_ref, queries)
    for place in range(COUPLE):
        span = slice(place * tokens, (place + 1) * tokens)
        grads[span] = do_ref[:, place * HEAD : (place + 1) * HEAD]

    log_total = jnp.concatenate([total_ref[0, place : place + 1] for place in range(COUPLE)], 1)
    delta = jnp.concatenate([delta_ref[0, place : place + 1] for place in range(COUPLE)], 1)

    for slot in range(count):
        scores = mm(keys[0, slot], queries[...], NT)
        if slot == 0:
            scores = causal(scores)
        probs = jnp.exp2(scores * (scale * LOG2E) - log_total)
        grad_probs = mm(kv_all[slot, :, HEAD:], grads[...], NT)
        grad_scores = (probs * (grad_probs - delta)).astype(BF)
        spread[slot * tokens : (slot + 1) * tokens] = grad_scores
        d_v[slot] += mm(probs.astype(BF), grads[...])
        d_k[slot] += mm(grad_scores, queries[:, 0:HEAD])
    d_q = mm(turned[...], spread[...])
    for place in range(COUPLE):
        span = slice(place * tokens, (place + 1) * tokens)
        piece = jnp.transpose(d_q[:, span]) * scale
        dq_ref[:, place * HEAD : (place + 1) * HEAD] = turn(
            piece, cos_ref[...], -sin_ref[...]
        ).astype(BF)

    @pl.when(step == pl.num_programs(0) - 1)
    def _():
        copies = []
        for place in range(count):
            packed[place, :, 0:HEAD] = d_k[place].astype(BF)
            packed[place, :, HEAD:] = d_v[place].astype(BF)
            columns = pl.ds(group * 2 * HEAD, 2 * HEAD)
            copies.append(
                pltpu.make_async_copy(
                    packed.at[place], outs[place].at[:, columns], sems.at[place]
                )
            )
            copies[-1].start()
        for copy in copies:
            copy.wait()


def attn_back_call(
    group, order, q, grad, log_total, delta, cosine, sine, slots, held=(), after=()
):
    tokens = q.shape[0]
    count = len(slots)
    steps = REPEAT // COUPLE
    column = lambda h, _: (0, group * steps + h)
    by_step = lambda h, _: (group * steps + h, 0, 0)
    fixed = lambda h, _: (0, 0)
    grid = pltpu.PrefetchScalarGridSpec(
        num_scalar_prefetch=1,
        grid=(steps,),
        in_specs=[
            pl.BlockSpec((tokens, COUPLE * HEAD), column),
            pl.BlockSpec((tokens, COUPLE * HEAD), column),
            pl.BlockSpec((1, 8, tokens), by_step),
            pl.BlockSpec((1, 8, tokens), by_step),
            pl.BlockSpec((tokens, HEAD), fixed),
            pl.BlockSpec((tokens, HEAD), fixed),
        ]
        + [ANY] * (count + len(held) + len(after)),
        out_specs=[pl.BlockSpec((tokens, COUPLE * HEAD), lambda h, _: (0, h))] + [ANY] * count,
        scratch_shapes=[
            pltpu.VMEM((count, tokens, 2 * HEAD), BF),
            pltpu.VMEM((1, count, tokens, 2 * HEAD), BF),
            pltpu.VMEM((HEAD, count * tokens), BF),
            pltpu.VMEM((COUPLE * tokens, 2 * HEAD), BF),
            pltpu.VMEM((COUPLE * tokens, HEAD), BF),
            pltpu.VMEM((count * tokens, COUPLE * tokens), BF),
            pltpu.VMEM((count, tokens, HEAD), F32),
            pltpu.VMEM((count, tokens, HEAD), F32),
            pltpu.VMEM((count, tokens, 2 * HEAD), BF),
            pltpu.SemaphoreType.DMA((count,)),
        ],
    )
    return pl.pallas_call(
        without(
            lambda *refs: attn_back_kernel(count, group, *refs),
            7 + count + len(held),
            len(after),
        ),
        name="attention_back",
        input_output_aliases={7 + count + place: 1 + place for place in range(len(held))},
        grid_spec=grid,
        out_shape=[sds((tokens, HQ // KV_HEADS), BF)] + [sds((tokens, 2 * KVW), BF)] * count,
        compiler_params=params(1),
        cost_estimate=busy(26),
    )(order, q, grad, log_total, delta, cosine, sine, *slots, *held, *after)


def out_kernel(x_ref, a_ref, *rest):
    w_refs, (gain_ref, rows_ref, low_ref) = rest[:-3], rest[-3:]
    made = mm(a_ref[:, 0:512], w_refs[0][...], NT)
    for place, w_ref in enumerate(w_refs[1:], 1):
        made += mm(a_ref[:, place * 512 : (place + 1) * 512], w_ref[...], NT)
    rows = made.astype(BF)
    rows_ref[...] = rows
    resid = x_ref[...].astype(F32) + rows.astype(F32)
    scale = lax.rsqrt(jnp.mean(resid * resid, -1, keepdims=True) + EPS)
    low_ref[...] = (resid * scale * gain_ref[1:2]).astype(BF)


def wo_specs(width):
    start = (HQ + 2 * KVW) // 512
    return [
        pl.BlockSpec((width, 512), lambda i, place=place: (0, start + place))
        for place in range(HQ // 512)
    ]


def out_call(x, attended, wo_t, gains, after=()):
    tokens, width = x.shape
    tile = 128
    return pl.pallas_call(
        without(out_kernel, 3 + HQ // 512, len(after)),
        name="attention_out",
        grid=(tokens // tile,),
        in_specs=[
            pl.BlockSpec((tile, width), lambda i: (i, 0)),
            pl.BlockSpec((tile, HQ), lambda i: (i, 0)),
            *wo_specs(width),
            whole((8, width)),
        ]
        + [ANY] * len(after),
        out_specs=[pl.BlockSpec((tile, width), lambda i: (i, 0))] * 2,
        out_shape=[sds((tokens, width), BF)] * 2,
        compiler_params=params(1),
        cost_estimate=busy(9),
    )(x, attended, *[wo_t] * (HQ // 512), gains, *after)


def weight_copies(shards, own, kinds, held, sems):
    size = shards[0].shape[2]
    groups = []
    for expert in range(shards[0].shape[1]):
        copies = []
        for slot, shard in enumerate(shards):
            rows = pl.ds(pl.multiple_of((own ^ slot) * size, 16), size)
            for place, kind in enumerate(kinds):
                copies.append(
                    pltpu.make_async_copy(
                        shard.at[kind, expert],
                        held.at[place, expert, rows],
                        sems.at[place, expert, slot],
                    )
                )
        groups.append(copies)
    return groups


def fetch_weights(shards, own, kinds, held, sems):
    groups = weight_copies(shards, own, kinds, held, sems)
    step = pl.program_id(0)

    @pl.when(step == 0)
    def _():
        for copies in groups:
            for copy in copies:
                copy.start()

    for expert, copies in enumerate(groups):

        @pl.when(step == expert)
        def _():
            for copy in copies:
                copy.wait()


def route_kernel(shards_of, capacity, order_ref, d0_ref, d1_ref, *rest):
    shards = rest[:shards_of]
    p0_ref, p1_ref, gate_ref, rows_ref, hid_ref, held, sems = rest[shards_of:]
    expert = pl.program_id(0)
    tokens = d0_ref.shape[0]
    width = rows_ref.shape[2]
    fetch_weights(shards, order_ref[0], (2,), held, sems)
    wanted = (order_ref[1] * held.shape[1] + expert).astype(F32)
    before = lax.broadcasted_iota(jnp.int32, (tokens, tokens), 0) < lax.broadcasted_iota(
        jnp.int32, (tokens, tokens), 1
    )
    before = jnp.where(before, 1.0, 0.0).astype(BF)
    places = lax.broadcasted_iota(jnp.int32, (capacity, tokens), 0).astype(F32)
    for side, (ref, p_ref) in enumerate(((d0_ref, p0_ref), (d1_ref, p1_ref))):
        info = jnp.transpose(ref[:, width:].astype(F32))
        chosen = jnp.where(info[0:TOPK] == wanted, 1.0, 0.0)
        gate = jnp.sum(
            chosen * (info[TOPK : 2 * TOPK] + info[2 * TOPK : 3 * TOPK] + info[3 * TOPK : 4 * TOPK]),
            0,
            keepdims=True,
        )
        named = jnp.sum(chosen, 0, keepdims=True)
        rank = mm(jnp.broadcast_to(named, (8, tokens)).astype(BF), before)[0:1]
        picks = jnp.where((places == rank) & (named > 0.5), 1.0, 0.0)
        weight = jnp.sum(picks * gate, 1, keepdims=True)
        picks = picks.astype(BF)
        p_ref[0] = picks
        span = slice(side * capacity, (side + 1) * capacity)
        gate_ref[0, span] = jnp.broadcast_to(weight, (capacity, LANES))
        rows_ref[0, span] = (mm(picks, ref[:, :width]) * weight).astype(BF)
    hid_ref[0] = mm(rows_ref[0], held[0, expert])


def route_call(order, grads, shards, capacity, width, after=()):
    tokens = grads[0].shape[0]
    _, experts, size, hidden = shards[0].shape
    rows = 2 * capacity
    by_expert = lambda e, _: (e, 0, 0)
    grid = pltpu.PrefetchScalarGridSpec(
        num_scalar_prefetch=1,
        grid=(experts,),
        in_specs=[pl.BlockSpec(grads[0].shape, lambda e, _: (0, 0))] * 2
        + [ANY] * (len(shards) + len(after)),
        out_specs=[pl.BlockSpec((1, capacity, tokens), by_expert)] * 2
        + [
            pl.BlockSpec((1, rows, LANES), by_expert),
            pl.BlockSpec((1, rows, width), by_expert),
            pl.BlockSpec((1, rows, hidden), by_expert),
        ],
        scratch_shapes=[
            pltpu.VMEM((1, experts, width, hidden), BF),
            pltpu.SemaphoreType.DMA((1, experts, len(shards))),
        ],
    )
    return pl.pallas_call(
        without(
            lambda *refs: route_kernel(len(shards), capacity, *refs), 3 + len(shards), len(after)
        ),
        name="route",
        grid_spec=grid,
        out_shape=[sds((experts, capacity, tokens), BF)] * 2
        + [
            sds((experts, rows, LANES), F32),
            sds((experts, rows, width), BF),
            sds((experts, rows, hidden), F32),
        ],
        compiler_params=params(1),
        cost_estimate=busy(8.5),
    )(order, *grads, *shards, *after)


def expert_kernel(shards_of, capacity, order_ref, x0_ref, x1_ref, p0_ref, p1_ref, gh_ref, *rest):
    shards = rest[:shards_of]
    rows_ref, hid_ref, gg_ref, gu_ref, out0_ref, out1_ref, held, slot, acc, sems = rest[shards_of:]
    expert = pl.program_id(0)
    hidden = gh_ref.shape[2]
    width = x0_ref.shape[1]
    fetch_weights(shards, order_ref[0], (0, 1), held, sems)
    for side, (ref, p_ref) in enumerate(((x0_ref, p0_ref), (x1_ref, p1_ref))):
        span = slice(side * capacity, (side + 1) * capacity)
        rows_ref[0, span] = mm(p_ref[0], ref[...]).astype(BF)
    rows = rows_ref[0]
    tile = 256
    for start in range(0, hidden, tile):
        span = slice(start, start + tile)
        gate = mm(rows, held[0, expert, :, span])
        up = mm(rows, held[1, expert, :, span])
        grad = gh_ref[0, :, span]
        sigma = 1.0 / (1.0 + jnp.exp(-gate))
        active = gate * sigma
        hid_ref[0, :, span] = (active * up).astype(BF)
        gg_ref[0, :, span] = (grad * up * (sigma * (1.0 + gate * (1.0 - sigma)))).astype(BF)
        gu_ref[0, :, span] = (grad * active).astype(BF)
    tile = 512
    for start in range(0, width, tile):
        span = slice(start, start + tile)
        slot[:, span] = (
            mm(gg_ref[0], held[0, expert, span, :], NT)
            + mm(gu_ref[0], held[1, expert, span, :], NT)
        ).astype(BF)
    for side, (p_ref, out_ref) in enumerate(((p0_ref, out0_ref), (p1_ref, out1_ref))):
        span = slice(side * capacity, (side + 1) * capacity)
        term = mm(p_ref[0], slot[span], TN)

        @pl.when(expert == 0)
        def _():
            acc[side] = term

        @pl.when(expert > 0)
        def _():
            acc[side] += term

        @pl.when(expert == pl.num_programs(0) - 1)
        def _():
            out_ref[...] = acc[side].astype(BF)


def expert_call(order, xs, picks, grad_hidden, shards, capacity, after=()):
    tokens, width = xs[0].shape
    _, experts, size, hidden = shards[0].shape
    rows = 2 * capacity
    by_expert = lambda e, _: (e, 0, 0)
    fixed = lambda e, _: (0, 0)
    grid = pltpu.PrefetchScalarGridSpec(
        num_scalar_prefetch=1,
        grid=(experts,),
        in_specs=[pl.BlockSpec((tokens, width), fixed)] * 2
        + [pl.BlockSpec((1, capacity, tokens), by_expert)] * 2
        + [pl.BlockSpec((1, rows, hidden), by_expert)]
        + [ANY] * (len(shards) + len(after)),
        out_specs=[pl.BlockSpec((1, rows, width), by_expert)]
        + [pl.BlockSpec((1, rows, hidden), by_expert)] * 3
        + [pl.BlockSpec((tokens, width), fixed)] * 2,
        scratch_shapes=[
            pltpu.VMEM((2, experts, width, hidden), BF),
            pltpu.VMEM((rows, width), BF),
            pltpu.VMEM((2, tokens, width), F32),
            pltpu.SemaphoreType.DMA((2, experts, len(shards))),
        ],
    )
    return pl.pallas_call(
        without(
            lambda *refs: expert_kernel(len(shards), capacity, *refs), 6 + len(shards), len(after)
        ),
        name="experts",
        grid_spec=grid,
        out_shape=[sds((experts, rows, width), BF)]
        + [sds((experts, rows, hidden), BF)] * 3
        + [sds((tokens, width), BF)] * 2,
        compiler_params=params(1),
        cost_estimate=busy(17),
    )(order, *xs, *picks, grad_hidden, *shards, *after)


def down_kernel(shards_of, capacity, place, order_ref, hid_ref, gate_ref, p0_ref, p1_ref, *rest):
    shards = rest[:shards_of]
    out_ref, pair_ref, held, slot, acc, packed, sems, out_sem = rest[-8:]
    expert = pl.program_id(0)
    width = out_ref.shape[1]
    fetch_weights(shards, order_ref[0], (2,), held, sems)
    tile = 512
    for start in range(0, width, tile):
        span = slice(start, start + tile)
        made = mm(hid_ref[0], held[0, expert, span, :], NT).astype(BF).astype(F32)
        slot[:, span] = (made * gate_ref[0, :, 0:1]).astype(BF)
    for side, p_ref in enumerate((p0_ref, p1_ref)):
        span = slice(side * capacity, (side + 1) * capacity)
        term = mm(p_ref[0], slot[span], TN)

        @pl.when(expert == 0)
        def _():
            acc[side] = term

        @pl.when(expert > 0)
        def _():
            acc[side] += term

    @pl.when(expert == pl.num_programs(0) - 1)
    def _():
        packed[...] = acc[1].astype(BF)
        copy = pltpu.make_async_copy(packed, pair_ref.at[place], out_sem)
        copy.start()
        out_ref[...] = acc[0].astype(BF)
        copy.wait()


def down_call(order, hid, gates, picks, shards, capacity, width, place, pair, total, after=()):
    tokens = picks[0].shape[2]
    _, experts, size, hidden = shards[0].shape
    rows = 2 * capacity
    by_expert = lambda e, _: (e, 0, 0)
    pair = [] if pair is None else [pair]
    grid = pltpu.PrefetchScalarGridSpec(
        num_scalar_prefetch=1,
        grid=(experts,),
        in_specs=[
            pl.BlockSpec((1, rows, hidden), by_expert),
            pl.BlockSpec((1, rows, LANES), by_expert),
        ]
        + [pl.BlockSpec((1, capacity, tokens), by_expert)] * 2
        + [ANY] * (len(shards) + len(pair) + len(after)),
        out_specs=[whole((tokens, width)), ANY],
        scratch_shapes=[
            pltpu.VMEM((1, experts, width, hidden), BF),
            pltpu.VMEM((rows, width), BF),
            pltpu.VMEM((2, tokens, width), F32),
            pltpu.VMEM((tokens, width), BF),
            pltpu.SemaphoreType.DMA((1, experts, len(shards))),
            pltpu.SemaphoreType.DMA,
        ],
    )
    return pl.pallas_call(
        lambda *refs: down_kernel(len(shards), capacity, place, *refs),
        name="experts_down",
        grid_spec=grid,
        out_shape=[sds((tokens, width), BF), sds((total, tokens, width), BF)],
        input_output_aliases={5 + len(shards): 1} if pair else {},
        compiler_params=params(1),
        cost_estimate=busy(9.3),
    )(order, hid, gates, *picks, *shards, *pair, *after)


def weight_grad_kernel(chunks, *rest):
    xs, gs = rest[:chunks], rest[chunks : 2 * chunks]
    ggs, gus = rest[2 * chunks : 3 * chunks], rest[3 * chunks : 4 * chunks]
    hids = rest[4 * chunks : 5 * chunks]
    out_ref, left, rights = rest[5 * chunks :]
    rows = xs[0].shape[1]

    @pl.when(pl.program_id(0) == 0)
    def _():
        for kind, group in enumerate((ggs, gus, hids)):
            for place, ref in enumerate(group):
                rights[kind, place * rows : (place + 1) * rows] = ref[0]

    for kind, group in ((0, xs), (2, gs)):
        for place, ref in enumerate(group):
            left[place * rows : (place + 1) * rows] = ref[0]
        out_ref[kind] = mm(left[...], rights[kind], TN).astype(BF)
        if kind == 0:
            out_ref[1] = mm(left[...], rights[1], TN).astype(BF)


def weight_grad_call(expert, xs, gs, ggs, gus, hids, after=()):
    chunks = len(xs)
    _, rows, width = xs[0].shape
    hidden = ggs[0].shape[2]
    tile = 256
    return pl.pallas_call(
        without(lambda *refs: weight_grad_kernel(chunks, *refs), 5 * chunks, len(after)),
        name="expert_weight_grads",
        grid=(width // tile,),
        in_specs=[pl.BlockSpec((1, rows, tile), lambda i: (expert, 0, i))] * (2 * chunks)
        + [pl.BlockSpec((1, rows, hidden), lambda i: (expert, 0, 0))] * (3 * chunks)
        + [ANY] * len(after),
        out_specs=pl.BlockSpec((3, tile, hidden), lambda i: (0, i, 0)),
        out_shape=sds((3, width, hidden), BF),
        scratch_shapes=[
            pltpu.VMEM((chunks * rows, tile), BF),
            pltpu.VMEM((3, chunks * rows, hidden), BF),
        ],
        compiler_params=params(1),
        cost_estimate=busy(18),
    )(*xs, *gs, *ggs, *gus, *hids, *after)


def resid_back_kernel(
    terms, x_ref, rows_ref, dy_ref, gain_ref, att_ref, *rest
):
    w_refs, rest = rest[: HQ // 512], rest[HQ // 512 :]
    parts = rest[:terms]
    resid_ref, attn_ref, do_ref, delta_ref, gain_out, deltas = rest[terms:]
    step = pl.program_id(0)
    grad = parts[0][...].astype(F32)
    for part in parts[1:]:
        grad += part[...].astype(F32)
    resid = x_ref[...].astype(F32) + rows_ref[...].astype(F32)
    scale = lax.rsqrt(jnp.mean(resid * resid, -1, keepdims=True) + EPS)
    normed = resid * scale
    product = grad * normed
    partial = jnp.sum(product, 0, keepdims=True)

    @pl.when(step == 0)
    def _():
        gain_out[...] = jnp.broadcast_to(partial, gain_out.shape)

    @pl.when(step > 0)
    def _():
        gain_out[...] += partial

    gain = gain_ref[1:2]
    mean = jnp.mean(product * gain, -1, keepdims=True)
    total = dy_ref[...].astype(F32) + scale * (grad * gain - normed * mean)
    resid_ref[...] = total
    low = total.astype(BF)
    attn_ref[...] = low
    for place, w_ref in enumerate(w_refs):
        do_ref[:, place * 512 : (place + 1) * 512] = mm(low, w_ref[...]).astype(BF)
    each = do_ref[...].astype(F32) * att_ref[...].astype(F32)
    lanes = lax.broadcasted_iota(jnp.int32, deltas.shape, 1)
    made = jnp.zeros(deltas.shape, F32)
    for head in range(HEADS):
        value = jnp.sum(each[:, head * HEAD : (head + 1) * HEAD], -1, keepdims=True)
        made = jnp.where(lanes == head, value, made)
    deltas[...] = made
    turned = jnp.transpose(deltas[...])
    for head in range(HEADS):
        delta_ref[head // COUPLE, head % COUPLE : head % COUPLE + 1] = turned[head : head + 1]


def resid_back_call(x, rows, dy, gains, wo_t, attended, parts, after=()):
    tokens, width = x.shape
    tile = 128
    by_row = lambda i: (i, 0)
    return pl.pallas_call(
        without(
            lambda *refs: resid_back_kernel(len(parts), *refs),
            5 + HQ // 512 + len(parts),
            len(after),
        ),
        name="resid_back",
        grid=(tokens // tile,),
        in_specs=[pl.BlockSpec((tile, width), by_row)] * 3
        + [whole((8, width)), pl.BlockSpec((tile, HQ), by_row)]
        + wo_specs(width)
        + [pl.BlockSpec((tile, width), by_row)] * len(parts)
        + [ANY] * len(after),
        out_specs=[pl.BlockSpec((tile, width), by_row)] * 2
        + [
            pl.BlockSpec((tile, HQ), by_row),
            pl.BlockSpec((COUPLES, 8, tile), lambda i: (0, 0, i)),
            whole((8, width)),
        ],
        out_shape=[
            sds((tokens, width), F32),
            sds((tokens, width), BF),
            sds((tokens, HQ), BF),
            sds((COUPLES, 8, tokens), F32),
            sds((8, width), F32),
        ],
        scratch_shapes=[pltpu.VMEM((tile, LANES), F32)],
        compiler_params=params(1),
        cost_estimate=busy(10.5),
    )(x, rows, dy, gains, attended, *[wo_t] * (HQ // 512), *parts, *after)


def block_copies(order_ref, source, near, far, sems):
    shards_of, sides, steps, rows, _ = near.shape
    shards_of = 2 * shards_of
    copies = []
    for slot in range(shards_of):
        for place in range(sides * steps):
            block = order_ref[2 + place] * shards_of + (order_ref[0] ^ slot)
            target = far if slot % 2 else near
            copies.append(
                pltpu.make_async_copy(
                    source.at[pl.ds(pl.multiple_of(block * rows, 16), rows)],
                    target.at[slot // 2, place % 2, place // 2],
                    sems.at[slot * sides * steps + place],
                )
            )
    return copies


def cross_kernel(order_ref, left_ref, right_ref, near, far, made, sems):
    step = pl.program_id(0)
    tile = left_ref.shape[1]
    made[pl.ds(pl.multiple_of(step * tile, tile), tile)] = mm(
        left_ref[...], right_ref[...], TN
    ).astype(BF)

    @pl.when(step == pl.num_programs(0) - 1)
    def _():
        copies = block_copies(order_ref, made, near, far, sems)
        for copy in copies:
            copy.start()
        for copy in copies:
            copy.wait()


def blocks_shape(count, shards_of, rows, columns):
    return (shards_of // 2, 2, count // 2, rows // (count * shards_of), columns)


def cross_call(order, left, right, count, shards_of, name):
    tokens, rows = left.shape
    columns = right.shape[1]
    tile = 512
    grid = pltpu.PrefetchScalarGridSpec(
        num_scalar_prefetch=1,
        grid=(rows // tile,),
        in_specs=[
            pl.BlockSpec((tokens, tile), lambda i, _: (0, i)),
            pl.BlockSpec((tokens, columns), lambda i, _: (0, 0)),
        ],
        out_specs=[ANY] * 2,
        scratch_shapes=[
            pltpu.VMEM((rows, columns), BF),
            pltpu.SemaphoreType.DMA((count * shards_of,)),
        ],
    )
    return pl.pallas_call(
        cross_kernel,
        name=name,
        grid_spec=grid,
        out_shape=[sds(blocks_shape(count, shards_of, rows, columns), BF)] * 2,
        compiler_params=params(1),
        cost_estimate=busy(7.5),
    )(order, left, right)


def plain_cross_kernel(left_ref, right_ref, out_ref):
    out_ref[...] = mm(left_ref[...], right_ref[...], TN).astype(out_ref.dtype)


def plain_cross_call(left, right, name):
    tokens, rows = left.shape
    columns = right.shape[1]
    tile = 512
    return pl.pallas_call(
        plain_cross_kernel,
        name=name,
        grid=(rows // tile,),
        in_specs=[pl.BlockSpec((tokens, tile), lambda i: (0, i)), whole((tokens, columns))],
        out_specs=pl.BlockSpec((tile, columns), lambda i: (i, 0)),
        out_shape=sds((rows, columns), BF),
        compiler_params=params(1),
        cost_estimate=busy(7.5),
    )(left, right)


def input_q_kernel(dq_ref, w_ref, out_ref):
    out_ref[...] = mm(dq_ref[...], w_ref[...], NT)


def input_q_call(d_q, w_full):
    tokens = d_q.shape[0]
    width = w_full.shape[0]
    tile = 512
    return pl.pallas_call(
        input_q_kernel,
        name="input_grad_q",
        grid=(width // tile,),
        in_specs=[whole((tokens, HQ)), pl.BlockSpec((tile, HQ), lambda i: (i, 0))],
        out_specs=pl.BlockSpec((tokens, tile), lambda i: (0, i)),
        out_shape=sds((tokens, width), F32),
        compiler_params=params(1),
        cost_estimate=busy(6),
    )(d_q, w_full)


def final_kernel(
    terms,
    order_ref,
    x_ref,
    low_ref,
    resid_ref,
    gq_ref,
    gain_ref,
    moe_ref,
    w_ref,
    cos_ref,
    sin_ref,
    *rest,
):
    parts = rest[:terms]
    grad_ref = rest[terms]
    outs = rest[terms + 1 : -2]
    made, sems = rest[-2:]
    scale_k = HEAD ** (-0.5)
    cosine, sine = cos_ref[...], -sin_ref[...]
    key_grads, value_grads = [], []
    for group in range(KV_HEADS):
        span = slice(group * 2 * HEAD, (group + 1) * 2 * HEAD)
        total = parts[0][:, span].astype(F32)
        for part in parts[1:]:
            total += part[:, span].astype(F32)
        key_grads.append(turn(total[:, 0:HEAD] * scale_k, cosine, sine).astype(BF))
        value_grads.append(total[:, HEAD:].astype(BF))
    low = jnp.concatenate(key_grads + value_grads, 1)
    made[:, 0 : 2 * KVW] = mm(low_ref[...], low, TN).astype(BF)
    wide = x_ref[...].astype(F32)
    scale = lax.rsqrt(jnp.mean(wide * wide, -1, keepdims=True) + EPS)
    normed = wide * scale
    grad = gq_ref[...] + mm(low, w_ref[...], NT)
    product = grad * normed
    gain_part = jnp.sum(product, 0, keepdims=True)
    width = x_ref.shape[1]
    lines = lax.broadcasted_iota(jnp.int32, (LANES, width), 0)
    both = jnp.where(lines == 0, gain_part, jnp.where(lines == 1, moe_ref[0:1], 0.0))
    made[:, 2 * KVW :] = jnp.transpose(both).astype(BF)
    if len(outs) == 2:
        copies = block_copies(order_ref, made, *outs, sems)
    else:
        copies = [pltpu.make_async_copy(made, outs[0], sems.at[0])]
    for copy in copies:
        copy.start()
    gain = gain_ref[0:1]
    mean = jnp.mean(product * gain, -1, keepdims=True)
    own = (scale * (grad * gain - normed * mean)).astype(BF)
    grad_ref[...] = (resid_ref[...] + own.astype(F32)).astype(BF)
    for copy in copies:
        copy.wait()


def final_call(
    order, x, low, resid, grad_q, gains, moe_part, w_full, cosine, sine, parts, layout, after=()
):
    tokens, width = x.shape
    columns = 2 * KVW + LANES
    if layout:
        outs = [sds(blocks_shape(*layout, width, columns), BF)] * 2
    else:
        outs = [sds((width, columns), BF)]
    grid = pltpu.PrefetchScalarGridSpec(
        num_scalar_prefetch=1,
        grid=(1,),
        in_specs=[whole((tokens, width))] * 4
        + [whole((8, width))] * 2
        + [pl.BlockSpec((width, 2 * KVW), lambda i, _: (0, HQ // (2 * KVW)))]
        + [whole((tokens, HEAD))] * 2
        + [whole((tokens, 2 * KVW))] * len(parts)
        + [ANY] * len(after),
        out_specs=[whole((tokens, width))] + [ANY] * len(outs),
        scratch_shapes=[
            pltpu.VMEM((width, columns), BF),
            pltpu.SemaphoreType.DMA((layout[0] * layout[1] if layout else 1,)),
        ],
    )
    return pl.pallas_call(
        without(lambda *refs: final_kernel(len(parts), *refs), 10 + len(parts), len(after)),
        name="final",
        grid_spec=grid,
        out_shape=[sds((tokens, width), BF)] + outs,
        compiler_params=params(1),
        cost_estimate=busy(10),
    )(order, x, low, resid, grad_q, gains, moe_part, w_full, cosine, sine, *parts, *after)


def hold_kernel(count, *refs):
    del count, refs


def hold(arrays, *until):
    until = [array for array in until if array is not None]
    if not until:
        return arrays
    count = len(arrays)
    return pl.pallas_call(
        lambda *refs: hold_kernel(count, *refs),
        name="hold",
        in_specs=[ANY] * (count + len(until)),
        out_specs=[ANY] * count,
        out_shape=[sds(array.shape, array.dtype) for array in arrays],
        input_output_aliases={place: place for place in range(count)},
        cost_estimate=busy(0.5),
    )(*arrays, *until)


def local(
    layer_input,
    lengths,
    expert_ids,
    gate_weights,
    attn_gain,
    wq,
    wk,
    wv,
    wo,
    moe_gain,
    w_gate,
    w_up,
    w_down,
    cotangent,
):
    count = lax.axis_size("ctx")
    shards_of = lax.axis_size("fsdp")
    both = ("ctx", "fsdp")
    ring = Ring(count)
    me = lax.axis_index("ctx").astype(jnp.int32)
    own = lax.axis_index("fsdp").astype(jnp.int32)
    x = layer_input[0]
    dy = cotangent[0]
    tokens, width = x.shape
    exp_dev = w_gate.shape[0]
    experts = exp_dev * count
    capacity = 3 * tokens * TOPK // (2 * experts)

    sources = ring.sources()
    places = jnp.concatenate([jnp.stack([own, me]), sources])
    layout = (count, shards_of) if ring.length == 4 and shards_of == 4 else None
    rows = wq.shape[0]
    gains_part = jnp.concatenate(
        [attn_gain[:, None], moe_gain[:, None], jnp.zeros((rows, LANES - 2), BF)], 1
    )
    w_full = lax.all_gather(
        jnp.concatenate([wq, wk, wv, wo.T, gains_part], 1), both, axis=0, tiled=True
    )

    gates = gate_weights[0]
    gate_high = gates.astype(BF)
    rest = gates - gate_high.astype(F32)
    gate_mid = rest.astype(BF)
    gate_low = (rest - gate_mid.astype(F32)).astype(BF)
    info = jnp.concatenate(
        [
            dy,
            expert_ids[0].astype(BF),
            gate_high,
            gate_mid,
            gate_low,
            jnp.zeros((tokens, LANES - 4 * TOPK), BF),
        ],
        1,
    )
    ends = jnp.cumsum(lengths[0])
    index = me * tokens + jnp.arange(tokens, dtype=jnp.int32)
    after = (index[:, None] >= ends[None, :]).astype(jnp.int32)
    start = jnp.sum(after * lengths[0][None, :], 1)
    half = HEAD // 2
    freq = jnp.exp(jnp.arange(half, dtype=F32) * (-2.0 * math.log(ROPE_BASE) / HEAD))
    angle = (index - start).astype(F32)[:, None] * freq[None, :]
    cosine = jnp.cos(angle)
    sine = jnp.sin(angle)
    cosine = jnp.concatenate([cosine, cosine], 1)
    sine = jnp.concatenate([-sine, sine], 1)
    order = jnp.concatenate(
        [me[None], (start[0] // tokens)[None], ends[: HEADER - 2], sources]
    )

    late = []
    run = ring.gather(info, late)
    next(run)
    grads = [run.send(None)]
    q, kv, low_one, gains = qkv_call(
        x, w_full, cosine, sine, [grads[0][1]] if layout else []
    )
    shards = gather_shards(
        jnp.stack([w_gate, w_up, jnp.swapaxes(w_down, 1, 2)]), shards_of, kv
    )
    kv_couples = ring.gather_now(kv)
    kv_slots = [part for couple in kv_couples for part in couple]
    half = count // 2
    parts, made, routed = [], [], []

    def route(step, after=()):
        routed.append(route_call(places, grads[step], shards, capacity, width, after))
        return routed[-1][4]

    late.append(kv_couples[3][0])
    grads.append(run.send(None))
    state = attn_call(order, q, kv_slots[:half], 0, False, after=[route(0)])
    attended, log_total = attn_call(order, q, kv_slots[half:], half, True, state)
    attn_rows, low_two = out_call(x, attended, w_full, gains)
    grads += [run.send(None) for _ in range(2, half)]

    def run_experts(step, couple, after):
        pick0, pick1, _, _, grad_hidden = routed[step]
        found = expert_call(
            places, couple, (pick0, pick1), grad_hidden, shards, capacity, after
        )
        made.append(found[:4])
        parts.append((found[4], found[5]))
        return found[4]

    rows_run = ring.gather(low_two)
    next(rows_run)
    mark = route(2, [route(1)])
    couple = rows_run.send(mark)
    mark = run_experts(0, couple, [mark])
    couple = rows_run.send(mark)
    for step in range(3, half):
        mark = route(step, [couple[1]])
    mark = run_experts(1, couple, [mark])
    for step in range(2, half):
        couple = rows_run.send(mark)
        mark = run_experts(step, couple, [mark])

    y_pairs = []

    def down(step, after):
        pick0, pick1, gate_rows = routed[step][:3]
        place = (half - 1 - step) % (half // 2)
        out, pair = down_call(
            places,
            made[step][1],
            gate_rows,
            (pick0, pick1),
            shards,
            capacity,
            width,
            place,
            y_pairs.pop() if place else None,
            half // 2,
            after,
        )
        y_pairs.append(pair)
        return out

    grad_run = ring.scatter(parts)
    grad_mark = next(grad_run)
    expert_grads = []
    for expert in range(exp_dev):
        made_grad = weight_grad_call(
            expert,
            [entry[0] for entry in made],
            [entry[3] for entry in routed],
            [entry[2] for entry in made],
            [entry[3] for entry in made],
            [entry[1] for entry in made],
            [mark, grad_mark],
        )
        expert_grads.append(
            lax.psum_scatter(made_grad, "fsdp", scatter_dimension=1, tiled=True).astype(F32)
        )
        mark = made_grad
        if expert < 2:
            grad_mark = grad_run.send(mark)
    expert_grads = jnp.stack(expert_grads, 1)
    y_parts = [None] * len(made)
    for step in reversed(range(len(made))):
        y_parts[step] = down(step, [mark, grad_mark])
        mark = y_parts[step]
        if step == len(made) // 2:
            grad_mark = grad_run.send(mark)
    grad_parts = grad_run.send(mark)
    y_run = ring.scatter_pairs(y_parts, hold(y_pairs, grad_mark))
    next(y_run)

    resid, grad_attn, grad_out, delta, moe_part = resid_back_call(
        x, attn_rows, dy, gains, w_full, attended, grad_parts
    )
    back = attn_back_call(
        0, order, q, grad_out, log_total, delta, cosine, sine, kv_slots
    )
    d_q = [back[0]]
    mark = y_run.send(back[0])
    back = attn_back_call(
        1,
        order,
        q,
        grad_out,
        log_total,
        delta,
        cosine,
        sine,
        kv_slots,
        back[1:],
        [mark],
    )
    d_q.append(back[0])
    kv_terms = ring.scatter_now(
        [(back[1 + 2 * step], back[2 + 2 * step]) for step in range(half)]
    )
    y_run.send(kv_terms[-1])

    d_q = jnp.concatenate(d_q, 1)
    grad_q = input_q_call(d_q, w_full)
    after = []
    if layout:
        wq_part = cross_call(places, low_one, d_q, *layout, "wq_grad")
        wo_part = cross_call(places, hold([grad_attn], d_q)[0], attended, *layout, "wo_grad")
        wo_terms, wo_sent = scatter_all_across(*wo_part, shards_of)
        wq_terms, wq_sent = scatter_all_across(*wq_part, shards_of)
        after = [wo_sent, wq_sent]
    else:
        wq_grad, wo_grad = [
            lax.psum_scatter(
                plain_cross_call(left, right, name), both, scatter_dimension=0, tiled=True
            ).astype(F32)
            for left, right, name in (
                (low_one, d_q, "wq_grad"),
                (grad_attn, attended, "wo_grad"),
            )
        ]
    input_grad, *tail = final_call(
        places,
        x,
        low_one,
        resid,
        grad_q,
        gains,
        moe_part,
        w_full,
        cosine,
        sine,
        kv_terms,
        layout,
        after,
    )
    if layout:
        terms = jnp.concatenate([wo_terms, wq_terms], -1)
        first_run = scatter_all_along(hold([terms], kv_terms[-1])[0], ring)
        next(first_run)
        tail, tail_sent = scatter_all_across(*tail, shards_of)
        y_run.send(tail_sent)
        last_run = scatter_all_along(tail, ring)
        next(last_run)
        for _ in range(4):
            terms = first_run.send(None)
            tail = last_run.send(None)
        wo_grad, wq_grad = terms[:, :HQ], terms[:, HQ:]
    else:
        y_run.send(None)
        tail = lax.psum_scatter(tail[0], both, scatter_dimension=0, tiled=True).astype(F32)
    y_terms = y_run.send(None)
    moe = y_terms[0].astype(F32)
    for term in y_terms[1:]:
        moe = moe + term.astype(F32)
    output = (x.astype(F32) + attn_rows.astype(F32) + moe).astype(BF)
    return (
        output[None],
        input_grad[None],
        tail[:, 2 * KVW],
        wq_grad,
        tail[:, 0:KVW],
        tail[:, KVW : 2 * KVW],
        wo_grad.T,
        tail[:, 2 * KVW + 1],
        expert_grads[0],
        expert_grads[1],
        jnp.swapaxes(expert_grads[2], 1, 2),
    )


def solution(mesh):
    return jax.shard_map(
        local,
        mesh=mesh,
        in_specs=(
            P("fsdp", "ctx", None),
            P("fsdp", None),
            P("fsdp", "ctx", None),
            P("fsdp", "ctx", None),
            P(("ctx", "fsdp")),
            P(("ctx", "fsdp"), None),
            P(("ctx", "fsdp"), None),
            P(("ctx", "fsdp"), None),
            P(None, ("ctx", "fsdp")),
            P(("ctx", "fsdp")),
            P("ctx", "fsdp", None),
            P("ctx", "fsdp", None),
            P("ctx", None, "fsdp"),
            P("fsdp", "ctx", None),
        ),
        out_specs=(
            P("fsdp", "ctx", None),
            P("fsdp", "ctx", None),
            P(("ctx", "fsdp")),
            P(("ctx", "fsdp"), None),
            P(("ctx", "fsdp"), None),
            P(("ctx", "fsdp"), None),
            P(None, ("ctx", "fsdp")),
            P(("ctx", "fsdp")),
            P("ctx", "fsdp", None),
            P("ctx", "fsdp", None),
            P("ctx", None, "fsdp"),
        ),
        check_vma=False,
    )
```

time: 1130 us -> 886 us (0.78)
  waiting for transfers between devices: 538 us -> 297 us
  starting transfers between devices: 215 us -> 136 us
  Pallas kernels: 283 us -> 319 us
  other arithmetic: 39.2 us -> 63 us
  local copies, waits for them, and re-layouts: 26.3 us -> 47.1 us
    ppermute x30 -> x36, waiting for transfers between devices: 206 us -> 82 us  [move(): return lax.ppermute(array, 'ctx', pairs)]
    reduce_scatter x3 -> x2, waiting for transfers between devices: 104 us -> 0.01 us  [local(): lax.psum_scatter(made_grad, 'fsdp', scatter_dimension=1, tiled=True)]
    ppermute x24, waiting for transfers between devices: 158 us -> 110 us  [swap(): return lax.ppermute(array, 'ctx', pairs)]
    ppermute x6 -> x9, waiting for transfers between devices: 0.02 us -> 44.8 us  [neighbour(): return lax.ppermute(array, 'fsdp', pairs)]
    ppermute x30 -> x36, starting transfers between devices: 151 us -> 107 us  [move(): return lax.ppermute(array, 'ctx', pairs)]
    ppermute x24, starting transfers between devices: 61.2 us -> 20.8 us  [swap(): return lax.ppermute(array, 'ctx', pairs)]
    pallas_call x21 -> x24, Pallas kernels: 277 us -> 313 us  [the longest x4 67.3 us: expert_call(): pl.pallas_call(without(lambda *refs: expert_kernel(len(shards), capacity,...]
    add x14 -> x26, other arithmetic: 11.4 us -> 29.2 us  [the longest x3 4.24 us: scatter_all_across(): sent = near[1] + arrived[1]]
  transfers between devices with their start and end apart: 65 -> 72, of which waited for: 30 -> 26; matrix products, arithmetic and copies ran while one was open for 5% -> 9% of each run, Pallas kernels for 22% -> 33%
where the time goes in v2:
time: 886 us; the launch traced here: 878 us
  Pallas kernels  319 us (36%)
  waiting for transfers between devices  297 us (34%)
  starting transfers between devices  136 us (15%)
  other arithmetic  63 us (7%)
  local copies, waits for them, and re-layouts  47.1 us (5%)
  between operations  17 us (2%)
    ppermute x24, waiting for transfers between devices, swap(): return lax.ppermute(array, 'ctx', pairs)  110 us
    ppermute x36, starting transfers between devices, move(): return lax.ppermute(array, 'ctx', pairs)  107 us
    ppermute x36, waiting for transfers between devices, move(): return lax.ppermute(array, 'ctx', pairs)  82 us
    pallas_call x4, Pallas kernels, expert_call(): pl.pallas_call(without(lambda *refs: expert_kernel(len(shards), capacity,...  67.3 us
    all_gather x1, waiting for transfers between devices, local(): lax.all_gather(jnp.concatenate([wq, wk, wv, wo.T, gains_part], 1), both,...  59.6 us
    pallas_call x2, Pallas kernels, attn_back_call(): pl.pallas_call(without(lambda *refs: attn_back_kernel(count, group, *refs...  52.7 us
    ppermute x9, waiting for transfers between devices, neighbour(): return lax.ppermute(array, 'fsdp', pairs)  44.8 us
    pallas_call x4, Pallas kernels, down_call(): pl.pallas_call(lambda *refs: down_kernel(len(shards), capacity, place, *r...  39.4 us
  transfers between devices with their start and end apart: 72, of which 26 were waited for; matrix products, arithmetic and copies ran while one was open for 9% of the time, Pallas kernels for 33%

profile of v2, /device:TPU:0, one launch (start us, length us, event | category | flops | bytes accessed | tf_op | source)
XLA Modules:
  0.0 878.5 jit_solution(9125897841262487607)
XLA Ops:
  37.4 42.4 %collective-permute-done.1.refs_0_ = bf16[384,1664]{1,0:T(8,128)(2,1)} collective-permute-done((bf16[384,1664]{1,0:T(8,128)(2,1)}, bf16[384,1664]{1,0:T(8,128)(2,1)}, u32[]{:S(2)}, u32[]{:S(2)}) %collective-permute-start.1) | collective-permute-done | bytes 1277984 | tf_op jit(solution)/shard_map/ppermute | solution.py:90
  79.8 59.6 %all-gather.2.cloned.1.call-done.refs_1_.refs_2_.refs_3_.refs_4_.refs_5_.refs_6_.refs_7_.w_ref = bf16[1536,3712]{1,0:T(8,128)(2,1)} async-done(((bf16[48,3712]{1,0:T(8,128)(2,1)}), bf16[1536,3712]{1,0:T(8,128)(2,1)}) %all-gather.2.cloned.1.call-update) | async-done | bytes 11403280 | tf_op jit(solution)/shard_map/all_gather | solution.py:1292
  166.3 11.1 %collective-permute-done.6.refs_0_ = bf16[384,512]{1,0:T(8,128)(2,1)} collective-permute-done((bf16[384,512]{1,0:T(8,128)(2,1)}, bf16[384,512]{1,0:T(8,128)(2,1)}, u32[]{:S(2)}, u32[]{:S(2)}) %collective-permute-start.6) | collective-permute-done | bytes 393248 | tf_op jit(solution)/shard_map/ppermute | solution.py:90
  186.3 16.6 %collective-permute-done.18.refs_0_ = bf16[384,1664]{1,0:T(8,128)(2,1)} collective-permute-done((bf16[384,1664]{1,0:T(8,128)(2,1)}, bf16[384,1664]{1,0:T(8,128)(2,1)}, u32[]{:S(2)}, u32[]{:S(2)}) %collective-permute-start.18) | collective-permute-done | bytes 1277984 | tf_op jit(solution)/shard_map/ppermute | solution.py:90
  228.7 17.7 %attention.2 = (f32[6,128,768]{2,1,0:T(8,128)}, f32[6,8,768]{2,1,0:T(8,128)}) custom-call(s32[13]{0:T(128)} %pad_add_fusion.1.refs_0_, bf16[384,1536]{1,0:T(8,128)(2,1)} %get-tuple-element.131.refs_1_, bf16[384,512]{1,0:T(8,128)(2,1)} %get-tuple-element.132.refs_1_.refs_2_.refs_7_, bf16[384,512]{1,0:T(8,128)(2,1)} %hold.29.refs_3_.refs_8_, ...), custom_call_target="tpu_custom_call" | custom-call | flops 8280000000 | bytes 1024 | tf_op jit(solution)/shard_map/attention/pallas_call | solution.py:487
  246.4 18.3 %attention.3 = (bf16[384,1536]{1,0:T(8,128)(2,1)}, f32[6,8,384]{2,1,0:T(8,128)}) custom-call(s32[13]{0:T(128)} %pad_add_fusion.1.refs_0_, bf16[384,1536]{1,0:T(8,128)(2,1)} %get-tuple-element.131.refs_1_, bf16[384,512]{1,0:T(8,128)(2,1)} %add.222.refs_2_.refs_11_, bf16[384,512]{1,0:T(8,128)(2,1)} %collective-permute-done.9.refs_1_.refs_3_.refs_12_, ...), custom_call_target="tpu_custom_call" | custom-call | flops 8280000000 | bytes 1024 | tf_op jit(solution)/shard_map/attention/pallas_call | solution.py:487
  314.6 16.7 %experts.4 = (bf16[2,288,1536]{2,1,0:T(8,128)(2,1)}, bf16[2,288,768]{2,1,0:T(8,128)(2,1)}, bf16[2,288,768]{2,1,0:T(8,128)(2,1)}, bf16[2,288,768]{2,1,0:T(8,128)(...) custom-call(s32[10]{0:T(128)} %pad_add_fusion.2.refs_0_.order_ref, ...), custom_call_target="tpu_custom_call" | custom-call | flops 7820000256 | bytes 1024 | tf_op jit(solution)/shard_map/experts/pallas_call | solution.py:837
  343.1 22.5 %collective-permute-done.24.refs_2_ = bf16[384,1664]{1,0:T(8,128)(2,1)} collective-permute-done((bf16[384,1664]{1,0:T(8,128)(2,1)S(1)}, bf16[384,1664]{1,0:T(8,128)(2,1)}, u32[]{:S(2)}, u32[]{:S(2)}) %collective-permute-start.24) | collective-permute-done | bytes 1277984 | tf_op jit(solution)/shard_map/ppermute | solution.py:98
  374.1 16.7 %experts.5 = (bf16[2,288,1536]{2,1,0:T(8,128)(2,1)}, bf16[2,288,768]{2,1,0:T(8,128)(2,1)}, bf16[2,288,768]{2,1,0:T(8,128)(2,1)}, bf16[2,288,768]{2,1,0:T(8,128)(...) custom-call(s32[10]{0:T(128)} %pad_add_fusion.2.refs_0_.order_ref, ...), custom_call_target="tpu_custom_call" | custom-call | flops 7820000256 | bytes 1024 | tf_op jit(solution)/shard_map/experts/pallas_call | solution.py:837
  396.4 16.7 %experts.6 = (bf16[2,288,1536]{2,1,0:T(8,128)(2,1)}, bf16[2,288,768]{2,1,0:T(8,128)(2,1)}, bf16[2,288,768]{2,1,0:T(8,128)(2,1)}, bf16[2,288,768]{2,1,0:T(8,128)(...) custom-call(s32[10]{0:T(128)} %pad_add_fusion.2.refs_0_.order_ref, bf16[384,1536]{1,0:T(8,128)(2,1)} %copy-done.50, ...), custom_call_target="tpu_custom_call" | custom-call | flops 7820000256 | bytes 1024 | tf_op jit(solution)/shard_map/experts/pallas_call | solution.py:837
  414.2 17.2 %experts.7 = (bf16[2,288,1536]{2,1,0:T(8,128)(2,1)}, bf16[2,288,768]{2,1,0:T(8,128)(2,1)}, bf16[2,288,768]{2,1,0:T(8,128)(2,1)}, bf16[2,288,768]{2,1,0:T(8,128)(...) custom-call(s32[10]{0:T(128)} %pad_add_fusion.2.refs_0_.order_ref, bf16[384,1536]{1,0:T(8,128)(2,1)} %copy-done.51, ...), custom_call_target="tpu_custom_call" | custom-call | flops 7820000256 | bytes 1024 | tf_op jit(solution)/shard_map/experts/pallas_call | solution.py:837
  431.3 15.3 %expert_weight_grads.2.refs_1_.refs_20_ = bf16[3,1536,768]{2,1,0:T(8,128)(2,1)} custom-call(bf16[2,288,1536]{2,1,0:T(8,128)(2,1)} %get-tuple-element.175.refs_0_, bf16[2,288,1536]{2,1,0:T(8,128)(2,1)} %get-tuple-element.176.refs_1_, bf16[2,288,1536]{2,1,0:T(8,128)(2,1)} %get-tuple-element.177.refs_2_, bf16[2,288,1536]{2,1,0:T(8,128)(2,1)} %get-tuple-element.178.refs_3_, ...), custom_call_target="tpu_custom_call" | custom-call | flops 8280000000 | bytes 1024 | tf_op jit(solution)/shard_map/expert_weight_grads/pallas_call | solution.py:945
  448.9 27.1 %collective-permute-done.30.refs_0_ = bf16[384,1536]{1,0:T(8,128)(2,1)S(1)} collective-permute-done((bf16[384,1536]{1,0:T(8,128)(2,1)}, bf16[384,1536]{1,0:T(8,128)(2,1)S(1)}, u32[]{:S(2)}, u32[]{:S(2)}) %collective-permute-start.30) | collective-permute-done | bytes 1179680 | tf_op jit(solution)/shard_map/ppermute | solution.py:98
  482.6 15.4 %expert_weight_grads.3.refs_2_.refs_9_ = bf16[3,1536,768]{2,1,0:T(8,128)(2,1)} custom-call(bf16[2,288,1536]{2,1,0:T(8,128)(2,1)} %get-tuple-element.175.refs_0_, bf16[2,288,1536]{2,1,0:T(8,128)(2,1)} %get-tuple-element.176.refs_1_, bf16[2,288,1536]{2,1,0:T(8,128)(2,1)} %get-tuple-element.177.refs_2_, bf16[2,288,1536]{2,1,0:T(8,128)(2,1)} %get-tuple-element.178.refs_3_, ...), custom_call_target="tpu_custom_call" | custom-call | flops 8280000000 | bytes 1024 | tf_op jit(solution)/shard_map/expert_weight_grads/pallas_call | solution.py:945
  514.4 10.0 %experts_down.4 = (bf16[384,1536]{1,0:T(8,128)(2,1)}, bf16[2,384,1536]{2,1,0:T(8,128)(2,1)}) custom-call(s32[10]{0:T(128)} %pad_add_fusion.2.refs_0_.order_ref, bf16[2,288,768]{2,1,0:T(8,128)(2,1)} %get-tuple-element.173.refs_19_.refs_1_, f32[2,288,128]{2,1,0:T(8,128)} %get-tuple-element.174.refs_2_, bf16[2,144,384]{2,1,0:T(8,128)(2,1)} %get-tuple-element.170.refs_3_, ...), custom_call_target="tpu_custom_call" | custom-call | flops 4278000128 | bytes 1024 | tf_op jit(solution)/shard_map/experts_down/pallas_call | solution.py:908
  565.7 10.3 %resid_back.1 = (f32[384,1536]{1,0:T(8,128)}, bf16[384,1536]{1,0:T(8,128)(2,1)}, bf16[384,1536]{1,0:T(8,128)(2,1)}, f32[6,8,384]{2,1,0:T(8,128)}, f32[8,1536]{1,0:T(8,128)}) custom-call(bf16[384,1536]{1,0:T(8,128)(2,1)} %bitcast.108, bf16[384,1536]{1,0:T(8,128)(2,1)} %get-tuple-element.142.refs_1_, bf16[384,1536]{1,0:T(8,128)(2,1)} %bitcast.111, ...), custom_call_target="tpu_custom_call" | custom-call | flops 4830000128 | bytes 1024 | tf_op jit(solution)/shard_map/resid_back/pallas_call | solution.py:1011
  576.0 26.2 %attention_back.2 = (bf16[384,768]{1,0:T(8,128)(2,1)}, bf16[384,512]{1,0:T(8,128)(2,1)}, bf16[384,512]{1,0:T(8,128)(2,1)}, bf16[384,512]{1,0:T(8,128)(2,1)}, bf1...) custom-call(s32[13]{0:T(128)} %pad_add_fusion.1.refs_0_, ...), custom_call_target="tpu_custom_call" | custom-call | flops 11960000512 | bytes 1024 | tf_op jit(solution)/shard_map/attention_back/pallas_call | solution.py:604
  609.9 26.5 %attention_back.3 = (bf16[384,768]{1,0:T(8,128)(2,1)}, bf16[384,512]{1,0:T(8,128)(2,1)}, bf16[384,512]{1,0:T(8,128)(2,1)}, bf16[384,512]{1,0:T(8,128)(2,1)}, bf1...) custom-call(s32[13]{0:T(128)} %pad_add_fusion.1.refs_0_, ...), custom_call_target="tpu_custom_call", output_to_operand_aliasing={{1}: (15, {}), {2}: (16, {}), {3}: (17, {}), {4}: (18, {}),... | custom-call | flops 11960000512 | bytes 1024 | tf_op jit(solution)/shard_map/attention_back/pallas_call | solution.py:604
  656.6 9.9 %collective-permute-done.44 = bf16[384,512]{1,0:T(8,128)(2,1)S(1)} collective-permute-done((bf16[384,512]{1,0:T(8,128)(2,1)S(1)}, bf16[384,512]{1,0:T(8,128)(2,1)S(1)}, u32[]{:S(2)}, u32[]{:S(2)}) %collective-permute-start.44) | collective-permute-done | bytes 393248 | tf_op jit(solution)/shard_map/ppermute | solution.py:98
  701.7 10.4 %final.1 = (bf16[384,1536]{1,0:T(8,128)(2,1)}, bf16[2,2,4,48,640]{4,3,2,1,0:T(8,128)(2,1)}, bf16[2,2,4,48,640]{4,3,2,1,0:T(8,128)(2,1)}) custom-call(s32[10]{0:T(128)} %pad_add_fusion.2.refs_0_.order_ref, bf16[384,1536]{1,0:T(8,128)(2,1)} %bitcast.109, bf16[384,1536]{1,0:T(8,128)(2,1)} %get-tuple-element.233.left_ref.refs_2_, ...), custom_call_target="tpu_custom_call" | custom-call | flops 4600000000 | bytes 1024 | tf_op jit(solution)/shard_map/final/pallas_call | solution.py:1226
  723.6 17.5 %collective-permute-done.63 = bf16[2,4,48,1536]{3,2,1,0:T(8,128)(2,1)S(1)} collective-permute-done((bf16[2,4,48,1536]{3,2,1,0:T(8,128)(2,1)S(1)}, bf16[2,4,48,1536]{3,2,1,0:T(8,128)(2,1)S(1)}, u32[]{:S(2)}, u32[]{:S(2)}) %collective-permute-start.63) | collective-permute-done | bytes 1179680 | tf_op jit(solution)/shard_map/ppermute | solution.py:220
  744.3 22.0 %collective-permute-done.64 = bf16[2,4,48,1536]{3,2,1,0:T(8,128)(2,1)S(1)} collective-permute-done((bf16[2,4,48,1536]{3,2,1,0:T(8,128)(2,1)S(1)}, bf16[2,4,48,1536]{3,2,1,0:T(8,128)(2,1)S(1)}, u32[]{:S(2)}, u32[]{:S(2)}) %collective-permute-start.64) | collective-permute-done | bytes 1179680 | tf_op jit(solution)/shard_map/ppermute | solution.py:220
  781.7 21.8 %collective-permute-done.59 = bf16[4,48,640]{2,1,0:T(8,128)(2,1)} collective-permute-done((bf16[4,48,640]{2,1,0:T(8,128)(2,1)}, bf16[4,48,640]{2,1,0:T(8,128)(2,1)}, u32[]{:S(2)}, u32[]{:S(2)}) %collective-permute-start.59) | collective-permute-done | bytes 245792 | tf_op jit(solution)/shard_map/ppermute | solution.py:98
  834.7 24.4 %collective-permute-start.68 = (bf16[48,3072]{1,0:T(8,128)(2,1)S(1)}, bf16[48,3072]{1,0:T(8,128)(2,1)S(1)}, u32[]{:S(2)}, u32[]{:S(2)}) collective-permute-start(bf16[48,3072]{1,0:T(8,128)(2,1)S(1)} %fusion.18), channel_id=1, source_target_pairs={{0,8},{4,12},{8,0},{12,4},{16,24},{20,28},{24,16},{28,20},{1,9},{5... | collective-permute-start | bytes 884744 | tf_op jit(solution)/shard_map/ppermute | solution.py:90
  (387 shorter events, 369.1 us)
Async XLA Ops:
  7.2 132.3 %all-gather.2.cloned.1.call-start = ((), (), s32[]{:S(2)}) async-start(), calls=%async_computation.2 | async-start | bytes 11759616 | tf_op jit(solution)/shard_map/all_gather | solution.py:1292
  10.6 854.1 %reduce-scatter.3.cloned.1.call-start = ((), (), s32[]{:S(2)}) async-start(), calls=%async_computation.3 | async-start | bytes 8847360 | tf_op jit(solution)/shard_map/reduce_scatter | solution.py:1410
  15.2 132.6 %collective-permute-start.13 = (bf16[3,2,384,768]{3,2,1,0:T(8,128)(2,1)S(1)}, bf16[3,2,384,768]{3,2,1,0:T(8,128)(2,1)}, u32[]{:S(2)}, u32[]{:S(2)}) collective-permute-start(bf16[3,2,384,768]{3,2,1,0:T(8,128)(2,1)S(1)} %pad_maximum_fusion.refs_3_.refs_6_.refs_5_), channel_id=1, source_target_pairs={{0,2},{1,3},{2,0},{3,1},{4,6},{5,7},{6,4},{7,5},{8,10},{9,11},{10,... | collective-permute-start | bytes 10616840 | tf_op jit(solution)/shard_map/ppermute | solution.py:220
  30.5 49.3 %collective-permute-start.1 = (bf16[384,1664]{1,0:T(8,128)(2,1)}, bf16[384,1664]{1,0:T(8,128)(2,1)}, u32[]{:S(2)}, u32[]{:S(2)}) collective-permute-start(bf16[384,1664]{1,0:T(8,128)(2,1)} %concatenate.28.refs_1_), channel_id=1, source_target_pairs={{0,8},{4,12},{8,0},{12,4},{16,24},{20,28},{24,16},{28,20},{1,9},{5... | collective-permute-start | bytes 3833864 | tf_op jit(solution)/shard_map/ppermute | solution.py:90
  33.9 45.9 %collective-permute-start = (bf16[384,1664]{1,0:T(8,128)(2,1)}, bf16[384,1664]{1,0:T(8,128)(2,1)}, u32[]{:S(2)}, u32[]{:S(2)}) collective-permute-start(bf16[384,1664]{1,0:T(8,128)(2,1)} %concatenate.28.refs_1_), channel_id=1, source_target_pairs={{0,4},{4,0},{8,12},{12,8},{16,20},{20,16},{24,28},{28,24},{1,5},{5... | collective-permute-start | bytes 3833864 | tf_op jit(solution)/shard_map/ppermute | solution.py:98
  35.4 184.8 %collective-permute-start.12 = (bf16[3,2,384,768]{3,2,1,0:T(8,128)(2,1)S(1)}, bf16[3,2,384,768]{3,2,1,0:T(8,128)(2,1)}, u32[]{:S(2)}, u32[]{:S(2)}) collective-permute-start(bf16[3,2,384,768]{3,2,1,0:T(8,128)(2,1)S(1)} %pad_maximum_fusion.refs_3_.refs_6_.refs_5_), channel_id=1, source_target_pairs={{0,1},{1,0},{2,3},{3,2},{4,5},{5,4},{6,7},{7,6},{8,9},{9,8},{10,11... | collective-permute-start | bytes 10616840 | tf_op jit(solution)/shard_map/ppermute | solution.py:220
  147.9 72.4 %collective-permute-start.14 = (bf16[3,2,384,768]{3,2,1,0:T(8,128)(2,1)}, bf16[3,2,384,768]{3,2,1,0:T(8,128)(2,1)}, u32[]{:S(2)}, u32[]{:S(2)}) collective-permute-start(bf16[3,2,384,768]{3,2,1,0:T(8,128)(2,1)} %hold.30.refs_5_.refs_8_.refs_7_), channel_id=1, source_target_pairs={{0,1},{1,0},{2,3},{3,2},{4,5},{5,4},{6,7},{7,6},{8,9},{9,8},{10,11... | collective-permute-start | bytes 10616840 | tf_op jit(solution)/shard_map/ppermute | solution.py:220
  218.0 73.9 %collective-permute-start.21 = (bf16[384,1664]{1,0:T(8,128)(2,1)}, bf16[384,1664]{1,0:T(8,128)(2,1)S(1)}, u32[]{:S(2)}, u32[]{:S(2)}) collective-permute-start(bf16[384,1664]{1,0:T(8,128)(2,1)} %get-tuple-element.147.refs_1_), channel_id=1, source_target_pairs={{0,4},{4,0},{8,12},{12,8},{16,20},{20,16},{24,28},{28,24},{1,5},{5... | collective-permute-start | bytes 3833864 | tf_op jit(solution)/shard_map/ppermute | solution.py:98
  218.5 92.6 %collective-permute-start.23 = (bf16[384,1664]{1,0:T(8,128)(2,1)}, bf16[384,1664]{1,0:T(8,128)(2,1)}, u32[]{:S(2)}, u32[]{:S(2)}) collective-permute-start(bf16[384,1664]{1,0:T(8,128)(2,1)} %get-tuple-element.158), channel_id=1, source_target_pairs={{8,0},{12,4},{16,24},{20,28},{9,1},{13,5},{17,25},{21,29},{10,2},{... | collective-permute-start | bytes 3833864 | tf_op jit(solution)/shard_map/ppermute | solution.py:90
  313.1 52.6 %collective-permute-start.24 = (bf16[384,1664]{1,0:T(8,128)(2,1)S(1)}, bf16[384,1664]{1,0:T(8,128)(2,1)}, u32[]{:S(2)}, u32[]{:S(2)}) collective-permute-start(bf16[384,1664]{1,0:T(8,128)(2,1)S(1)} %add.226.refs_1_), channel_id=1, source_target_pairs={{0,4},{4,0},{8,12},{12,8},{16,20},{20,16},{24,28},{28,24},{1,5},{5... | collective-permute-start | bytes 3833864 | tf_op jit(solution)/shard_map/ppermute | solution.py:98
  341.2 49.7 %collective-permute-start.27 = (bf16[384,1536]{1,0:T(8,128)(2,1)S(1)}, bf16[384,1536]{1,0:T(8,128)(2,1)S(1)}, u32[]{:S(2)}, u32[]{:S(2)}) collective-permute-start(bf16[384,1536]{1,0:T(8,128)(2,1)S(1)} %add.227.refs_1_), channel_id=1, source_target_pairs={{0,4},{4,0},{8,12},{12,8},{16,20},{20,16},{24,28},{28,24},{1,5},{5... | collective-permute-start | bytes 3538952 | tf_op jit(solution)/shard_map/ppermute | solution.py:98
  341.8 49.1 %collective-permute-start.28 = (bf16[384,1536]{1,0:T(8,128)(2,1)S(1)}, bf16[384,1536]{1,0:T(8,128)(2,1)S(1)}, u32[]{:S(2)}, u32[]{:S(2)}) collective-permute-start(bf16[384,1536]{1,0:T(8,128)(2,1)S(1)} %copy-done.29), channel_id=1, source_target_pairs={{8,0},{12,4},{16,24},{20,28},{9,1},{13,5},{17,25},{21,29},{10,2},{... | collective-permute-start | bytes 3538952 | tf_op jit(solution)/shard_map/ppermute | solution.py:90
  446.7 418.0 %reduce-scatter.5.cloned.1.call-start = ((), (), s32[]{:S(2)}) async-start(), calls=%async_computation.4 | async-start | bytes 8847360 | tf_op jit(solution)/shard_map/reduce_scatter | solution.py:1410
  448.3 52.9 %collective-permute-start.32 = (bf16[384,1536]{1,0:T(8,128)(2,1)}, bf16[384,1536]{1,0:T(8,128)(2,1)S(1)}, u32[]{:S(2)}, u32[]{:S(2)}) collective-permute-start(bf16[384,1536]{1,0:T(8,128)(2,1)} %get-tuple-element.193), channel_id=1, source_target_pairs={{0,4},{4,0},{8,12},{12,8},{16,20},{20,16},{24,28},{28,24},{1,5},{5... | collective-permute-start | bytes 3538952 | tf_op jit(solution)/shard_map/ppermute | solution.py:98
  481.0 53.2 %collective-permute-start.35 = (bf16[384,1536]{1,0:T(8,128)(2,1)}, bf16[384,1536]{1,0:T(8,128)(2,1)}, u32[]{:S(2)}, u32[]{:S(2)}) collective-permute-start(bf16[384,1536]{1,0:T(8,128)(2,1)} %get-tuple-element.199), channel_id=1, source_target_pairs={{0,4},{4,0},{8,12},{12,8},{16,20},{20,16},{24,28},{28,24},{1,5},{5... | collective-permute-start | bytes 3538952 | tf_op jit(solution)/shard_map/ppermute | solution.py:98
  513.7 52.0 %collective-permute-start.39 = (bf16[384,1536]{1,0:T(8,128)(2,1)}, bf16[384,1536]{1,0:T(8,128)(2,1)}, u32[]{:S(2)}, u32[]{:S(2)}) collective-permute-start(bf16[384,1536]{1,0:T(8,128)(2,1)} %get-tuple-element.209), channel_id=1, source_target_pairs={{0,4},{4,0},{8,12},{12,8},{16,20},{20,16},{24,28},{28,24},{1,5},{5... | collective-permute-start | bytes 3538952 | tf_op jit(solution)/shard_map/ppermute | solution.py:98
  565.1 39.1 %collective-permute-start.36 = (bf16[2,384,1536]{2,1,0:T(8,128)(2,1)}, bf16[2,384,1536]{2,1,0:T(8,128)(2,1)S(1)}, u32[]{:S(2)}, u32[]{:S(2)}) collective-permute-start(bf16[2,384,1536]{2,1,0:T(8,128)(2,1)} %get-tuple-element.207), channel_id=1, source_target_pairs={{0,4},{4,0},{8,12},{12,8},{16,20},{20,16},{24,28},{28,24},{1,5},{5... | collective-permute-start | bytes 7077896 | tf_op jit(solution)/shard_map/ppermute | solution.py:98
  646.2 47.7 %collective-permute-start.54 = (bf16[2,2,4,48,1536]{4,3,2,1,0:T(8,128)(2,1)}, bf16[2,2,4,48,1536]{4,3,2,1,0:T(8,128)(2,1)S(1)}, u32[]{:S(2)}, u32[]{:S(2)}) collective-permute-start(bf16[2,2,4,48,1536]{4,3,2,1,0:T(8,128)(2,1)} %get-tuple-element.243), channel_id=1, source_target_pairs={{0,1},{1,0},{2,3},{3,2},{4,5},{5,4},{6,7},{7,6},{8,9},{9,8},{10,11... | collective-permute-start | bytes 7077896 | tf_op jit(solution)/shard_map/ppermute | solution.py:220
  654.0 41.7 %collective-permute-start.55 = (bf16[2,2,4,48,1536]{4,3,2,1,0:T(8,128)(2,1)}, bf16[2,2,4,48,1536]{4,3,2,1,0:T(8,128)(2,1)S(1)}, u32[]{:S(2)}, u32[]{:S(2)}) collective-permute-start(bf16[2,2,4,48,1536]{4,3,2,1,0:T(8,128)(2,1)} %get-tuple-element.245), channel_id=1, source_target_pairs={{0,1},{1,0},{2,3},{3,2},{4,5},{5,4},{6,7},{7,6},{8,9},{9,8},{10,11... | collective-permute-start | bytes 7077896 | tf_op jit(solution)/shard_map/ppermute | solution.py:220
  713.7 52.6 %collective-permute-start.64 = (bf16[2,4,48,1536]{3,2,1,0:T(8,128)(2,1)S(1)}, bf16[2,4,48,1536]{3,2,1,0:T(8,128)(2,1)S(1)}, u32[]{:S(2)}, u32[]{:S(2)}) collective-permute-start(bf16[2,4,48,1536]{3,2,1,0:T(8,128)(2,1)S(1)} %copy-done.17), channel_id=1, source_target_pairs={{0,2},{1,3},{2,0},{3,1},{4,6},{5,7},{6,4},{7,5},{8,10},{9,11},{10,... | collective-permute-start | bytes 3538952 | tf_op jit(solution)/shard_map/ppermute | solution.py:220
  714.3 64.6 %collective-permute-start.42 = (bf16[2,384,1536]{2,1,0:T(8,128)(2,1)S(1)}, bf16[2,384,1536]{2,1,0:T(8,128)(2,1)}, u32[]{:S(2)}, u32[]{:S(2)}) collective-permute-start(bf16[2,384,1536]{2,1,0:T(8,128)(2,1)S(1)} %copy-done.11), channel_id=1, source_target_pairs={{0,4},{4,0},{8,12},{12,8},{16,20},{20,16},{24,28},{28,24},{1,5},{5... | collective-permute-start | bytes 7077896 | tf_op jit(solution)/shard_map/ppermute | solution.py:98
  714.7 64.1 %collective-permute-start.41 = (bf16[384,1536]{1,0:T(8,128)(2,1)S(1)}, bf16[384,1536]{1,0:T(8,128)(2,1)}, u32[]{:S(2)}, u32[]{:S(2)}) collective-permute-start(bf16[384,1536]{1,0:T(8,128)(2,1)S(1)} %copy-done.26), channel_id=1, source_target_pairs={{0,8},{4,12},{24,16},{28,20},{1,9},{5,13},{25,17},{29,21},{2,10},{... | collective-permute-start | bytes 3538952 | tf_op jit(solution)/shard_map/ppermute | solution.py:90
  719.4 59.5 %collective-permute-start.40 = (bf16[384,1536]{1,0:T(8,128)(2,1)}, bf16[384,1536]{1,0:T(8,128)(2,1)}, u32[]{:S(2)}, u32[]{:S(2)}) collective-permute-start(bf16[384,1536]{1,0:T(8,128)(2,1)} %get-tuple-element.299), channel_id=1, source_target_pairs={{0,8},{4,12},{24,16},{28,20},{1,9},{5,13},{25,17},{29,21},{2,10},{... | collective-permute-start | bytes 3538952 | tf_op jit(solution)/shard_map/ppermute | solution.py:90
  817.2 41.9 %collective-permute-start.48 = (bf16[384,1536]{1,0:T(8,128)(2,1)}, bf16[384,1536]{1,0:T(8,128)(2,1)}, u32[]{:S(2)}, u32[]{:S(2)}) collective-permute-start(bf16[384,1536]{1,0:T(8,128)(2,1)} %add.242), channel_id=1, source_target_pairs={{8,16},{12,20},{16,8},{20,12},{9,17},{13,21},{17,9},{21,13},{10,18... | collective-permute-start | bytes 3538952 | tf_op jit(solution)/shard_map/ppermute | solution.py:90
  (118 other events, 1580.0 us)
Sparse Core Ops, SparseCore 0:
  11.5 127.9 all-gather.1
  446.8 63.5 reduce-scatter.2
  646.4 63.7 reduce-scatter.4

commit v3 on v2

--- a/solution.py
+++ b/solution.py
@@ -111,7 +111,7 @@
         ]
         return [(rows[2 * step], rows[2 * step + 1]) for step in range(self.length)]
 
-    def gather(self, array, late=()):
+    def gather(self, array):
         if self.length != 4:
             yield
             for couple in self.spread(array):
@@ -132,23 +132,22 @@
         until = yield (array, swapped)
         outward, cross_two = hold([outward, cross_two], until, swapped_first)
         second = cross + outward
-        if late:
-            cross_two, second = hold([cross_two, second], late[0])
+        swapped_first = hold([swapped_first], second)[0]
+        until = yield (first, swapped_first)
+        cross_two, second = hold([cross_two, second], until)
         outward_two = self.move(cross_two, ends)
         swapped_second = self.swap(second)
-        until = yield (first, swapped_first)
+        until = yield (second, swapped_second)
         outward_two = hold([outward_two], until, swapped_second)[0]
         third = cross_two + outward_two
-        swapped_third = self.swap(third)
-        yield (second, swapped_second)
-        yield (third, swapped_third)
+        yield (third, self.swap(third))
 
     def gather_now(self, array):
         run = self.gather(array)
         next(run)
         return [run.send(None) for _ in range(self.length)]
 
-    def scatter(self, parts):
+    def scatter(self, parts, chained=False):
         if self.length != 4:
             order = self.sources()
             rows = jnp.stack([part for couple in parts for part in couple])
@@ -161,52 +160,57 @@
         inward = [(0, 1), (3, 2)]
         middle = [(1, 2), (2, 1)]
         couples = [(0, 1), (1, 0), (2, 3), (3, 2)]
-        swapped = [self.swap(part[1]) for part in parts]
+
+        others = [part[1] for part in parts]
+        if chained:
+            others[:3] = hold(others[:3], others[3])
+        swapped = [self.swap(other) for other in others]
         until = yield parts[3][1]
-        third = parts[3][0] + hold([swapped[3]], until)[0]
+        arrived = hold([swapped[3]], until)[0]
+        third = parts[3][0] + arrived
         from_end = self.move(third, inward)
+        arrived = swapped[2]
         until = yield third
-        from_end, arrived = hold([from_end, swapped[2]], until)
+        from_end, arrived = hold([from_end, arrived], until)
         sent = third + from_end
         crossed = self.move(sent, middle)
         second = parts[2][0] + arrived
         from_end_two = self.move(second, inward)
+        arrived = swapped[1]
         until = yield second
-        crossed, from_end_two, arrived = hold([crossed, from_end_two, swapped[1]], until)
+        crossed, from_end_two, arrived = hold([crossed, from_end_two, arrived], until)
         sent = parts[1][0] + arrived + crossed
         last = self.move(sent, couples)
         crossed_two = self.move(second + from_end_two, middle)
+        arrived = swapped[0]
         until = yield sent
-        last, crossed_two, arrived = hold([last, crossed_two, swapped[0]], until)
+        last, crossed_two, arrived = hold([last, crossed_two, arrived], until)
         yield [parts[0][0], arrived, crossed_two, last]
 
-    def scatter_pairs(self, parts, pairs):
+    def scatter_late(self, parts, others):
         if self.length != 4:
-            flat = [pair[place] for pair in pairs for place in range(self.length // 2)]
+            flat = [other[place] for other in others for place in range(other.shape[0])]
             yield from self.scatter(list(zip(parts, reversed(flat))))
             return
         inward = [(0, 1), (3, 2)]
         middle = [(1, 2), (2, 1)]
         couples = [(0, 1), (1, 0), (2, 3), (3, 2)]
-        swapped = [self.swap(pair) for pair in pairs]
-        until = yield pairs[0]
-        arrived = hold([swapped[0]], until)[0]
-        third = parts[3] + arrived[0]
-        second = parts[2] + arrived[1]
+        swapped = [self.swap(other) for other in others]
+        until = yield others[0]
+        third = parts[3] + hold([swapped[0]], until)[0][0]
         from_end = self.move(third, inward)
+        until = yield third
+        from_end, *swapped = hold([from_end, *swapped[1:]], until)
+        until = yield from_end
+        third, *swapped = hold([third, *swapped], until)
+        crossed = self.move(third + from_end, middle)
+        second = parts[2] + swapped[0][0]
         from_end_two = self.move(second, inward)
         until = yield second
-        from_end, from_end_two, arrived = hold([from_end, from_end_two, swapped[1]], until)
-        crossed = self.move(third + from_end, middle)
-        sent = second + from_end_two
-        crossed_two = self.move(sent, middle)
-        until = yield sent
-        crossed = hold([crossed], until)[0]
-        sent = parts[1] + arrived[0] + crossed
-        last = self.move(sent, couples)
-        until = yield sent
-        last, crossed_two = hold([last, crossed_two], until)
-        yield [parts[0], arrived[1], crossed_two, last]
+        crossed, from_end_two = hold([crossed, from_end_two], until)
+        last = self.move(parts[1] + swapped[1][0] + crossed, couples)
+        crossed_two = self.move(second + from_end_two, middle)
+        yield [parts[0], swapped[1][1], crossed_two, last]
 
     def scatter_now(self, parts):
         run = self.scatter(parts)
@@ -1324,15 +1328,14 @@
         [me[None], (start[0] // tokens)[None], ends[: HEADER - 2], sources]
     )
 
-    late = []
-    run = ring.gather(info, late)
+    run = ring.gather(info)
     next(run)
-    grads = [run.send(None)]
+    grads = [run.send(None), run.send(None)]
     q, kv, low_one, gains = qkv_call(
-        x, w_full, cosine, sine, [grads[0][1]] if layout else []
+        x, w_full, cosine, sine, [grads[1][1]] if layout else []
     )
     shards = gather_shards(
-        jnp.stack([w_gate, w_up, jnp.swapaxes(w_down, 1, 2)]), shards_of, kv
+        jnp.stack([w_gate, w_up, jnp.swapaxes(w_down, 1, 2)]), shards_of, grads[1][1]
     )
     kv_couples = ring.gather_now(kv)
     kv_slots = [part for couple in kv_couples for part in couple]
@@ -1343,12 +1346,13 @@
         routed.append(route_call(places, grads[step], shards, capacity, width, after))
         return routed[-1][4]
 
-    late.append(kv_couples[3][0])
-    grads.append(run.send(None))
+    grads.append(run.send(kv_couples[3][1]))
     state = attn_call(order, q, kv_slots[:half], 0, False, after=[route(0)])
-    attended, log_total = attn_call(order, q, kv_slots[half:], half, True, state)
-    attn_rows, low_two = out_call(x, attended, w_full, gains)
-    grads += [run.send(None) for _ in range(2, half)]
+    grads += [run.send(state[1]) for _ in range(3, half)]
+    attended, log_total = attn_call(
+        order, q, kv_slots[half:], half, True, state, [grads[3][0]]
+    )
+    attn_rows, low_two = out_call(x, attended, w_full, gains, [grads[3][1]])
 
     def run_experts(step, couple, after):
         pick0, pick1, _, _, grad_hidden = routed[step]
@@ -1365,18 +1369,20 @@
     couple = rows_run.send(mark)
     mark = run_experts(0, couple, [mark])
     couple = rows_run.send(mark)
+    mark = run_experts(1, couple, [mark])
     for step in range(3, half):
-        mark = route(step, [couple[1]])
-    mark = run_experts(1, couple, [mark])
+        mark = route(step, [mark])
+    couple = rows_run.send(None)
+    couples = [couple] + [rows_run.send(mark) for _ in range(3, half)]
     for step in range(2, half):
-        couple = rows_run.send(mark)
-        mark = run_experts(step, couple, [mark])
+        mark = run_experts(step, couples[step - 2], [mark, couples[1][0]])
 
     y_pairs = []
 
     def down(step, after):
         pick0, pick1, gate_rows = routed[step][:3]
-        place = (half - 1 - step) % (half // 2)
+        packed = step < half // 2
+        place = half // 2 - 1 - step if packed else 0
         out, pair = down_call(
             places,
             made[step][1],
@@ -1387,13 +1393,13 @@
             width,
             place,
             y_pairs.pop() if place else None,
-            half // 2,
+            half // 2 if packed else 1,
             after,
         )
         y_pairs.append(pair)
         return out
 
-    grad_run = ring.scatter(parts)
+    grad_run = ring.scatter(parts, True)
     grad_mark = next(grad_run)
     expert_grads = []
     for expert in range(exp_dev):
@@ -1406,13 +1412,14 @@
             [entry[1] for entry in made],
             [mark, grad_mark],
         )
-        expert_grads.append(
-            lax.psum_scatter(made_grad, "fsdp", scatter_dimension=1, tiled=True).astype(F32)
-        )
         mark = made_grad
         if expert < 2:
             grad_mark = grad_run.send(mark)
-    expert_grads = jnp.stack(expert_grads, 1)
+        expert_grads.append(
+            lax.psum_scatter(
+                hold([made_grad], grad_mark)[0], "fsdp", scatter_dimension=1, tiled=True
+            )
+        )
     y_parts = [None] * len(made)
     for step in reversed(range(len(made))):
         y_parts[step] = down(step, [mark, grad_mark])
@@ -1420,7 +1427,7 @@
         if step == len(made) // 2:
             grad_mark = grad_run.send(mark)
     grad_parts = grad_run.send(mark)
-    y_run = ring.scatter_pairs(y_parts, hold(y_pairs, grad_mark))
+    y_run = ring.scatter_late(y_parts, hold(y_pairs, grad_mark))
     next(y_run)
 
     resid, grad_attn, grad_out, delta, moe_part = resid_back_call(
@@ -1442,23 +1449,29 @@
         sine,
         kv_slots,
         back[1:],
-        [mark],
+        [mark] + expert_grads,
     )
     d_q.append(back[0])
-    kv_terms = ring.scatter_now(
-        [(back[1 + 2 * step], back[2 + 2 * step]) for step in range(half)]
-    )
+    expert_grads = jnp.stack(expert_grads, 1).astype(F32)
+    d_q = jnp.concatenate(d_q, 1)
+    waits = [y_run.send(back[0])]
+    if layout:
+        wo_part = cross_call(places, hold([grad_attn], back[0])[0], attended, *layout, "wo_grad")
+        wq_part = cross_call(places, low_one, d_q, *layout, "wq_grad")
+        waits += [wo_part[0], wq_part[0]]
+    kv_parts = hold(back[1:], *waits)
+    kv_run = ring.scatter([(kv_parts[2 * step], kv_parts[2 * step + 1]) for step in range(half)])
+    next(kv_run)
+    for _ in range(4):
+        kv_terms = kv_run.send(None)
     y_run.send(kv_terms[-1])
 
-    d_q = jnp.concatenate(d_q, 1)
     grad_q = input_q_call(d_q, w_full)
     after = []
     if layout:
-        wq_part = cross_call(places, low_one, d_q, *layout, "wq_grad")
-        wo_part = cross_call(places, hold([grad_attn], d_q)[0], attended, *layout, "wo_grad")
         wo_terms, wo_sent = scatter_all_across(*wo_part, shards_of)
         wq_terms, wq_sent = scatter_all_across(*wq_part, shards_of)
-        after = [wo_sent, wq_sent]
+        after = [wo_terms, wq_sent]
     else:
         wq_grad, wo_grad = [
             lax.psum_scatter(
@@ -1485,19 +1498,14 @@
         after,
     )
     if layout:
-        terms = jnp.concatenate([wo_terms, wq_terms], -1)
-        first_run = scatter_all_along(hold([terms], kv_terms[-1])[0], ring)
-        next(first_run)
-        tail, tail_sent = scatter_all_across(*tail, shards_of)
-        y_run.send(tail_sent)
-        last_run = scatter_all_along(tail, ring)
-        next(last_run)
+        wo_terms = hold([wo_terms], kv_terms[-1])[0]
+        tail, _ = scatter_all_across(*tail, shards_of)
+        runs = [scatter_all_along(terms, ring) for terms in (wo_terms, wq_terms, tail)]
+        for one in runs:
+            next(one)
         for _ in range(4):
-            terms = first_run.send(None)
-            tail = last_run.send(None)
-        wo_grad, wq_grad = terms[:, :HQ], terms[:, HQ:]
+            wo_grad, wq_grad, tail = [one.send(None) for one in runs]
     else:
-        y_run.send(None)
         tail = lax.psum_scatter(tail[0], both, scatter_dimension=0, tiled=True).astype(F32)
     y_terms = y_run.send(None)
     moe = y_terms[0].astype(F32)

time: 886 us -> 790 us (0.89)
  waiting for transfers between devices: 297 us -> 205 us
  starting transfers between devices: 136 us -> 123 us
    all_gather x1, waiting for transfers between devices: 59.6 us -> 0.01 us  [local(): lax.all_gather(jnp.concatenate([wq, wk, wv, wo.T, gains_part], 1), both,...]
    ppermute x9, waiting for transfers between devices: 44.8 us -> 12 us  [neighbour(): return lax.ppermute(array, 'fsdp', pairs)]
    ppermute x24 -> x26, waiting for transfers between devices: 110 us -> 136 us  [swap(): return lax.ppermute(array, 'ctx', pairs)]
    ppermute x36 -> x39, waiting for transfers between devices: 82 us -> 56.8 us  [move(): return lax.ppermute(array, 'ctx', pairs)]
    ppermute x36 -> x39, starting transfers between devices: 107 us -> 90.1 us  [move(): return lax.ppermute(array, 'ctx', pairs)]
    unnamed x145 -> x119, local copies, waits for them, and re-layouts: 29 us -> 38.4 us
    ppermute x24 -> x26, starting transfers between devices: 20.8 us -> 26.8 us  [swap(): return lax.ppermute(array, 'ctx', pairs)]
  transfers between devices with their start and end apart: 72 -> 77, of which waited for: 26 -> 28; matrix products, arithmetic and copies ran while one was open for 9% -> 11% of each run, Pallas kernels for 33% -> 38%
where the time goes in v3:
time: 790 us; the launch traced here: 782 us
  Pallas kernels  320 us (41%)
  waiting for transfers between devices  205 us (26%)
  starting transfers between devices  123 us (16%)
  other arithmetic  62.6 us (8%)
  local copies, waits for them, and re-layouts  53.6 us (7%)
  between operations  17.2 us (2%)
    ppermute x26, waiting for transfers between devices, swap(): return lax.ppermute(array, 'ctx', pairs)  136 us
    ppermute x39, starting transfers between devices, move(): return lax.ppermute(array, 'ctx', pairs)  90.1 us
    pallas_call x4, Pallas kernels, expert_call(): pl.pallas_call(without(lambda *refs: expert_kernel(len(shards), capacity,...  67.1 us
    ppermute x39, waiting for transfers between devices, move(): return lax.ppermute(array, 'ctx', pairs)  56.8 us
    pallas_call x2, Pallas kernels, attn_back_call(): pl.pallas_call(without(lambda *refs: attn_back_kernel(count, group, *refs...  52.6 us
    pallas_call x4, Pallas kernels, down_call(): pl.pallas_call(lambda *refs: down_kernel(len(shards), capacity, place, *r...  40.1 us
    unnamed x119, local copies, waits for them, and re-layouts  38.4 us
    pallas_call x2, Pallas kernels, attn_call(): pl.pallas_call(without(lambda *refs: attn_kernel(count, base, last, *refs...  36 us
  transfers between devices with their start and end apart: 77, of which 28 were waited for; matrix products, arithmetic and copies ran while one was open for 11% of the time, Pallas kernels for 38%

profile of v3, /device:TPU:0, one launch (start us, length us, event | category | flops | bytes accessed | tf_op | source)
XLA Modules:
  0.0 782.0 jit_solution(5696081066369081122)
XLA Ops:
  35.4 33.4 %collective-permute-done.2.refs_2_.refs_0_ = bf16[384,1664]{1,0:T(8,128)(2,1)} collective-permute-done((bf16[384,1664]{1,0:T(8,128)(2,1)}, bf16[384,1664]{1,0:T(8,128)(2,1)}, u32[]{:S(2)}, u32[]{:S(2)}) %collective-permute-start.2) | collective-permute-done | bytes 1277984 | tf_op jit(solution)/shard_map/ppermute | solution.py:98
  68.8 11.2 %collective-permute-done.refs_0_ = bf16[384,1664]{1,0:T(8,128)(2,1)} collective-permute-done((bf16[384,1664]{1,0:T(8,128)(2,1)}, bf16[384,1664]{1,0:T(8,128)(2,1)}, u32[]{:S(2)}, u32[]{:S(2)}) %collective-permute-start) | collective-permute-done | bytes 1277984 | tf_op jit(solution)/shard_map/ppermute | solution.py:90
  84.6 47.2 %collective-permute-done.3.refs_2_.refs_0_ = bf16[384,1664]{1,0:T(8,128)(2,1)} collective-permute-done((bf16[384,1664]{1,0:T(8,128)(2,1)}, bf16[384,1664]{1,0:T(8,128)(2,1)}, u32[]{:S(2)}, u32[]{:S(2)}) %collective-permute-start.3) | collective-permute-done | bytes 1277984 | tf_op jit(solution)/shard_map/ppermute | solution.py:98
  131.7 12.2 %collective-permute-done.4.refs_0_ = bf16[384,1664]{1,0:T(8,128)(2,1)} collective-permute-done((bf16[384,1664]{1,0:T(8,128)(2,1)}, bf16[384,1664]{1,0:T(8,128)(2,1)}, u32[]{:S(2)}, u32[]{:S(2)}) %collective-permute-start.4) | collective-permute-done | bytes 1277984 | tf_op jit(solution)/shard_map/ppermute | solution.py:90
  175.4 8.9 %collective-permute-done.9.refs_0_ = bf16[384,512]{1,0:T(8,128)(2,1)} collective-permute-done((bf16[384,512]{1,0:T(8,128)(2,1)}, bf16[384,512]{1,0:T(8,128)(2,1)}, u32[]{:S(2)}, u32[]{:S(2)}) %collective-permute-start.9) | collective-permute-done | bytes 393248 | tf_op jit(solution)/shard_map/ppermute | solution.py:90
  221.7 17.6 %attention.2 = (f32[6,128,768]{2,1,0:T(8,128)}, f32[6,8,768]{2,1,0:T(8,128)}) custom-call(s32[13]{0:T(128)} %pad_add_fusion.1.refs_0_, bf16[384,1536]{1,0:T(8,128)(2,1)} %get-tuple-element.148.refs_1_, bf16[384,512]{1,0:T(8,128)(2,1)} %get-tuple-element.149.refs_2_.refs_7_, bf16[384,512]{1,0:T(8,128)(2,1)} %hold.37.refs_3_.refs_8_, ...), custom_call_target="tpu_custom_call" | custom-call | flops 8280000000 | bytes 1024 | tf_op jit(solution)/shard_map/attention/pallas_call | solution.py:491
  243.0 18.3 %attention.3 = (bf16[384,1536]{1,0:T(8,128)(2,1)}, f32[6,8,384]{2,1,0:T(8,128)}) custom-call(s32[13]{0:T(128)} %pad_add_fusion.1.refs_0_, bf16[384,1536]{1,0:T(8,128)(2,1)} %get-tuple-element.148.refs_1_, bf16[384,512]{1,0:T(8,128)(2,1)} %add.246.refs_1_.refs_2_.refs_11_, bf16[384,512]{1,0:T(8,128)(2,1)} %collective-permute-done.12.refs_1_.refs_3_.refs_12_, ...), custom_call_target="tpu_custom_call" | custom-call | flops 8280000000 | bytes 1024 | tf_op jit(solution)/shard_map/attention/pallas_call | solution.py:491
  267.3 8.8 %attention_out.1 = (bf16[384,1536]{1,0:T(8,128)(2,1)}, bf16[384,1536]{1,0:T(8,128)(2,1)}) custom-call(bf16[384,1536]{1,0:T(8,128)(2,1)} %bitcast.115, bf16[384,1536]{1,0:T(8,128)(2,1)} %get-tuple-element.160.refs_1_.refs_4_.right_ref, bf16[1536,3712]{1,0:T(8,128)(2,1)} %all-gather.2.cloned.1.call-done.refs_1_.refs_2_.refs_3_.refs_4_.refs_5_.refs_6_.refs_7_.w_ref, ...), custom_call_target="tpu_custom_call" | custom-call | flops 4140000000 | bytes 1024 | tf_op jit(solution)/shard_map/attention_out/pallas_call | solution.py:646
  292.6 8.4 %route.6 = (bf16[2,144,384]{2,1,0:T(8,128)(2,1)}, bf16[2,144,384]{2,1,0:T(8,128)(2,1)}, f32[2,288,128]{2,1,0:T(8,128)}, bf16[2,288,1536]{2,1,0:T(8,128)(2,1)}, f32[2,288,768]{2,1,0:T(8,128)}) custom-call(s32[10]{0:T(128)} %pad_add_fusion.2.refs_0_.order_ref, bf16[384,1664]{1,0:T(8,128)(2,1)} %get-tuple-element.159.refs_1_, ...), custom_call_target="tpu_custom_call" | custom-call | flops 3910000128 | bytes 1024 | tf_op jit(solution)/shard_map/route/pallas_call | solution.py:755
  310.3 16.7 %experts.4 = (bf16[2,288,1536]{2,1,0:T(8,128)(2,1)}, bf16[2,288,768]{2,1,0:T(8,128)(2,1)}, bf16[2,288,768]{2,1,0:T(8,128)(2,1)}, bf16[2,288,768]{2,1,0:T(8,128)(...) custom-call(s32[10]{0:T(128)} %pad_add_fusion.2.refs_0_.order_ref, ...), custom_call_target="tpu_custom_call" | custom-call | flops 7820000256 | bytes 1024 | tf_op jit(solution)/shard_map/experts/pallas_call | solution.py:841
  337.9 16.8 %experts.5 = (bf16[2,288,1536]{2,1,0:T(8,128)(2,1)}, bf16[2,288,768]{2,1,0:T(8,128)(2,1)}, bf16[2,288,768]{2,1,0:T(8,128)(2,1)}, bf16[2,288,768]{2,1,0:T(8,128)(...) custom-call(s32[10]{0:T(128)} %pad_add_fusion.2.refs_0_.order_ref, ...), custom_call_target="tpu_custom_call" | custom-call | flops 7820000256 | bytes 1024 | tf_op jit(solution)/shard_map/experts/pallas_call | solution.py:841
  366.8 16.7 %experts.6 = (bf16[2,288,1536]{2,1,0:T(8,128)(2,1)}, bf16[2,288,768]{2,1,0:T(8,128)(2,1)}, bf16[2,288,768]{2,1,0:T(8,128)(2,1)}, bf16[2,288,768]{2,1,0:T(8,128)(...) custom-call(s32[10]{0:T(128)} %pad_add_fusion.2.refs_0_.order_ref, bf16[384,1536]{1,0:T(8,128)(2,1)} %copy-done.27, ...), custom_call_target="tpu_custom_call" | custom-call | flops 7820000256 | bytes 1024 | tf_op jit(solution)/shard_map/experts/pallas_call | solution.py:841
  384.6 16.9 %experts.7 = (bf16[2,288,1536]{2,1,0:T(8,128)(2,1)}, bf16[2,288,768]{2,1,0:T(8,128)(2,1)}, bf16[2,288,768]{2,1,0:T(8,128)(2,1)}, bf16[2,288,768]{2,1,0:T(8,128)(...) custom-call(s32[10]{0:T(128)} %pad_add_fusion.2.refs_0_.order_ref, bf16[384,1536]{1,0:T(8,128)(2,1)} %copy-done.45, ...), custom_call_target="tpu_custom_call" | custom-call | flops 7820000256 | bytes 1024 | tf_op jit(solution)/shard_map/experts/pallas_call | solution.py:841
  402.6 15.4 %expert_weight_grads.2.refs_1_.refs_20_ = bf16[3,1536,768]{2,1,0:T(8,128)(2,1)} custom-call(bf16[2,288,1536]{2,1,0:T(8,128)(2,1)} %get-tuple-element.190.refs_0_, bf16[2,288,1536]{2,1,0:T(8,128)(2,1)} %get-tuple-element.191.refs_1_, bf16[2,288,1536]{2,1,0:T(8,128)(2,1)} %get-tuple-element.192.refs_2_, bf16[2,288,1536]{2,1,0:T(8,128)(2,1)} %get-tuple-element.193.refs_3_, ...), custom_call_target="tpu_custom_call" | custom-call | flops 8280000000 | bytes 1024 | tf_op jit(solution)/shard_map/expert_weight_grads/pallas_call | solution.py:949
  435.2 16.4 %expert_weight_grads.3.refs_2_.refs_9_ = bf16[3,1536,768]{2,1,0:T(8,128)(2,1)} custom-call(bf16[2,288,1536]{2,1,0:T(8,128)(2,1)} %get-tuple-element.190.refs_0_, bf16[2,288,1536]{2,1,0:T(8,128)(2,1)} %get-tuple-element.191.refs_1_, bf16[2,288,1536]{2,1,0:T(8,128)(2,1)} %get-tuple-element.192.refs_2_, bf16[2,288,1536]{2,1,0:T(8,128)(2,1)} %get-tuple-element.193.refs_3_, ...), custom_call_target="tpu_custom_call" | custom-call | flops 8280000000 | bytes 1024 | tf_op jit(solution)/shard_map/expert_weight_grads/pallas_call | solution.py:949
  471.8 10.0 %experts_down.4 = (bf16[384,1536]{1,0:T(8,128)(2,1)}, bf16[1,384,1536]{2,1,0:T(8,128)(2,1)}) custom-call(s32[10]{0:T(128)} %pad_add_fusion.2.refs_0_.order_ref, bf16[2,288,768]{2,1,0:T(8,128)(2,1)} %get-tuple-element.188.refs_19_.refs_1_, f32[2,288,128]{2,1,0:T(8,128)} %get-tuple-element.189.refs_2_, bf16[2,144,384]{2,1,0:T(8,128)(2,1)} %get-tuple-element.185.refs_3_, ...), custom_call_target="tpu_custom_call" | custom-call | flops 4278000128 | bytes 1024 | tf_op jit(solution)/shard_map/experts_down/pallas_call | solution.py:912
  481.9 9.8 %experts_down.5 = (bf16[384,1536]{1,0:T(8,128)(2,1)}, bf16[1,384,1536]{2,1,0:T(8,128)(2,1)}) custom-call(s32[10]{0:T(128)} %pad_add_fusion.2.refs_0_.order_ref, bf16[2,288,768]{2,1,0:T(8,128)(2,1)} %get-tuple-element.183.refs_18_.refs_1_, f32[2,288,128]{2,1,0:T(8,128)} %get-tuple-element.184.refs_2_, bf16[2,144,384]{2,1,0:T(8,128)(2,1)} %get-tuple-element.178.refs_3_, ...), custom_call_target="tpu_custom_call" | custom-call | flops 4278000128 | bytes 1024 | tf_op jit(solution)/shard_map/experts_down/pallas_call | solution.py:912
  499.5 10.4 %experts_down.6 = (bf16[384,1536]{1,0:T(8,128)(2,1)}, bf16[2,384,1536]{2,1,0:T(8,128)(2,1)}) custom-call(s32[10]{0:T(128)} %pad_add_fusion.2.refs_0_.order_ref, bf16[2,288,768]{2,1,0:T(8,128)(2,1)} %get-tuple-element.176.refs_17_.refs_1_, f32[2,288,128]{2,1,0:T(8,128)} %get-tuple-element.177.refs_2_, bf16[2,144,384]{2,1,0:T(8,128)(2,1)} %get-tuple-element.174.refs_3_, ...), custom_call_target="tpu_custom_call" | custom-call | flops 4278000128 | bytes 1024 | tf_op jit(solution)/shard_map/experts_down/pallas_call | solution.py:912
  509.9 9.8 %experts_down.7 = (bf16[384,1536]{1,0:T(8,128)(2,1)}, bf16[2,384,1536]{2,1,0:T(8,128)(2,1)}) custom-call(s32[10]{0:T(128)} %pad_add_fusion.2.refs_0_.order_ref, bf16[2,288,768]{2,1,0:T(8,128)(2,1)} %get-tuple-element.169.refs_16_.refs_1_, f32[2,288,128]{2,1,0:T(8,128)} %get-tuple-element.170.refs_2_, ...), custom_call_target="tpu_custom_call", output_to_operand_aliasing={{1}: (9, {})} | custom-call | flops 4278000128 | bytes 1024 | tf_op jit(solution)/shard_map/experts_down/pallas_call | solution.py:912
  524.5 10.3 %resid_back.1 = (f32[384,1536]{1,0:T(8,128)}, bf16[384,1536]{1,0:T(8,128)(2,1)}, bf16[384,1536]{1,0:T(8,128)(2,1)}, f32[6,8,384]{2,1,0:T(8,128)}, f32[8,1536]{1,0:T(8,128)}) custom-call(bf16[384,1536]{1,0:T(8,128)(2,1)} %bitcast.116, bf16[384,1536]{1,0:T(8,128)(2,1)} %get-tuple-element.162.refs_1_, bf16[384,1536]{1,0:T(8,128)(2,1)} %bitcast.119, ...), custom_call_target="tpu_custom_call" | custom-call | flops 4830000128 | bytes 1024 | tf_op jit(solution)/shard_map/resid_back/pallas_call | solution.py:1015
  534.9 26.5 %attention_back.2 = (bf16[384,768]{1,0:T(8,128)(2,1)}, bf16[384,512]{1,0:T(8,128)(2,1)}, bf16[384,512]{1,0:T(8,128)(2,1)}, bf16[384,512]{1,0:T(8,128)(2,1)}, bf1...) custom-call(s32[13]{0:T(128)} %pad_add_fusion.1.refs_0_, ...), custom_call_target="tpu_custom_call" | custom-call | flops 11960000512 | bytes 1024 | tf_op jit(solution)/shard_map/attention_back/pallas_call | solution.py:608
  570.0 26.1 %attention_back.3 = (bf16[384,768]{1,0:T(8,128)(2,1)}, bf16[384,512]{1,0:T(8,128)(2,1)}, bf16[384,512]{1,0:T(8,128)(2,1)}, bf16[384,512]{1,0:T(8,128)(2,1)}, bf1...) custom-call(s32[13]{0:T(128)} %pad_add_fusion.1.refs_0_, ...), custom_call_target="tpu_custom_call", output_to_operand_aliasing={{1}: (15, {}), {2}: (16, {}), {3}: (17, {}), {4}: (18, {}),... | custom-call | flops 11960000512 | bytes 1024 | tf_op jit(solution)/shard_map/attention_back/pallas_call | solution.py:608
  636.9 9.7 %collective-permute-start.47 = (bf16[384,512]{1,0:T(8,128)(2,1)S(1)}, bf16[384,512]{1,0:T(8,128)(2,1)S(1)}, u32[]{:S(2)}, u32[]{:S(2)}) collective-permute-start(bf16[384,512]{1,0:T(8,128)(2,1)S(1)} %add_add_fusion.1), channel_id=1, source_target_pairs={{0,8},{4,12},{8,0},{12,4},{16,24},{20,28},{24,16},{28,20},{1,9},{5... | collective-permute-start | bytes 1179656 | tf_op jit(solution)/shard_map/ppermute | solution.py:90
  706.9 10.0 %final.1 = (bf16[384,1536]{1,0:T(8,128)(2,1)}, bf16[2,2,4,48,640]{4,3,2,1,0:T(8,128)(2,1)}, bf16[2,2,4,48,640]{4,3,2,1,0:T(8,128)(2,1)}) custom-call(s32[10]{0:T(128)} %pad_add_fusion.2.refs_0_.order_ref, bf16[384,1536]{1,0:T(8,128)(2,1)} %bitcast.117, bf16[384,1536]{1,0:T(8,128)(2,1)} %get-tuple-element.259.left_ref.refs_2_, ...), custom_call_target="tpu_custom_call" | custom-call | flops 4600000000 | bytes 1024 | tf_op jit(solution)/shard_map/final/pallas_call | solution.py:1230
  (383 shorter events, 377.0 us)
Async XLA Ops:
  7.2 142.4 %all-gather.2.cloned.1.call-start = ((), (), s32[]{:S(2)}) async-start(), calls=%async_computation.2 | async-start | bytes 11759616 | tf_op jit(solution)/shard_map/all_gather | solution.py:1296
  10.6 559.4 %reduce-scatter.3.cloned.1.call-start = ((), (), s32[]{:S(2)}) async-start(), calls=%async_computation.3 | async-start | bytes 8847360 | tf_op jit(solution)/shard_map/reduce_scatter | solution.py:1419
  15.2 131.7 %collective-permute-start.16 = (bf16[3,2,384,768]{3,2,1,0:T(8,128)(2,1)S(1)}, bf16[3,2,384,768]{3,2,1,0:T(8,128)(2,1)}, u32[]{:S(2)}, u32[]{:S(2)}) collective-permute-start(bf16[3,2,384,768]{3,2,1,0:T(8,128)(2,1)S(1)} %pad_maximum_fusion.refs_3_.refs_6_.refs_5_), channel_id=1, source_target_pairs={{0,2},{1,3},{2,0},{3,1},{4,6},{5,7},{6,4},{7,5},{8,10},{9,11},{10,... | collective-permute-start | bytes 10616840 | tf_op jit(solution)/shard_map/ppermute | solution.py:224
  28.8 40.0 %collective-permute-start.2 = (bf16[384,1664]{1,0:T(8,128)(2,1)}, bf16[384,1664]{1,0:T(8,128)(2,1)}, u32[]{:S(2)}, u32[]{:S(2)}) collective-permute-start(bf16[384,1664]{1,0:T(8,128)(2,1)} %concatenate.25.refs_1_), channel_id=1, source_target_pairs={{0,4},{4,0},{8,12},{12,8},{16,20},{20,16},{24,28},{28,24},{1,5},{5... | collective-permute-start | bytes 3833864 | tf_op jit(solution)/shard_map/ppermute | solution.py:98
  30.3 38.5 %collective-permute-start.1 = (bf16[384,1664]{1,0:T(8,128)(2,1)}, bf16[384,1664]{1,0:T(8,128)(2,1)}, u32[]{:S(2)}, u32[]{:S(2)}) collective-permute-start(bf16[384,1664]{1,0:T(8,128)(2,1)} %concatenate.25.refs_1_), channel_id=1, source_target_pairs={{8,16},{12,20},{16,8},{20,12},{9,17},{13,21},{17,9},{21,13},{10,18... | collective-permute-start | bytes 3833864 | tf_op jit(solution)/shard_map/ppermute | solution.py:90
  32.0 48.0 %collective-permute-start = (bf16[384,1664]{1,0:T(8,128)(2,1)}, bf16[384,1664]{1,0:T(8,128)(2,1)}, u32[]{:S(2)}, u32[]{:S(2)}) collective-permute-start(bf16[384,1664]{1,0:T(8,128)(2,1)} %concatenate.25.refs_1_), channel_id=1, source_target_pairs={{0,8},{4,12},{8,0},{12,4},{16,24},{20,28},{24,16},{28,20},{1,9},{5... | collective-permute-start | bytes 3833864 | tf_op jit(solution)/shard_map/ppermute | solution.py:90
  81.8 50.0 %collective-permute-start.3 = (bf16[384,1664]{1,0:T(8,128)(2,1)}, bf16[384,1664]{1,0:T(8,128)(2,1)}, u32[]{:S(2)}, u32[]{:S(2)}) collective-permute-start(bf16[384,1664]{1,0:T(8,128)(2,1)} %get-tuple-element.145.refs_1_), channel_id=1, source_target_pairs={{0,4},{4,0},{8,12},{12,8},{16,20},{20,16},{24,28},{28,24},{1,5},{5... | collective-permute-start | bytes 3833864 | tf_op jit(solution)/shard_map/ppermute | solution.py:98
  83.2 60.7 %collective-permute-start.4 = (bf16[384,1664]{1,0:T(8,128)(2,1)}, bf16[384,1664]{1,0:T(8,128)(2,1)}, u32[]{:S(2)}, u32[]{:S(2)}) collective-permute-start(bf16[384,1664]{1,0:T(8,128)(2,1)} %get-tuple-element.146.refs_1_), channel_id=1, source_target_pairs={{8,0},{12,4},{16,24},{20,28},{9,1},{13,5},{17,25},{21,29},{10,2},{... | collective-permute-start | bytes 3833864 | tf_op jit(solution)/shard_map/ppermute | solution.py:90
  84.5 128.8 %collective-permute-start.15 = (bf16[3,2,384,768]{3,2,1,0:T(8,128)(2,1)S(1)}, bf16[3,2,384,768]{3,2,1,0:T(8,128)(2,1)}, u32[]{:S(2)}, u32[]{:S(2)}) collective-permute-start(bf16[3,2,384,768]{3,2,1,0:T(8,128)(2,1)S(1)} %pad_maximum_fusion.refs_3_.refs_6_.refs_5_), channel_id=1, source_target_pairs={{0,1},{1,0},{2,3},{3,2},{4,5},{5,4},{6,7},{7,6},{8,9},{9,8},{10,11... | collective-permute-start | bytes 10616840 | tf_op jit(solution)/shard_map/ppermute | solution.py:224
  147.0 66.3 %collective-permute-start.17 = (bf16[3,2,384,768]{3,2,1,0:T(8,128)(2,1)}, bf16[3,2,384,768]{3,2,1,0:T(8,128)(2,1)}, u32[]{:S(2)}, u32[]{:S(2)}) collective-permute-start(bf16[3,2,384,768]{3,2,1,0:T(8,128)(2,1)} %hold.40.refs_5_.refs_8_.refs_7_), channel_id=1, source_target_pairs={{0,1},{1,0},{2,3},{3,2},{4,5},{5,4},{6,7},{7,6},{8,9},{9,8},{10,11... | collective-permute-start | bytes 10616840 | tf_op jit(solution)/shard_map/ppermute | solution.py:224
  210.6 28.7 %collective-permute-start.18 = (bf16[384,1664]{1,0:T(8,128)(2,1)}, bf16[384,1664]{1,0:T(8,128)(2,1)}, u32[]{:S(2)}, u32[]{:S(2)}) collective-permute-start(bf16[384,1664]{1,0:T(8,128)(2,1)} %get-tuple-element.158), channel_id=1, source_target_pairs={{8,0},{12,4},{16,24},{20,28},{9,1},{13,5},{17,25},{21,29},{10,2},{... | collective-permute-start | bytes 3833864 | tf_op jit(solution)/shard_map/ppermute | solution.py:90
  428.6 141.4 %reduce-scatter.5.cloned.1.call-start = ((), (), s32[]{:S(2)}) async-start(), calls=%async_computation.4 | async-start | bytes 8847360 | tf_op jit(solution)/shard_map/reduce_scatter | solution.py:1419
  428.7 29.6 %collective-permute-start.32 = (bf16[384,1536]{1,0:T(8,128)(2,1)}, bf16[384,1536]{1,0:T(8,128)(2,1)S(1)}, u32[]{:S(2)}, u32[]{:S(2)}) collective-permute-start(bf16[384,1536]{1,0:T(8,128)(2,1)} %get-tuple-element.211), channel_id=1, source_target_pairs={{0,4},{4,0},{8,12},{12,8},{16,20},{20,16},{24,28},{28,24},{1,5},{5... | collective-permute-start | bytes 3538952 | tf_op jit(solution)/shard_map/ppermute | solution.py:98
  471.2 50.6 %collective-permute-start.39 = (bf16[384,1536]{1,0:T(8,128)(2,1)}, bf16[384,1536]{1,0:T(8,128)(2,1)S(1)}, u32[]{:S(2)}, u32[]{:S(2)}) collective-permute-start(bf16[384,1536]{1,0:T(8,128)(2,1)} %get-tuple-element.227), channel_id=1, source_target_pairs={{0,4},{4,0},{8,12},{12,8},{16,20},{20,16},{24,28},{28,24},{1,5},{5... | collective-permute-start | bytes 3538952 | tf_op jit(solution)/shard_map/ppermute | solution.py:98
  519.8 41.6 %collective-permute-start.36 = (bf16[1,384,1536]{2,1,0:T(8,128)(2,1)}, bf16[1,384,1536]{2,1,0:T(8,128)(2,1)}, u32[]{:S(2)}, u32[]{:S(2)}) collective-permute-start(bf16[1,384,1536]{2,1,0:T(8,128)(2,1)} %get-tuple-element.225), channel_id=1, source_target_pairs={{0,4},{4,0},{8,12},{12,8},{16,20},{20,16},{24,28},{28,24},{1,5},{5... | collective-permute-start | bytes 3538952 | tf_op jit(solution)/shard_map/ppermute | solution.py:98
  521.4 91.9 %collective-permute-start.41 = (bf16[1,384,1536]{2,1,0:T(8,128)(2,1)}, bf16[1,384,1536]{2,1,0:T(8,128)(2,1)}, u32[]{:S(2)}, u32[]{:S(2)}) collective-permute-start(bf16[1,384,1536]{2,1,0:T(8,128)(2,1)} %get-tuple-element.235), channel_id=1, source_target_pairs={{0,4},{4,0},{8,12},{12,8},{16,20},{20,16},{24,28},{28,24},{1,5},{5... | collective-permute-start | bytes 3538952 | tf_op jit(solution)/shard_map/ppermute | solution.py:98
  522.9 90.4 %collective-permute-start.42 = (bf16[2,384,1536]{2,1,0:T(8,128)(2,1)}, bf16[2,384,1536]{2,1,0:T(8,128)(2,1)S(1)}, u32[]{:S(2)}, u32[]{:S(2)}) collective-permute-start(bf16[2,384,1536]{2,1,0:T(8,128)(2,1)} %get-tuple-element.236), channel_id=1, source_target_pairs={{0,4},{4,0},{8,12},{12,8},{16,20},{20,16},{24,28},{28,24},{1,5},{5... | collective-permute-start | bytes 7077896 | tf_op jit(solution)/shard_map/ppermute | solution.py:98
  563.2 50.1 %collective-permute-start.40 = (bf16[384,1536]{1,0:T(8,128)(2,1)S(1)}, bf16[384,1536]{1,0:T(8,128)(2,1)}, u32[]{:S(2)}, u32[]{:S(2)}) collective-permute-start(bf16[384,1536]{1,0:T(8,128)(2,1)S(1)} %bitcast_add_fusion.2.refs_23_.refs_0_), channel_id=1, source_target_pairs={{0,8},{4,12},{24,16},{28,20},{1,9},{5,13},{25,17},{29,21},{2,10},{... | collective-permute-start | bytes 3538952 | tf_op jit(solution)/shard_map/ppermute | solution.py:90
  615.2 54.5 %collective-permute-start.56 = (bf16[2,2,4,48,1536]{4,3,2,1,0:T(8,128)(2,1)}, bf16[2,2,4,48,1536]{4,3,2,1,0:T(8,128)(2,1)}, u32[]{:S(2)}, u32[]{:S(2)}) collective-permute-start(bf16[2,2,4,48,1536]{4,3,2,1,0:T(8,128)(2,1)} %get-tuple-element.274), channel_id=1, source_target_pairs={{0,1},{1,0},{2,3},{3,2},{4,5},{5,4},{6,7},{7,6},{8,9},{9,8},{10,11... | collective-permute-start | bytes 7077896 | tf_op jit(solution)/shard_map/ppermute | solution.py:224
  635.1 47.3 %collective-permute-start.58 = (bf16[2,2,4,48,1536]{4,3,2,1,0:T(8,128)(2,1)}, bf16[2,2,4,48,1536]{4,3,2,1,0:T(8,128)(2,1)}, u32[]{:S(2)}, u32[]{:S(2)}) collective-permute-start(bf16[2,2,4,48,1536]{4,3,2,1,0:T(8,128)(2,1)} %get-tuple-element.275), channel_id=1, source_target_pairs={{0,1},{1,0},{2,3},{3,2},{4,5},{5,4},{6,7},{7,6},{8,9},{9,8},{10,11... | collective-permute-start | bytes 7077896 | tf_op jit(solution)/shard_map/ppermute | solution.py:224
  649.4 31.8 %collective-permute-start.54 = (bf16[384,512]{1,0:T(8,128)(2,1)S(1)}, bf16[384,512]{1,0:T(8,128)(2,1)S(1)}, u32[]{:S(2)}, u32[]{:S(2)}) collective-permute-start(bf16[384,512]{1,0:T(8,128)(2,1)S(1)} %add.272), channel_id=1, source_target_pairs={{0,8},{4,12},{24,16},{28,20},{1,9},{5,13},{25,17},{29,21},{2,10},{... | collective-permute-start | bytes 1179656 | tf_op jit(solution)/shard_map/ppermute | solution.py:90
  672.2 29.2 %collective-permute-start.57 = (bf16[2,4,48,1536]{3,2,1,0:T(8,128)(2,1)}, bf16[2,4,48,1536]{3,2,1,0:T(8,128)(2,1)}, u32[]{:S(2)}, u32[]{:S(2)}) collective-permute-start(bf16[2,4,48,1536]{3,2,1,0:T(8,128)(2,1)} %fusion.8), channel_id=1, source_target_pairs={{0,2},{1,3},{2,0},{3,1},{4,6},{5,7},{6,4},{7,5},{8,10},{9,11},{10,... | collective-permute-start | bytes 3538952 | tf_op jit(solution)/shard_map/ppermute | solution.py:224
  685.3 33.7 %collective-permute-start.65 = (bf16[2,4,48,1536]{3,2,1,0:T(8,128)(2,1)S(1)}, bf16[2,4,48,1536]{3,2,1,0:T(8,128)(2,1)}, u32[]{:S(2)}, u32[]{:S(2)}) collective-permute-start(bf16[2,4,48,1536]{3,2,1,0:T(8,128)(2,1)S(1)} %fusion.7.refs_15_), channel_id=1, source_target_pairs={{0,2},{1,3},{2,0},{3,1},{4,6},{5,7},{6,4},{7,5},{8,10},{9,11},{10,... | collective-permute-start | bytes 3538952 | tf_op jit(solution)/shard_map/ppermute | solution.py:224
  688.9 33.8 %collective-permute-start.51 = (bf16[384,1536]{1,0:T(8,128)(2,1)}, bf16[384,1536]{1,0:T(8,128)(2,1)}, u32[]{:S(2)}, u32[]{:S(2)}) collective-permute-start(bf16[384,1536]{1,0:T(8,128)(2,1)} %fusion.11), channel_id=1, source_target_pairs={{0,8},{4,12},{8,0},{12,4},{16,24},{20,28},{24,16},{28,20},{1,9},{5... | collective-permute-start | bytes 3538952 | tf_op jit(solution)/shard_map/ppermute | solution.py:90
  (109 other events, 1162.3 us)
Sparse Core Ops, SparseCore 0:
  11.5 135.3 all-gather.1
  428.7 64.0 reduce-scatter.2
  495.5 63.6 reduce-scatter.4

commit v4 on v3

--- a/solution.py
+++ b/solution.py
@@ -642,7 +642,7 @@
 
 def out_call(x, attended, wo_t, gains, after=()):
     tokens, width = x.shape
-    tile = 128
+    tile = 384
     return pl.pallas_call(
         without(out_kernel, 3 + HQ // 512, len(after)),
         name="attention_out",
@@ -1010,7 +1010,7 @@
 
 def resid_back_call(x, rows, dy, gains, wo_t, attended, parts, after=()):
     tokens, width = x.shape
-    tile = 128
+    tile = 384
     by_row = lambda i: (i, 0)
     return pl.pallas_call(
         without(

time: 790 us -> 787 us (level)
  no operation moved by 1% of the time
where the time goes in v4:
time: 787 us; the launch traced here: 779 us
  Pallas kernels  317 us (40%)
  waiting for transfers between devices  205 us (26%)
  starting transfers between devices  124 us (16%)
  other arithmetic  62.6 us (8%)
  local copies, waits for them, and re-layouts  53.6 us (7%)
  between operations  17.2 us (2%)
    ppermute x26, waiting for transfers between devices, swap(): return lax.ppermute(array, 'ctx', pairs)  136 us
    ppermute x39, starting transfers between devices, move(): return lax.ppermute(array, 'ctx', pairs)  90.6 us
    pallas_call x4, Pallas kernels, expert_call(): pl.pallas_call(without(lambda *refs: expert_kernel(len(shards), capacity,...  67.1 us
    ppermute x39, waiting for transfers between devices, move(): return lax.ppermute(array, 'ctx', pairs)  56.7 us
    pallas_call x2, Pallas kernels, attn_back_call(): pl.pallas_call(without(lambda *refs: attn_back_kernel(count, group, *refs...  52.5 us
    pallas_call x4, Pallas kernels, down_call(): pl.pallas_call(lambda *refs: down_kernel(len(shards), capacity, place, *r...  39.9 us
    unnamed x119, local copies, waits for them, and re-layouts  38.3 us
    pallas_call x2, Pallas kernels, attn_call(): pl.pallas_call(without(lambda *refs: attn_kernel(count, base, last, *refs...  36 us
  transfers between devices with their start and end apart: 77, of which 28 were waited for; matrix products, arithmetic and copies ran while one was open for 11% of the time, Pallas kernels for 38%

profile of v4, /device:TPU:0, one launch (start us, length us, event | category | flops | bytes accessed | tf_op | source)
XLA Modules:
  0.0 779.2 jit_solution(4680248795183426601)
XLA Ops:
  35.4 33.4 %collective-permute-done.2.refs_2_.refs_0_ = bf16[384,1664]{1,0:T(8,128)(2,1)} collective-permute-done((bf16[384,1664]{1,0:T(8,128)(2,1)}, bf16[384,1664]{1,0:T(8,128)(2,1)}, u32[]{:S(2)}, u32[]{:S(2)}) %collective-permute-start.2) | collective-permute-done | bytes 1277984 | tf_op jit(solution)/shard_map/ppermute | solution.py:98
  68.8 11.2 %collective-permute-done.refs_0_ = bf16[384,1664]{1,0:T(8,128)(2,1)} collective-permute-done((bf16[384,1664]{1,0:T(8,128)(2,1)}, bf16[384,1664]{1,0:T(8,128)(2,1)}, u32[]{:S(2)}, u32[]{:S(2)}) %collective-permute-start) | collective-permute-done | bytes 1277984 | tf_op jit(solution)/shard_map/ppermute | solution.py:90
  84.6 47.2 %collective-permute-done.3.refs_2_.refs_0_ = bf16[384,1664]{1,0:T(8,128)(2,1)} collective-permute-done((bf16[384,1664]{1,0:T(8,128)(2,1)}, bf16[384,1664]{1,0:T(8,128)(2,1)}, u32[]{:S(2)}, u32[]{:S(2)}) %collective-permute-start.3) | collective-permute-done | bytes 1277984 | tf_op jit(solution)/shard_map/ppermute | solution.py:98
  131.7 12.2 %collective-permute-done.4.refs_0_ = bf16[384,1664]{1,0:T(8,128)(2,1)} collective-permute-done((bf16[384,1664]{1,0:T(8,128)(2,1)}, bf16[384,1664]{1,0:T(8,128)(2,1)}, u32[]{:S(2)}, u32[]{:S(2)}) %collective-permute-start.4) | collective-permute-done | bytes 1277984 | tf_op jit(solution)/shard_map/ppermute | solution.py:90
  175.4 8.9 %collective-permute-done.9.refs_0_ = bf16[384,512]{1,0:T(8,128)(2,1)} collective-permute-done((bf16[384,512]{1,0:T(8,128)(2,1)}, bf16[384,512]{1,0:T(8,128)(2,1)}, u32[]{:S(2)}, u32[]{:S(2)}) %collective-permute-start.9) | collective-permute-done | bytes 393248 | tf_op jit(solution)/shard_map/ppermute | solution.py:90
  221.7 17.6 %attention.2 = (f32[6,128,768]{2,1,0:T(8,128)}, f32[6,8,768]{2,1,0:T(8,128)}) custom-call(s32[13]{0:T(128)} %pad_add_fusion.1.refs_0_, bf16[384,1536]{1,0:T(8,128)(2,1)} %get-tuple-element.148.refs_1_, bf16[384,512]{1,0:T(8,128)(2,1)} %get-tuple-element.149.refs_2_.refs_7_, bf16[384,512]{1,0:T(8,128)(2,1)} %hold.37.refs_3_.refs_8_, ...), custom_call_target="tpu_custom_call" | custom-call | flops 8280000000 | bytes 1024 | tf_op jit(solution)/shard_map/attention/pallas_call | solution.py:491
  243.0 18.3 %attention.3 = (bf16[384,1536]{1,0:T(8,128)(2,1)}, f32[6,8,384]{2,1,0:T(8,128)}) custom-call(s32[13]{0:T(128)} %pad_add_fusion.1.refs_0_, bf16[384,1536]{1,0:T(8,128)(2,1)} %get-tuple-element.148.refs_1_, bf16[384,512]{1,0:T(8,128)(2,1)} %add.246.refs_1_.refs_2_.refs_11_, bf16[384,512]{1,0:T(8,128)(2,1)} %collective-permute-done.12.refs_1_.refs_3_.refs_12_, ...), custom_call_target="tpu_custom_call" | custom-call | flops 8280000000 | bytes 1024 | tf_op jit(solution)/shard_map/attention/pallas_call | solution.py:491
  282.0 8.4 %route.5 = (bf16[2,144,384]{2,1,0:T(8,128)(2,1)}, bf16[2,144,384]{2,1,0:T(8,128)(2,1)}, f32[2,288,128]{2,1,0:T(8,128)}, bf16[2,288,1536]{2,1,0:T(8,128)(2,1)}, f32[2,288,768]{2,1,0:T(8,128)}) custom-call(s32[10]{0:T(128)} %pad_add_fusion.2.refs_0_.order_ref, bf16[384,1664]{1,0:T(8,128)(2,1)} %get-tuple-element.145.refs_1_, ...), custom_call_target="tpu_custom_call" | custom-call | flops 3910000128 | bytes 1024 | tf_op jit(solution)/shard_map/route/pallas_call | solution.py:755
  290.5 8.4 %route.6 = (bf16[2,144,384]{2,1,0:T(8,128)(2,1)}, bf16[2,144,384]{2,1,0:T(8,128)(2,1)}, f32[2,288,128]{2,1,0:T(8,128)}, bf16[2,288,1536]{2,1,0:T(8,128)(2,1)}, f32[2,288,768]{2,1,0:T(8,128)}) custom-call(s32[10]{0:T(128)} %pad_add_fusion.2.refs_0_.order_ref, bf16[384,1664]{1,0:T(8,128)(2,1)} %get-tuple-element.159.refs_1_, ...), custom_call_target="tpu_custom_call" | custom-call | flops 3910000128 | bytes 1024 | tf_op jit(solution)/shard_map/route/pallas_call | solution.py:755
  308.2 16.7 %experts.4 = (bf16[2,288,1536]{2,1,0:T(8,128)(2,1)}, bf16[2,288,768]{2,1,0:T(8,128)(2,1)}, bf16[2,288,768]{2,1,0:T(8,128)(2,1)}, bf16[2,288,768]{2,1,0:T(8,128)(...) custom-call(s32[10]{0:T(128)} %pad_add_fusion.2.refs_0_.order_ref, ...), custom_call_target="tpu_custom_call" | custom-call | flops 7820000256 | bytes 1024 | tf_op jit(solution)/shard_map/experts/pallas_call | solution.py:841
  335.8 16.8 %experts.5 = (bf16[2,288,1536]{2,1,0:T(8,128)(2,1)}, bf16[2,288,768]{2,1,0:T(8,128)(2,1)}, bf16[2,288,768]{2,1,0:T(8,128)(2,1)}, bf16[2,288,768]{2,1,0:T(8,128)(...) custom-call(s32[10]{0:T(128)} %pad_add_fusion.2.refs_0_.order_ref, ...), custom_call_target="tpu_custom_call" | custom-call | flops 7820000256 | bytes 1024 | tf_op jit(solution)/shard_map/experts/pallas_call | solution.py:841
  364.7 16.7 %experts.6 = (bf16[2,288,1536]{2,1,0:T(8,128)(2,1)}, bf16[2,288,768]{2,1,0:T(8,128)(2,1)}, bf16[2,288,768]{2,1,0:T(8,128)(2,1)}, bf16[2,288,768]{2,1,0:T(8,128)(...) custom-call(s32[10]{0:T(128)} %pad_add_fusion.2.refs_0_.order_ref, bf16[384,1536]{1,0:T(8,128)(2,1)} %copy-done.27, ...), custom_call_target="tpu_custom_call" | custom-call | flops 7820000256 | bytes 1024 | tf_op jit(solution)/shard_map/experts/pallas_call | solution.py:841
  382.4 16.9 %experts.7 = (bf16[2,288,1536]{2,1,0:T(8,128)(2,1)}, bf16[2,288,768]{2,1,0:T(8,128)(2,1)}, bf16[2,288,768]{2,1,0:T(8,128)(2,1)}, bf16[2,288,768]{2,1,0:T(8,128)(...) custom-call(s32[10]{0:T(128)} %pad_add_fusion.2.refs_0_.order_ref, bf16[384,1536]{1,0:T(8,128)(2,1)} %copy-done.45, ...), custom_call_target="tpu_custom_call" | custom-call | flops 7820000256 | bytes 1024 | tf_op jit(solution)/shard_map/experts/pallas_call | solution.py:841
  400.5 15.4 %expert_weight_grads.2.refs_1_.refs_20_ = bf16[3,1536,768]{2,1,0:T(8,128)(2,1)} custom-call(bf16[2,288,1536]{2,1,0:T(8,128)(2,1)} %get-tuple-element.190.refs_0_, bf16[2,288,1536]{2,1,0:T(8,128)(2,1)} %get-tuple-element.191.refs_1_, bf16[2,288,1536]{2,1,0:T(8,128)(2,1)} %get-tuple-element.192.refs_2_, bf16[2,288,1536]{2,1,0:T(8,128)(2,1)} %get-tuple-element.193.refs_3_, ...), custom_call_target="tpu_custom_call" | custom-call | flops 8280000000 | bytes 1024 | tf_op jit(solution)/shard_map/expert_weight_grads/pallas_call | solution.py:949
  433.0 16.4 %expert_weight_grads.3.refs_2_.refs_9_ = bf16[3,1536,768]{2,1,0:T(8,128)(2,1)} custom-call(bf16[2,288,1536]{2,1,0:T(8,128)(2,1)} %get-tuple-element.190.refs_0_, bf16[2,288,1536]{2,1,0:T(8,128)(2,1)} %get-tuple-element.191.refs_1_, bf16[2,288,1536]{2,1,0:T(8,128)(2,1)} %get-tuple-element.192.refs_2_, bf16[2,288,1536]{2,1,0:T(8,128)(2,1)} %get-tuple-element.193.refs_3_, ...), custom_call_target="tpu_custom_call" | custom-call | flops 8280000000 | bytes 1024 | tf_op jit(solution)/shard_map/expert_weight_grads/pallas_call | solution.py:949
  469.7 10.0 %experts_down.4 = (bf16[384,1536]{1,0:T(8,128)(2,1)}, bf16[1,384,1536]{2,1,0:T(8,128)(2,1)}) custom-call(s32[10]{0:T(128)} %pad_add_fusion.2.refs_0_.order_ref, bf16[2,288,768]{2,1,0:T(8,128)(2,1)} %get-tuple-element.188.refs_19_.refs_1_, f32[2,288,128]{2,1,0:T(8,128)} %get-tuple-element.189.refs_2_, bf16[2,144,384]{2,1,0:T(8,128)(2,1)} %get-tuple-element.185.refs_3_, ...), custom_call_target="tpu_custom_call" | custom-call | flops 4278000128 | bytes 1024 | tf_op jit(solution)/shard_map/experts_down/pallas_call | solution.py:912
  479.7 9.8 %experts_down.5 = (bf16[384,1536]{1,0:T(8,128)(2,1)}, bf16[1,384,1536]{2,1,0:T(8,128)(2,1)}) custom-call(s32[10]{0:T(128)} %pad_add_fusion.2.refs_0_.order_ref, bf16[2,288,768]{2,1,0:T(8,128)(2,1)} %get-tuple-element.183.refs_18_.refs_1_, f32[2,288,128]{2,1,0:T(8,128)} %get-tuple-element.184.refs_2_, bf16[2,144,384]{2,1,0:T(8,128)(2,1)} %get-tuple-element.178.refs_3_, ...), custom_call_target="tpu_custom_call" | custom-call | flops 4278000128 | bytes 1024 | tf_op jit(solution)/shard_map/experts_down/pallas_call | solution.py:912
  497.4 10.2 %experts_down.6 = (bf16[384,1536]{1,0:T(8,128)(2,1)}, bf16[2,384,1536]{2,1,0:T(8,128)(2,1)}) custom-call(s32[10]{0:T(128)} %pad_add_fusion.2.refs_0_.order_ref, bf16[2,288,768]{2,1,0:T(8,128)(2,1)} %get-tuple-element.176.refs_17_.refs_1_, f32[2,288,128]{2,1,0:T(8,128)} %get-tuple-element.177.refs_2_, bf16[2,144,384]{2,1,0:T(8,128)(2,1)} %get-tuple-element.174.refs_3_, ...), custom_call_target="tpu_custom_call" | custom-call | flops 4278000128 | bytes 1024 | tf_op jit(solution)/shard_map/experts_down/pallas_call | solution.py:912
  507.6 9.8 %experts_down.7 = (bf16[384,1536]{1,0:T(8,128)(2,1)}, bf16[2,384,1536]{2,1,0:T(8,128)(2,1)}) custom-call(s32[10]{0:T(128)} %pad_add_fusion.2.refs_0_.order_ref, bf16[2,288,768]{2,1,0:T(8,128)(2,1)} %get-tuple-element.169.refs_16_.refs_1_, f32[2,288,128]{2,1,0:T(8,128)} %get-tuple-element.170.refs_2_, ...), custom_call_target="tpu_custom_call", output_to_operand_aliasing={{1}: (9, {})} | custom-call | flops 4278000128 | bytes 1024 | tf_op jit(solution)/shard_map/experts_down/pallas_call | solution.py:912
  522.3 9.8 %resid_back.1 = (f32[384,1536]{1,0:T(8,128)}, bf16[384,1536]{1,0:T(8,128)(2,1)}, bf16[384,1536]{1,0:T(8,128)(2,1)}, f32[6,8,384]{2,1,0:T(8,128)}, f32[8,1536]{1,0:T(8,128)}) custom-call(bf16[384,1536]{1,0:T(8,128)(2,1)} %bitcast.116, bf16[384,1536]{1,0:T(8,128)(2,1)} %get-tuple-element.162.refs_1_, bf16[384,1536]{1,0:T(8,128)(2,1)} %bitcast.119, ...), custom_call_target="tpu_custom_call" | custom-call | flops 4830000128 | bytes 1024 | tf_op jit(solution)/shard_map/resid_back/pallas_call | solution.py:1015
  532.0 26.4 %attention_back.2 = (bf16[384,768]{1,0:T(8,128)(2,1)}, bf16[384,512]{1,0:T(8,128)(2,1)}, bf16[384,512]{1,0:T(8,128)(2,1)}, bf16[384,512]{1,0:T(8,128)(2,1)}, bf1...) custom-call(s32[13]{0:T(128)} %pad_add_fusion.1.refs_0_, ...), custom_call_target="tpu_custom_call" | custom-call | flops 11960000512 | bytes 1024 | tf_op jit(solution)/shard_map/attention_back/pallas_call | solution.py:608
  566.6 26.1 %attention_back.3 = (bf16[384,768]{1,0:T(8,128)(2,1)}, bf16[384,512]{1,0:T(8,128)(2,1)}, bf16[384,512]{1,0:T(8,128)(2,1)}, bf16[384,512]{1,0:T(8,128)(2,1)}, bf1...) custom-call(s32[13]{0:T(128)} %pad_add_fusion.1.refs_0_, ...), custom_call_target="tpu_custom_call", output_to_operand_aliasing={{1}: (15, {}), {2}: (16, {}), {3}: (17, {}), {4}: (18, {}),... | custom-call | flops 11960000512 | bytes 1024 | tf_op jit(solution)/shard_map/attention_back/pallas_call | solution.py:608
  634.2 9.7 %collective-permute-start.47 = (bf16[384,512]{1,0:T(8,128)(2,1)S(1)}, bf16[384,512]{1,0:T(8,128)(2,1)S(1)}, u32[]{:S(2)}, u32[]{:S(2)}) collective-permute-start(bf16[384,512]{1,0:T(8,128)(2,1)S(1)} %add_add_fusion.1), channel_id=1, source_target_pairs={{0,8},{4,12},{8,0},{12,4},{16,24},{20,28},{24,16},{28,20},{1,9},{5... | collective-permute-start | bytes 1179656 | tf_op jit(solution)/shard_map/ppermute | solution.py:90
  704.1 10.0 %final.1 = (bf16[384,1536]{1,0:T(8,128)(2,1)}, bf16[2,2,4,48,640]{4,3,2,1,0:T(8,128)(2,1)}, bf16[2,2,4,48,640]{4,3,2,1,0:T(8,128)(2,1)}) custom-call(s32[10]{0:T(128)} %pad_add_fusion.2.refs_0_.order_ref, bf16[384,1536]{1,0:T(8,128)(2,1)} %bitcast.117, bf16[384,1536]{1,0:T(8,128)(2,1)} %get-tuple-element.259.left_ref.refs_2_, ...), custom_call_target="tpu_custom_call" | custom-call | flops 4600000000 | bytes 1024 | tf_op jit(solution)/shard_map/final/pallas_call | solution.py:1230
  (383 shorter events, 375.5 us)
Async XLA Ops:
  7.2 142.4 %all-gather.2.cloned.1.call-start = ((), (), s32[]{:S(2)}) async-start(), calls=%async_computation.2 | async-start | bytes 11759616 | tf_op jit(solution)/shard_map/all_gather | solution.py:1296
  10.6 556.0 %reduce-scatter.3.cloned.1.call-start = ((), (), s32[]{:S(2)}) async-start(), calls=%async_computation.3 | async-start | bytes 8847360 | tf_op jit(solution)/shard_map/reduce_scatter | solution.py:1419
  15.2 131.7 %collective-permute-start.16 = (bf16[3,2,384,768]{3,2,1,0:T(8,128)(2,1)S(1)}, bf16[3,2,384,768]{3,2,1,0:T(8,128)(2,1)}, u32[]{:S(2)}, u32[]{:S(2)}) collective-permute-start(bf16[3,2,384,768]{3,2,1,0:T(8,128)(2,1)S(1)} %pad_maximum_fusion.refs_3_.refs_6_.refs_5_), channel_id=1, source_target_pairs={{0,2},{1,3},{2,0},{3,1},{4,6},{5,7},{6,4},{7,5},{8,10},{9,11},{10,... | collective-permute-start | bytes 10616840 | tf_op jit(solution)/shard_map/ppermute | solution.py:224
  28.8 40.0 %collective-permute-start.2 = (bf16[384,1664]{1,0:T(8,128)(2,1)}, bf16[384,1664]{1,0:T(8,128)(2,1)}, u32[]{:S(2)}, u32[]{:S(2)}) collective-permute-start(bf16[384,1664]{1,0:T(8,128)(2,1)} %concatenate.25.refs_1_), channel_id=1, source_target_pairs={{0,4},{4,0},{8,12},{12,8},{16,20},{20,16},{24,28},{28,24},{1,5},{5... | collective-permute-start | bytes 3833864 | tf_op jit(solution)/shard_map/ppermute | solution.py:98
  30.3 38.5 %collective-permute-start.1 = (bf16[384,1664]{1,0:T(8,128)(2,1)}, bf16[384,1664]{1,0:T(8,128)(2,1)}, u32[]{:S(2)}, u32[]{:S(2)}) collective-permute-start(bf16[384,1664]{1,0:T(8,128)(2,1)} %concatenate.25.refs_1_), channel_id=1, source_target_pairs={{8,16},{12,20},{16,8},{20,12},{9,17},{13,21},{17,9},{21,13},{10,18... | collective-permute-start | bytes 3833864 | tf_op jit(solution)/shard_map/ppermute | solution.py:90
  32.0 48.0 %collective-permute-start = (bf16[384,1664]{1,0:T(8,128)(2,1)}, bf16[384,1664]{1,0:T(8,128)(2,1)}, u32[]{:S(2)}, u32[]{:S(2)}) collective-permute-start(bf16[384,1664]{1,0:T(8,128)(2,1)} %concatenate.25.refs_1_), channel_id=1, source_target_pairs={{0,8},{4,12},{8,0},{12,4},{16,24},{20,28},{24,16},{28,20},{1,9},{5... | collective-permute-start | bytes 3833864 | tf_op jit(solution)/shard_map/ppermute | solution.py:90
  81.8 50.0 %collective-permute-start.3 = (bf16[384,1664]{1,0:T(8,128)(2,1)}, bf16[384,1664]{1,0:T(8,128)(2,1)}, u32[]{:S(2)}, u32[]{:S(2)}) collective-permute-start(bf16[384,1664]{1,0:T(8,128)(2,1)} %get-tuple-element.145.refs_1_), channel_id=1, source_target_pairs={{0,4},{4,0},{8,12},{12,8},{16,20},{20,16},{24,28},{28,24},{1,5},{5... | collective-permute-start | bytes 3833864 | tf_op jit(solution)/shard_map/ppermute | solution.py:98
  83.2 60.7 %collective-permute-start.4 = (bf16[384,1664]{1,0:T(8,128)(2,1)}, bf16[384,1664]{1,0:T(8,128)(2,1)}, u32[]{:S(2)}, u32[]{:S(2)}) collective-permute-start(bf16[384,1664]{1,0:T(8,128)(2,1)} %get-tuple-element.146.refs_1_), channel_id=1, source_target_pairs={{8,0},{12,4},{16,24},{20,28},{9,1},{13,5},{17,25},{21,29},{10,2},{... | collective-permute-start | bytes 3833864 | tf_op jit(solution)/shard_map/ppermute | solution.py:90
  84.5 128.8 %collective-permute-start.15 = (bf16[3,2,384,768]{3,2,1,0:T(8,128)(2,1)S(1)}, bf16[3,2,384,768]{3,2,1,0:T(8,128)(2,1)}, u32[]{:S(2)}, u32[]{:S(2)}) collective-permute-start(bf16[3,2,384,768]{3,2,1,0:T(8,128)(2,1)S(1)} %pad_maximum_fusion.refs_3_.refs_6_.refs_5_), channel_id=1, source_target_pairs={{0,1},{1,0},{2,3},{3,2},{4,5},{5,4},{6,7},{7,6},{8,9},{9,8},{10,11... | collective-permute-start | bytes 10616840 | tf_op jit(solution)/shard_map/ppermute | solution.py:224
  147.0 66.3 %collective-permute-start.17 = (bf16[3,2,384,768]{3,2,1,0:T(8,128)(2,1)}, bf16[3,2,384,768]{3,2,1,0:T(8,128)(2,1)}, u32[]{:S(2)}, u32[]{:S(2)}) collective-permute-start(bf16[3,2,384,768]{3,2,1,0:T(8,128)(2,1)} %hold.40.refs_5_.refs_8_.refs_7_), channel_id=1, source_target_pairs={{0,1},{1,0},{2,3},{3,2},{4,5},{5,4},{6,7},{7,6},{8,9},{9,8},{10,11... | collective-permute-start | bytes 10616840 | tf_op jit(solution)/shard_map/ppermute | solution.py:224
  210.6 28.7 %collective-permute-start.18 = (bf16[384,1664]{1,0:T(8,128)(2,1)}, bf16[384,1664]{1,0:T(8,128)(2,1)}, u32[]{:S(2)}, u32[]{:S(2)}) collective-permute-start(bf16[384,1664]{1,0:T(8,128)(2,1)} %get-tuple-element.158), channel_id=1, source_target_pairs={{8,0},{12,4},{16,24},{20,28},{9,1},{13,5},{17,25},{21,29},{10,2},{... | collective-permute-start | bytes 3833864 | tf_op jit(solution)/shard_map/ppermute | solution.py:90
  426.5 140.1 %reduce-scatter.5.cloned.1.call-start = ((), (), s32[]{:S(2)}) async-start(), calls=%async_computation.4 | async-start | bytes 8847360 | tf_op jit(solution)/shard_map/reduce_scatter | solution.py:1419
  426.5 29.5 %collective-permute-start.32 = (bf16[384,1536]{1,0:T(8,128)(2,1)}, bf16[384,1536]{1,0:T(8,128)(2,1)S(1)}, u32[]{:S(2)}, u32[]{:S(2)}) collective-permute-start(bf16[384,1536]{1,0:T(8,128)(2,1)} %get-tuple-element.211), channel_id=1, source_target_pairs={{0,4},{4,0},{8,12},{12,8},{16,20},{20,16},{24,28},{28,24},{1,5},{5... | collective-permute-start | bytes 3538952 | tf_op jit(solution)/shard_map/ppermute | solution.py:98
  469.1 50.4 %collective-permute-start.39 = (bf16[384,1536]{1,0:T(8,128)(2,1)}, bf16[384,1536]{1,0:T(8,128)(2,1)S(1)}, u32[]{:S(2)}, u32[]{:S(2)}) collective-permute-start(bf16[384,1536]{1,0:T(8,128)(2,1)} %get-tuple-element.227), channel_id=1, source_target_pairs={{0,4},{4,0},{8,12},{12,8},{16,20},{20,16},{24,28},{28,24},{1,5},{5... | collective-permute-start | bytes 3538952 | tf_op jit(solution)/shard_map/ppermute | solution.py:98
  517.5 41.0 %collective-permute-start.36 = (bf16[1,384,1536]{2,1,0:T(8,128)(2,1)}, bf16[1,384,1536]{2,1,0:T(8,128)(2,1)}, u32[]{:S(2)}, u32[]{:S(2)}) collective-permute-start(bf16[1,384,1536]{2,1,0:T(8,128)(2,1)} %get-tuple-element.225), channel_id=1, source_target_pairs={{0,4},{4,0},{8,12},{12,8},{16,20},{20,16},{24,28},{28,24},{1,5},{5... | collective-permute-start | bytes 3538952 | tf_op jit(solution)/shard_map/ppermute | solution.py:98
  519.2 90.7 %collective-permute-start.41 = (bf16[1,384,1536]{2,1,0:T(8,128)(2,1)}, bf16[1,384,1536]{2,1,0:T(8,128)(2,1)}, u32[]{:S(2)}, u32[]{:S(2)}) collective-permute-start(bf16[1,384,1536]{2,1,0:T(8,128)(2,1)} %get-tuple-element.235), channel_id=1, source_target_pairs={{0,4},{4,0},{8,12},{12,8},{16,20},{20,16},{24,28},{28,24},{1,5},{5... | collective-permute-start | bytes 3538952 | tf_op jit(solution)/shard_map/ppermute | solution.py:98
  520.6 89.3 %collective-permute-start.42 = (bf16[2,384,1536]{2,1,0:T(8,128)(2,1)}, bf16[2,384,1536]{2,1,0:T(8,128)(2,1)S(1)}, u32[]{:S(2)}, u32[]{:S(2)}) collective-permute-start(bf16[2,384,1536]{2,1,0:T(8,128)(2,1)} %get-tuple-element.236), channel_id=1, source_target_pairs={{0,4},{4,0},{8,12},{12,8},{16,20},{20,16},{24,28},{28,24},{1,5},{5... | collective-permute-start | bytes 7077896 | tf_op jit(solution)/shard_map/ppermute | solution.py:98
  560.3 49.6 %collective-permute-start.40 = (bf16[384,1536]{1,0:T(8,128)(2,1)S(1)}, bf16[384,1536]{1,0:T(8,128)(2,1)}, u32[]{:S(2)}, u32[]{:S(2)}) collective-permute-start(bf16[384,1536]{1,0:T(8,128)(2,1)S(1)} %bitcast_add_fusion.2.refs_23_.refs_0_), channel_id=1, source_target_pairs={{0,8},{4,12},{24,16},{28,20},{1,9},{5,13},{25,17},{29,21},{2,10},{... | collective-permute-start | bytes 3538952 | tf_op jit(solution)/shard_map/ppermute | solution.py:90
  611.8 55.1 %collective-permute-start.56 = (bf16[2,2,4,48,1536]{4,3,2,1,0:T(8,128)(2,1)}, bf16[2,2,4,48,1536]{4,3,2,1,0:T(8,128)(2,1)}, u32[]{:S(2)}, u32[]{:S(2)}) collective-permute-start(bf16[2,2,4,48,1536]{4,3,2,1,0:T(8,128)(2,1)} %get-tuple-element.274), channel_id=1, source_target_pairs={{0,1},{1,0},{2,3},{3,2},{4,5},{5,4},{6,7},{7,6},{8,9},{9,8},{10,11... | collective-permute-start | bytes 7077896 | tf_op jit(solution)/shard_map/ppermute | solution.py:224
  632.3 47.4 %collective-permute-start.58 = (bf16[2,2,4,48,1536]{4,3,2,1,0:T(8,128)(2,1)}, bf16[2,2,4,48,1536]{4,3,2,1,0:T(8,128)(2,1)}, u32[]{:S(2)}, u32[]{:S(2)}) collective-permute-start(bf16[2,2,4,48,1536]{4,3,2,1,0:T(8,128)(2,1)} %get-tuple-element.275), channel_id=1, source_target_pairs={{0,1},{1,0},{2,3},{3,2},{4,5},{5,4},{6,7},{7,6},{8,9},{9,8},{10,11... | collective-permute-start | bytes 7077896 | tf_op jit(solution)/shard_map/ppermute | solution.py:224
  646.6 31.9 %collective-permute-start.54 = (bf16[384,512]{1,0:T(8,128)(2,1)S(1)}, bf16[384,512]{1,0:T(8,128)(2,1)S(1)}, u32[]{:S(2)}, u32[]{:S(2)}) collective-permute-start(bf16[384,512]{1,0:T(8,128)(2,1)S(1)} %add.272), channel_id=1, source_target_pairs={{0,8},{4,12},{24,16},{28,20},{1,9},{5,13},{25,17},{29,21},{2,10},{... | collective-permute-start | bytes 1179656 | tf_op jit(solution)/shard_map/ppermute | solution.py:90
  669.4 29.2 %collective-permute-start.57 = (bf16[2,4,48,1536]{3,2,1,0:T(8,128)(2,1)}, bf16[2,4,48,1536]{3,2,1,0:T(8,128)(2,1)}, u32[]{:S(2)}, u32[]{:S(2)}) collective-permute-start(bf16[2,4,48,1536]{3,2,1,0:T(8,128)(2,1)} %fusion.8), channel_id=1, source_target_pairs={{0,2},{1,3},{2,0},{3,1},{4,6},{5,7},{6,4},{7,5},{8,10},{9,11},{10,... | collective-permute-start | bytes 3538952 | tf_op jit(solution)/shard_map/ppermute | solution.py:224
  682.5 33.6 %collective-permute-start.65 = (bf16[2,4,48,1536]{3,2,1,0:T(8,128)(2,1)S(1)}, bf16[2,4,48,1536]{3,2,1,0:T(8,128)(2,1)}, u32[]{:S(2)}, u32[]{:S(2)}) collective-permute-start(bf16[2,4,48,1536]{3,2,1,0:T(8,128)(2,1)S(1)} %fusion.7.refs_15_), channel_id=1, source_target_pairs={{0,2},{1,3},{2,0},{3,1},{4,6},{5,7},{6,4},{7,5},{8,10},{9,11},{10,... | collective-permute-start | bytes 3538952 | tf_op jit(solution)/shard_map/ppermute | solution.py:224
  686.1 33.8 %collective-permute-start.51 = (bf16[384,1536]{1,0:T(8,128)(2,1)}, bf16[384,1536]{1,0:T(8,128)(2,1)}, u32[]{:S(2)}, u32[]{:S(2)}) collective-permute-start(bf16[384,1536]{1,0:T(8,128)(2,1)} %fusion.11), channel_id=1, source_target_pairs={{0,8},{4,12},{8,0},{12,4},{16,24},{20,28},{24,16},{28,20},{1,9},{5... | collective-permute-start | bytes 3538952 | tf_op jit(solution)/shard_map/ppermute | solution.py:90
  (109 other events, 1164.0 us)
Sparse Core Ops, SparseCore 0:
  11.5 135.3 all-gather.1
  426.6 64.1 reduce-scatter.2
  493.4 63.7 reduce-scatter.4
